TPU v7x, 32 devices: a whole 2x2x4 slice. The times are simulated.
32 devices in a mesh: replica: 8 (over y, x, core), group: 4 (over z).
Axes of the slice: x: 2, y: 2, z: 4, core: 2. Of those that a mesh axis runs over, the one named last changes fastest.
Arguments:
- tokens: bfloat16 [8, 1024, 2048], P('replica', 'group'), may hold values from -6 to 6
- cotangent: bfloat16 [8, 1024, 2048], P('replica', 'group'), may hold values from -6 to 6
- doc_start: int32 [8, 1024], P('replica', 'group'), may hold values from 0 to 1023, as said below
- norm_gain: bfloat16 [2048], P('group'), may hold values from 0.099609375 to 1.8984375
- qkv_weight: bfloat16 [2048, 6144], P('group'), may hold values from -0.125 to 0.125
- conv_weight: bfloat16 [6144, 4], P('group'), may hold values from -3 to 3
- beta_weight: bfloat16 [2048, 16], P('group'), may hold values from -0.125 to 0.125
- head_gain: bfloat16 [128], replicated, may hold values from 0.099609375 to 1.8984375
- out_weight: bfloat16 [2048, 2048], P('group'), may hold values from -0.125 to 0.125
- ffn_gain: bfloat16 [2048], P('group'), may hold values from 0.099609375 to 1.8984375
- gate_up_weight: bfloat16 [2048, 11264], P('group'), may hold values from -0.125 to 0.125
- down_weight: bfloat16 [5632, 2048], P('group'), may hold values from -0.078125 to 0.078125
Outputs:
- output: bfloat16 [8, 1024, 2048], P('replica', 'group')
- input_grad: float32 [8, 1024, 2048], P('replica', 'group')
- norm_gain_grad: float32 [2048], P('group')
- qkv_grad: float32 [2048, 6144], P('group')
- conv_grad: float32 [6144, 4], P('group')
- beta_grad: float32 [2048, 16], P('group')
- head_gain_grad: float32 [128], replicated
- out_grad: float32 [2048, 2048], P('group')
- ffn_gain_grad: float32 [2048], P('group')
- gate_up_grad: float32 [2048, 11264], P('group')
- down_grad: float32 [5632, 2048], P('group')
Inputs may be any that keep to these rules, and one draw needn't show every extreme that they name: doc_start never falls along a sequence and at each position equals that position or the previous token's value; in each aligned pair of sequences (rows 2k and 2k + 1) one, drawn from the seed, is a single document, and in the other the last token starts a document of its own.
All inputs are finite; a program needn't handle non-finite values.
Results may differ from a plain program's by a relative error of at most 0.02.
Values may be sent and summed in bfloat16 or wider, within the bound.
No kernel may reach another device: no remote copies, remote signals or barrier semaphores. Data moves between devices by JAX's collectives and lax.ppermute only.
A program may use at most 512 MiB of HBM per device.

v0:
```python
import jax
import jax.numpy as jnp
from jax import lax
from jax.sharding import PartitionSpec as P

D = 2048
HEADS = 16
HEAD_DIM = 128
FF = 5632
CONV = 4
STRETCH = 64


EPS = 1e-06
HIGH = lax.Precision.HIGHEST


def shifted(shard, axis, by):
    devices = lax.axis_size(axis)
    pairs = [(i, i + by) for i in range(devices) if 0 <= i + by < devices]
    return lax.ppermute(shard, axis, pairs)


def norm_rows(values, gain):
    return values * lax.rsqrt(jnp.mean(values * values, axis=-1, keepdims=True) + EPS) * gain


def unit_rows(values):
    return values * lax.rsqrt(jnp.sum(values * values, axis=-1, keepdims=True) + EPS)


def rounded(values):
    return lax.optimization_barrier(values.astype(jnp.bfloat16)).astype(jnp.float32)


def stretch_step(carry_state, queries, key_rows, value_rows, strength, documents, first_pos, quick):
    span_size = queries.shape[1]
    positions = first_pos + jnp.arange(span_size, dtype=jnp.int32)
    causal = positions[:, None] >= positions[None, :]
    same_doc = (documents[:, :, None] <= positions[None, None, :]) & causal[None]
    strict = same_doc & (positions[:, None] > positions[None, :])[None]
    carried = (documents < first_pos).astype(jnp.float32)
    rates = jnp.swapaxes(strength, 1, 2)[..., None]
    if quick:
        key_half = key_rows.astype(jnp.bfloat16)
        key_gram = jnp.einsum(
            "bihe,bjhe->bhij", key_half, key_half, preferred_element_type=jnp.float32
        )
        raw_scores = jnp.einsum(
            "bihe,bjhe->bhij",
            queries.astype(jnp.bfloat16),
            key_half,
            preferred_element_type=jnp.float32,
        )
    else:
        key_gram = jnp.einsum("bihe,bjhe->bhij", key_rows, key_rows, precision=HIGH)
        raw_scores = jnp.einsum("bihe,bjhe->bhij", queries, key_rows, precision=HIGH)
    coupling = key_gram * rates * strict[:, None].astype(jnp.float32)
    key_state = jnp.einsum("bihe,bhef->bhif", key_rows, carry_state, precision=HIGH)
    target = rates * (jnp.swapaxes(value_rows, 1, 2) - key_state * carried[:, None, :, None])
    identity = jnp.eye(span_size, dtype=jnp.float32)
    update = jax.scipy.linalg.solve_triangular(
        identity + coupling, target, lower=True, unit_diagonal=True
    )
    scores = raw_scores * same_doc[:, None].astype(jnp.float32)
    result_rows = jnp.einsum("bhij,bhjf->bihf", scores, update, precision=HIGH)
    result_rows = (
        result_rows
        + jnp.einsum("bihe,bhef->bihf", queries, carry_state, precision=HIGH)
        * carried[:, :, None, None]
    )
    last_row = same_doc[:, -1, :].astype(jnp.float32)
    next_state = carry_state * carried[:, -1][:, None, None, None]
    next_state = next_state + jnp.einsum(
        "bjhe,bhjf->bhef", key_rows * last_row[:, :, None, None], update, precision=HIGH
    )
    return (next_state, result_rows)


def run_stretches(
    carry_state, queries, key_rows, value_rows, strength, documents, start_pos, quick=False
):
    batch_size = queries.shape[0]
    length = queries.shape[1]
    blocks = length // STRETCH

    def to_blocks(values):
        return jnp.moveaxis(values.reshape((batch_size, blocks, STRETCH) + values.shape[2:]), 1, 0)

    def block_step(state_now, block_item):
        block_index, query_block, key_block, value_block, rate_block, doc_block = block_item
        return stretch_step(
            state_now,
            query_block,
            key_block,
            value_block,
            rate_block,
            doc_block,
            start_pos + block_index * STRETCH,
            quick,
        )

    final_state, block_outs = lax.scan(
        block_step,
        carry_state,
        (
            jnp.arange(blocks, dtype=jnp.int32),
            to_blocks(queries),
            to_blocks(key_rows),
            to_blocks(value_rows),
            to_blocks(strength),
            to_blocks(documents),
        ),
    )
    return (jnp.moveaxis(block_outs, 0, 1).reshape(queries.shape), final_state)


def conv_act(extended, conv_cols, documents, base_pos):
    batch_size = extended.shape[0]
    length = extended.shape[1] - (CONV - 1)
    positions = base_pos + jnp.arange(length, dtype=jnp.int32)
    mixed = jnp.zeros((batch_size, length, extended.shape[2]), jnp.float32)
    for tap_index in range(CONV):
        tap_valid = (positions[None, :] - (CONV - 1) + tap_index >= documents).astype(jnp.float32)
        mixed = (
            mixed
            + extended[:, tap_index : tap_index + length]
            * conv_cols[:, tap_index]
            * tap_valid[..., None]
        )
    activity = jax.nn.silu(mixed)
    shape_heads = (batch_size, length, HEADS, HEAD_DIM)
    queries = unit_rows(activity[..., :D].reshape(shape_heads)) * HEAD_DIM ** (-0.5)
    key_rows = unit_rows(activity[..., D : 2 * D].reshape(shape_heads))
    value_rows = activity[..., 2 * D :].reshape(shape_heads)
    return (queries, key_rows, value_rows)


def swiglu(gate_up):
    return jax.nn.silu(gate_up[..., :FF]) * gate_up[..., FF:]


def body(
    tokens,
    cotangent,
    doc_start,
    norm_gain,
    qkv_weight,
    conv_weight,
    beta_weight,
    head_gain,
    out_weight,
    ffn_gain,
    gate_up_weight,
    down_weight,
):
    group_size = lax.axis_size("group")
    batch_size = tokens.shape[0]
    local_len = tokens.shape[1]
    base_pos = lax.axis_index("group") * local_len
    gathered = (
        lax.all_gather(norm_gain, "group", axis=0, tiled=True),
        lax.all_gather(qkv_weight, "group", axis=0, tiled=True),
        lax.all_gather(conv_weight, "group", axis=0, tiled=True),
        lax.all_gather(beta_weight, "group", axis=0, tiled=True),
        lax.all_gather(out_weight, "group", axis=0, tiled=True),
        lax.all_gather(ffn_gain, "group", axis=0, tiled=True),
        lax.all_gather(gate_up_weight, "group", axis=0, tiled=True),
        lax.all_gather(down_weight, "group", axis=0, tiled=True),
    )
    gain_first, qkv_full, conv_full, beta_full, out_full, gain_second, gate_full, down_full = (
        gathered
    )
    inputs = tokens.astype(jnp.float32)
    first_val, first_back = jax.vjp(norm_rows, inputs, gain_first.astype(jnp.float32))
    normed_in = first_val.astype(jnp.bfloat16)
    projected = jnp.dot(normed_in, qkv_full, preferred_element_type=jnp.float32).astype(
        jnp.bfloat16
    )
    rim_rows = shifted(projected[:, local_len - (CONV - 1) :], "group", 1)
    extended = jnp.concatenate([rim_rows, projected], axis=1).astype(jnp.float32)

    def conv_piece(ext_rows, conv_param):
        return conv_act(ext_rows, conv_param, doc_start, base_pos)

    (queries, key_rows, value_rows), conv_back = jax.vjp(
        conv_piece, extended, conv_full.astype(jnp.float32)
    )
    query_low = rounded(queries)
    key_low = rounded(key_rows)
    value_low = rounded(value_rows)
    strength = jax.nn.sigmoid(jnp.dot(normed_in, beta_full, preferred_element_type=jnp.float32))
    zero_state = jnp.zeros((batch_size, HEADS, HEAD_DIM, HEAD_DIM), jnp.float32)
    identity = jnp.broadcast_to(jnp.eye(HEAD_DIM, dtype=jnp.float32), zero_state.shape)
    free_end = run_stretches(
        zero_state, query_low, key_low, value_low, strength, doc_start, base_pos, True
    )[1]
    transfer = run_stretches(
        identity, query_low, key_low, jnp.zeros_like(value_low), strength, doc_start, base_pos, True
    )[1]
    incoming = zero_state
    for step_index in range(group_size - 1):
        outgoing = jnp.einsum("bhij,bhjk->bhik", transfer, incoming, precision=HIGH) + free_end
        incoming = shifted(outgoing.astype(jnp.bfloat16), "group", 1).astype(outgoing.dtype)

    def delta_piece(query_in, key_in, value_in, rate_in, start_state):
        return run_stretches(start_state, query_in, key_in, value_in, rate_in, doc_start, base_pos)

    (head_out, end_state), delta_back = jax.vjp(
        delta_piece, query_low, key_low, value_low, strength, incoming
    )
    head_val, head_back = jax.vjp(norm_rows, head_out, head_gain.astype(jnp.float32))
    normed = head_val.astype(jnp.bfloat16).reshape(batch_size, local_len, D)
    middle = inputs + jnp.dot(normed, out_full, preferred_element_type=jnp.float32)
    mid_val, mid_back = jax.vjp(norm_rows, middle, gain_second.astype(jnp.float32))
    normed_mid = mid_val.astype(jnp.bfloat16)
    gate_up = jnp.dot(normed_mid, gate_full, preferred_element_type=jnp.float32)
    hidden_val, swiglu_back = jax.vjp(swiglu, gate_up)
    hidden = hidden_val.astype(jnp.bfloat16)
    output = (middle + jnp.dot(hidden, down_full, preferred_element_type=jnp.float32)).astype(
        jnp.bfloat16
    )
    qkv_back, beta_back, out_back, gate_back, down_back = (
        lax.all_gather(qkv_weight, "group", axis=0, tiled=True),
        lax.all_gather(beta_weight, "group", axis=0, tiled=True),
        lax.all_gather(out_weight, "group", axis=0, tiled=True),
        lax.all_gather(gate_up_weight, "group", axis=0, tiled=True),
        lax.all_gather(down_weight, "group", axis=0, tiled=True),
    )
    hidden_grad = jnp.einsum(
        "bld,fd->blf", cotangent, down_back, preferred_element_type=jnp.float32
    )
    gate_up_cot = swiglu_back(hidden_grad)[0].astype(jnp.bfloat16)
    mid_in_grad = jnp.einsum(
        "blf,df->bld", gate_up_cot, gate_back, preferred_element_type=jnp.float32
    )
    middle_grad, gain_second_grad = mid_back(mid_in_grad)
    middle_grad = cotangent.astype(jnp.float32) + middle_grad
    branch_cot = middle_grad.astype(jnp.bfloat16)
    normed_grad = jnp.einsum(
        "ble,de->bld", branch_cot, out_back, preferred_element_type=jnp.float32
    )
    head_grad, head_gain_part = head_back(normed_grad.reshape(head_out.shape))
    query_one, key_one, value_one, rate_one, local_add = delta_back(
        (head_grad, jnp.zeros_like(end_state))
    )
    back_map = jnp.swapaxes(transfer, -1, -2)
    later_grad = zero_state
    for step_index in range(group_size - 1):
        outgoing_grad = (
            jnp.einsum("bhij,bhjk->bhik", back_map, later_grad, precision=HIGH) + local_add
        )
        later_grad = shifted(outgoing_grad.astype(jnp.bfloat16), "group", -1).astype(
            outgoing_grad.dtype
        )
    query_two, key_two, value_two, rate_two, unused_grad = delta_back(
        (jnp.zeros_like(head_out), later_grad)
    )
    logit_grad = (rate_one + rate_two) * strength * (1.0 - strength)
    ext_grad, conv_part = conv_back(
        (query_one + query_two, key_one + key_two, value_one + value_two)
    )
    rim_back = shifted(ext_grad[:, : CONV - 1].astype(jnp.bfloat16), "group", -1).astype(
        jnp.float32
    )
    proj_grad = ext_grad[:, CONV - 1 :]
    proj_grad = proj_grad.at[:, local_len - (CONV - 1) :].add(rim_back)
    proj_cot = proj_grad.astype(jnp.bfloat16)
    in_grad = jnp.einsum("blc,dc->bld", proj_cot, qkv_back, preferred_element_type=jnp.float32)
    in_grad = in_grad + jnp.einsum(
        "blh,dh->bld", logit_grad, beta_back.astype(jnp.float32), precision=HIGH
    )
    input_part, gain_first_grad = first_back(in_grad)
    input_grad = middle_grad + input_part
    flat_in = normed_in.reshape(-1, D)
    flat_proj = proj_cot.reshape(-1, 3 * D)
    flat_normed = normed.reshape(-1, D)
    flat_branch = branch_cot.reshape(-1, D)
    flat_mid = normed_mid.reshape(-1, D)
    flat_gate = gate_up_cot.reshape(-1, 2 * FF)
    flat_hidden = hidden.reshape(-1, FF)
    flat_cot = cotangent.reshape(-1, D)
    first_part = jnp.einsum("nr,nc->rc", flat_in, flat_proj, preferred_element_type=jnp.float32)
    second_part = jnp.einsum(
        "nr,nc->rc", flat_normed, flat_branch, preferred_element_type=jnp.float32
    )
    attn_sum = lax.psum_scatter(
        jnp.concatenate([first_part, second_part], axis=1).astype(jnp.bfloat16),
        "group",
        scatter_dimension=0,
        tiled=True,
    )
    ffn_sum = lax.psum_scatter(
        jnp.einsum("nr,nc->rc", flat_mid, flat_gate, preferred_element_type=jnp.float32).astype(
            jnp.bfloat16
        ),
        "group",
        scatter_dimension=0,
        tiled=True,
    )
    down_sum = lax.psum_scatter(
        jnp.einsum("nr,nc->rc", flat_hidden, flat_cot, preferred_element_type=jnp.float32).astype(
            jnp.bfloat16
        ),
        "group",
        scatter_dimension=0,
        tiled=True,
    )
    beta_part = jnp.einsum(
        "nd,nh->dh", flat_in.astype(jnp.float32), logit_grad.reshape(-1, HEADS), precision=HIGH
    )
    head_tile = jnp.broadcast_to(head_gain_part[None, :], (group_size, HEAD_DIM))
    small_sum = (
        lax.psum_scatter(
            gain_first_grad.astype(jnp.bfloat16), "group", scatter_dimension=0, tiled=True
        ).astype(jnp.float32),
        lax.psum_scatter(
            conv_part.astype(jnp.bfloat16), "group", scatter_dimension=0, tiled=True
        ).astype(jnp.float32),
        lax.psum_scatter(
            beta_part.astype(jnp.bfloat16), "group", scatter_dimension=0, tiled=True
        ).astype(jnp.float32),
        lax.psum_scatter(
            gain_second_grad.astype(jnp.bfloat16), "group", scatter_dimension=0, tiled=True
        ).astype(jnp.float32),
        lax.psum_scatter(
            head_tile.astype(jnp.bfloat16), "group", scatter_dimension=0, tiled=True
        ).astype(jnp.float32),
    )
    totals = (
        lax.psum(small_sum[0].astype(jnp.bfloat16), "replica").astype(jnp.float32),
        lax.psum(small_sum[1].astype(jnp.bfloat16), "replica").astype(jnp.float32),
        lax.psum(small_sum[2].astype(jnp.bfloat16), "replica").astype(jnp.float32),
        lax.psum(small_sum[3].astype(jnp.bfloat16), "replica").astype(jnp.float32),
        lax.psum(small_sum[4].astype(jnp.bfloat16), "replica").astype(jnp.float32),
        lax.psum(attn_sum, "replica").astype(jnp.float32),
        lax.psum(ffn_sum, "replica").astype(jnp.float32),
        lax.psum(down_sum, "replica").astype(jnp.float32),
    )
    (
        norm_gain_grad,
        conv_grad,
        beta_grad,
        ffn_gain_grad,
        head_rows,
        attn_total,
        gate_up_grad,
        down_grad,
    ) = totals
    qkv_grad = attn_total[:, : 3 * D]
    out_grad = attn_total[:, 3 * D :]
    return (
        output,
        input_grad,
        norm_gain_grad,
        qkv_grad,
        conv_grad,
        beta_grad,
        head_rows[0],
        out_grad,
        ffn_gain_grad,
        gate_up_grad,
        down_grad,
    )


def solution(mesh):
    placed = (
        P("replica", "group", None),
        P("replica", "group", None),
        P("replica", "group"),
        P("group"),
        P("group", None),
        P("group", None),
        P("group", None),
        P(),
        P("group", None),
        P("group"),
        P("group", None),
        P("group", None),
    )
    return jax.shard_map(
        body,
        mesh=mesh,
        in_specs=placed,
        out_specs=(
            P("replica", "group", None),
            P("replica", "group", None),
            P("group"),
            P("group", None),
            P("group", None),
            P("group", None),
            P(),
            P("group", None),
            P("group"),
            P("group", None),
            P("group", None),
        ),
        check_vma=False,
    )
```

profile of v0, /device:TPU:0, one launch (start us, length us, event | category | flops | bytes accessed | tf_op | source)
XLA Modules:
  0.0 4779.8 jit_solution(4236827815166441751)
XLA Ops:
  37.8 31.3 all_gather.32
  69.7 368.9 %all-gather.7.cloned.1.call-done = bf16[2048,6144]{1,0:T(8,128)(2,1)} async-done(((bf16[512,6144]{1,0:T(8,128)(2,1)}), bf16[2048,6144]{1,0:T(8,128)(2,1)}) %all-gather.7.cloned.1.call-update) | async-done | bytes 25165840 | tf_op jit(solution)/shard_map/all_gather | solution.py:163
  473.6 371.2 %while.114 = (s32[]{:T(128)}, f32[1,16,128,128]{3,2,1,0:T(8,128)}, s32[4,1,64]{2,1,0:T(1,128)S(1)}, s32[4]{0:T(128)S(1)}, s32[]{:T(128)}, /*index=5*/f32[4,1,64,...) while((s32[]{:T(128)}, f32[1,16,128,128]{3,2,1,0:T(8,128)}, ...), condition=%wide.region_5.7_spmd.clone, body=%wide.region_4.6_spmd.clone.sunk | while | flops 522039872 | bytes 7792166 | solution.py:103
  478.3 79.4 %custom-call.40 = f32[16,1,64,64]{2,3,1,0:T(8,128)S(1)} custom-call(f32[16,1,64,64]{3,2,1,0:T(8,128)} %fusion.602), custom_call_target="InvertDiagBlocksLowerTriangular" | custom-call | tf_op jit(solution)/shard_map/while/body/eval_jaxpr/jit(_solve_triangular)/vmap()/triangular_solve/custom-call.1 | solution.py:62
  570.2 79.4 %custom-call.40 = f32[16,1,64,64]{2,3,1,0:T(8,128)S(1)} custom-call(f32[16,1,64,64]{3,2,1,0:T(8,128)} %fusion.602), custom_call_target="InvertDiagBlocksLowerTriangular" | custom-call | tf_op jit(solution)/shard_map/while/body/eval_jaxpr/jit(_solve_triangular)/vmap()/triangular_solve/custom-call.1 | solution.py:62
  663.4 79.4 %custom-call.40 = f32[16,1,64,64]{2,3,1,0:T(8,128)S(1)} custom-call(f32[16,1,64,64]{3,2,1,0:T(8,128)} %fusion.602), custom_call_target="InvertDiagBlocksLowerTriangular" | custom-call | tf_op jit(solution)/shard_map/while/body/eval_jaxpr/jit(_solve_triangular)/vmap()/triangular_solve/custom-call.1 | solution.py:62
  756.6 79.4 %custom-call.40 = f32[16,1,64,64]{2,3,1,0:T(8,128)S(1)} custom-call(f32[16,1,64,64]{3,2,1,0:T(8,128)} %fusion.602), custom_call_target="InvertDiagBlocksLowerTriangular" | custom-call | tf_op jit(solution)/shard_map/while/body/eval_jaxpr/jit(_solve_triangular)/vmap()/triangular_solve/custom-call.1 | solution.py:62
  844.9 370.1 %while.111 = (s32[]{:T(128)}, f32[1,16,128,128]{3,2,1,0:T(8,128)S(1)}, s32[4,1,64]{2,1,0:T(1,128)S(1)}, s32[4]{0:T(128)S(1)}, s32[]{:T(128)}, /*index=5*/f32[4,1...) while((s32[]{:T(128)}, f32[1,16,128,128]{3,2,1,0:T(8,128)S(1)}, ...), condition=%wide.region_3.5_spmd, body=%wide.region_2.0_spmd.sunk | while | flops 521515584 | bytes 7266320 | solution.py:103
  849.6 80.0 %custom-call.37 = f32[16,1,64,64]{2,3,1,0:T(8,128)} custom-call(f32[16,1,64,64]{3,2,1,0:T(8,128)} %fusion.538), custom_call_target="InvertDiagBlocksLowerTriangular" | custom-call | tf_op jit(solution)/shard_map/while/body/eval_jaxpr/jit(_solve_triangular)/vmap()/triangular_solve/custom-call.1 | solution.py:62
  942.0 80.0 %custom-call.37 = f32[16,1,64,64]{2,3,1,0:T(8,128)} custom-call(f32[16,1,64,64]{3,2,1,0:T(8,128)} %fusion.538), custom_call_target="InvertDiagBlocksLowerTriangular" | custom-call | tf_op jit(solution)/shard_map/while/body/eval_jaxpr/jit(_solve_triangular)/vmap()/triangular_solve/custom-call.1 | solution.py:62
  1034.5 80.0 %custom-call.37 = f32[16,1,64,64]{2,3,1,0:T(8,128)} custom-call(f32[16,1,64,64]{3,2,1,0:T(8,128)} %fusion.538), custom_call_target="InvertDiagBlocksLowerTriangular" | custom-call | tf_op jit(solution)/shard_map/while/body/eval_jaxpr/jit(_solve_triangular)/vmap()/triangular_solve/custom-call.1 | solution.py:62
  1127.0 80.0 %custom-call.37 = f32[16,1,64,64]{2,3,1,0:T(8,128)} custom-call(f32[16,1,64,64]{3,2,1,0:T(8,128)} %fusion.538), custom_call_target="InvertDiagBlocksLowerTriangular" | custom-call | tf_op jit(solution)/shard_map/while/body/eval_jaxpr/jit(_solve_triangular)/vmap()/triangular_solve/custom-call.1 | solution.py:62
  1223.8 69.7 %all-gather.1 = bf16[4,1,512]{2,1,0:T(2,128)(2,1)S(1)} all-gather(bf16[1,1,512]{2,1,0:T(2,128)(2,1)S(1)} %reshape.2817), channel_id=1, replica_groups=mesh['replica'=8,'group'=4] {'group'}, dimensions={0}, use_global_device_ids=true | all-gather | bytes 5120 | tf_op jit(solution)/shard_map/all_gather | solution.py:167
  1360.0 449.2 %while.112 = (s32[]{:T(128)}, f32[1,16,128,128]{3,2,1,0:T(8,128)S(1)}, f32[4,1,64,16,128]{4,2,3,1,0:T(8,128)}, f32[4,1,16,64,1]{3,2,4,1,0:T(8,128)}, f32[4,1,16,...) while((s32[]{:T(128)}, ...), condition=%wide.region_8.10_spmd.clone, body=%wide.region_7.9_spmd.clone.sunk | while | flops 1008743232 | bytes 35963288 | solution.py:103
  1370.2 80.0 %custom-call.38 = f32[16,1,64,64]{2,3,1,0:T(8,128)} custom-call(f32[16,1,64,64]{3,2,1,0:T(8,128)} %add_bitcast_fusion.2), custom_call_target="InvertDiagBlocksLowerTriangular" | custom-call | tf_op jit(solution)/shard_map/jvp()/while/body/eval_jaxpr/jit(_solve_triangular)/vmap()/triangular_solve/custom-call.1 | solution.py:62
  1482.3 80.0 %custom-call.38 = f32[16,1,64,64]{2,3,1,0:T(8,128)} custom-call(f32[16,1,64,64]{3,2,1,0:T(8,128)} %add_bitcast_fusion.2), custom_call_target="InvertDiagBlocksLowerTriangular" | custom-call | tf_op jit(solution)/shard_map/jvp()/while/body/eval_jaxpr/jit(_solve_triangular)/vmap()/triangular_solve/custom-call.1 | solution.py:62
  1594.5 80.0 %custom-call.38 = f32[16,1,64,64]{2,3,1,0:T(8,128)} custom-call(f32[16,1,64,64]{3,2,1,0:T(8,128)} %add_bitcast_fusion.2), custom_call_target="InvertDiagBlocksLowerTriangular" | custom-call | tf_op jit(solution)/shard_map/jvp()/while/body/eval_jaxpr/jit(_solve_triangular)/vmap()/triangular_solve/custom-call.1 | solution.py:62
  1706.8 80.0 %custom-call.38 = f32[16,1,64,64]{2,3,1,0:T(8,128)} custom-call(f32[16,1,64,64]{3,2,1,0:T(8,128)} %add_bitcast_fusion.2), custom_call_target="InvertDiagBlocksLowerTriangular" | custom-call | tf_op jit(solution)/shard_map/jvp()/while/body/eval_jaxpr/jit(_solve_triangular)/vmap()/triangular_solve/custom-call.1 | solution.py:62
  1850.9 27.7 fusion.347
  1936.2 468.6 %while.115 = (s32[]{:T(128)}, f32[1,16,128,128]{2,3,1,0:T(8,128)}, f32[4,1,64,16,128]{4,3,2,0,1:T(8,128)}, f32[4,1,64,16,128]{4,3,2,0,1:T(8,128)}, f32[4,1,64,16...) while((s32[]{:T(128)}, f32[1,16,128,128]{2,3,1,0:T(8,128)}, ...), condition=%wide.region_16.19_spmd.clone, body=%wide.region_13.18_spmd.clone.sunk | while | flops 2068196352 | bytes 70763736 | solution.py:103
  1947.7 79.4 %custom-call.41 = f32[16,1,64,64]{2,3,1,0:T(8,128)S(1)} custom-call(f32[16,1,64,64]{3,2,1,0:T(8,128)} %fusion.636), custom_call_target="InvertDiagBlocksLowerTriangular" | custom-call | tf_op jit(solution)/shard_map/transpose(jvp())/while/body/eval_jaxpr/jit(_solve_triangular)/vmap()/triangular_solve | solution.py:62
  2063.9 79.4 %custom-call.41 = f32[16,1,64,64]{2,3,1,0:T(8,128)S(1)} custom-call(f32[16,1,64,64]{3,2,1,0:T(8,128)} %fusion.636), custom_call_target="InvertDiagBlocksLowerTriangular" | custom-call | tf_op jit(solution)/shard_map/transpose(jvp())/while/body/eval_jaxpr/jit(_solve_triangular)/vmap()/triangular_solve | solution.py:62
  2181.4 79.4 %custom-call.41 = f32[16,1,64,64]{2,3,1,0:T(8,128)S(1)} custom-call(f32[16,1,64,64]{3,2,1,0:T(8,128)} %fusion.636), custom_call_target="InvertDiagBlocksLowerTriangular" | custom-call | tf_op jit(solution)/shard_map/transpose(jvp())/while/body/eval_jaxpr/jit(_solve_triangular)/vmap()/triangular_solve | solution.py:62
  2298.9 79.4 %custom-call.41 = f32[16,1,64,64]{2,3,1,0:T(8,128)S(1)} custom-call(f32[16,1,64,64]{3,2,1,0:T(8,128)} %fusion.636), custom_call_target="InvertDiagBlocksLowerTriangular" | custom-call | tf_op jit(solution)/shard_map/transpose(jvp())/while/body/eval_jaxpr/jit(_solve_triangular)/vmap()/triangular_solve | solution.py:62
  2471.4 469.0 %while.113 = (s32[]{:T(128)}, f32[1,16,128,128]{2,3,1,0:T(8,128)S(1)}, f32[4,1,64,16,128]{4,3,2,0,1:T(8,128)}, f32[4,1,64,16,128]{4,3,2,0,1:T(8,128)}, f32[4,1,6...) while((s32[]{:T(128)}, ...), condition=%wide.region_20.23_spmd.clone, body=%wide.region_17.22_spmd.clone.sunk | while | flops 2067147904 | bytes 63664888 | solution.py:103
  2483.4 80.0 %custom-call.39 = f32[16,1,64,64]{2,3,1,0:T(8,128)} custom-call(f32[16,1,64,64]{3,2,1,0:T(8,128)} %fusion.583), custom_call_target="InvertDiagBlocksLowerTriangular" | custom-call | tf_op jit(solution)/shard_map/transpose(jvp())/while/body/eval_jaxpr/jit(_solve_triangular)/vmap()/triangular_solve | solution.py:62
  2600.5 80.0 %custom-call.39 = f32[16,1,64,64]{2,3,1,0:T(8,128)} custom-call(f32[16,1,64,64]{3,2,1,0:T(8,128)} %fusion.583), custom_call_target="InvertDiagBlocksLowerTriangular" | custom-call | tf_op jit(solution)/shard_map/transpose(jvp())/while/body/eval_jaxpr/jit(_solve_triangular)/vmap()/triangular_solve | solution.py:62
  2717.6 80.0 %custom-call.39 = f32[16,1,64,64]{2,3,1,0:T(8,128)} custom-call(f32[16,1,64,64]{3,2,1,0:T(8,128)} %fusion.583), custom_call_target="InvertDiagBlocksLowerTriangular" | custom-call | tf_op jit(solution)/shard_map/transpose(jvp())/while/body/eval_jaxpr/jit(_solve_triangular)/vmap()/triangular_solve | solution.py:62
  2834.7 80.0 %custom-call.39 = f32[16,1,64,64]{2,3,1,0:T(8,128)} custom-call(f32[16,1,64,64]{3,2,1,0:T(8,128)} %fusion.583), custom_call_target="InvertDiagBlocksLowerTriangular" | custom-call | tf_op jit(solution)/shard_map/transpose(jvp())/while/body/eval_jaxpr/jit(_solve_triangular)/vmap()/triangular_solve | solution.py:62
  3081.2 525.7 %reduce-scatter.18.cloned.1.call-done = bf16[512,8192]{1,0:T(8,128)(2,1)} async-done(((bf16[2048,8192]{1,0:T(8,128)(2,1)}), bf16[512,8192]{1,0:T(8,128)(2,1)}) %reduce-scatter.18.cloned.1.call-update) | async-done | bytes 8388624
  3606.9 756.6 %reduce-scatter.12.cloned.1.call-done = bf16[512,11264]{1,0:T(8,128)(2,1)} async-done(((bf16[2048,11264]{1,0:T(8,128)(2,1)}), bf16[512,11264]{1,0:T(8,128)(2,1)}) %reduce-scatter.12.cloned.1.call-update) | async-done | bytes 11534352 | tf_op jit(solution)/shard_map/reduce_scatter | solution.py:293
  4451.5 289.9 %all-reduce.22.cloned.1.call-done = (bf16[512,8192]{1,0:T(8,128)(2,1)}, bf16[512,11264]{1,0:T(8,128)(2,1)}, bf16[1408,2048]{1,0:T(8,128)(2,1)}) async-done(((bf16[512,8192]{1,0:T(8,128)(2,1)}, bf16[512,11264]{1,0:T(8,128)(2,1)}, bf16[1408,2048]{1,0:T(8,128)(2,1)}), (bf16[512,8192]{1,0:T(8,128)(2,1)}, bf16[512,11264]{1,0:T(8,128)(2,1)}, bf16[1408,2048]{1,0:T(8,128)(2,1)})) %all-reduce.22.cloned.1.call-update) | async-done | bytes 25690128 | tf_op jit(solution)/shard_map/psum | solution.py:336
  (1074 shorter events, 1078.6 us)
Async XLA Ops:
  7.2 431.4 %all-gather.7.cloned.1.call-start = ((), (), s32[]{:S(2)}) async-start(), calls=%async_computation.5 | async-start | bytes 31457280 | tf_op jit(solution)/shard_map/all_gather | solution.py:163
  7.9 1808.3 %all-gather.9.cloned.1.call-start = ((), (), s32[]{:S(2)}) async-start(), calls=%async_computation.6 | async-start | bytes 10485760 | tf_op jit(solution)/shard_map/all_gather | solution.py:166
  8.7 1817.4 %all-gather.11.cloned.1.call-start = ((), (), s32[]{:S(2)}) async-start(), calls=%async_computation.7 | async-start | bytes 57671680 | tf_op jit(solution)/shard_map/all_gather | solution.py:168
  9.4 1841.4 %all-gather.13.cloned.1.call-start = ((), (), s32[]{:S(2)}) async-start(), calls=%async_computation.8 | async-start | bytes 28835840 | tf_op jit(solution)/shard_map/all_gather | solution.py:169
  10.0 3071.2 %reduce-scatter.14.cloned.1.call-start = ((), (), s32[]{:S(2)}) async-start(), calls=%async_computation.11 | async-start | bytes 28835840 | tf_op jit(solution)/shard_map/reduce_scatter | solution.py:301
  24.9 435.0 %copy-start.64 = (f32[6144,1]{0,1:T(1,128)}, f32[6144,1]{0,1:T(1,128)S(1)}, u32[]{:S(2)}) copy-start(f32[6144,1]{0,1:T(1,128)S(1)} %get-tuple-element.2068) | copy-start | bytes 73732
  24.9 435.0 %copy-start.66 = (f32[6144,1]{0,1:T(1,128)}, f32[6144,1]{0,1:T(1,128)S(1)}, u32[]{:S(2)}) copy-start(f32[6144,1]{0,1:T(1,128)S(1)} %get-tuple-element.2069) | copy-start | bytes 73732
  24.9 435.0 %copy-start.68 = (f32[6144,1]{0,1:T(1,128)}, f32[6144,1]{0,1:T(1,128)S(1)}, u32[]{:S(2)}) copy-start(f32[6144,1]{0,1:T(1,128)S(1)} %get-tuple-element.2070) | copy-start | bytes 73732
  24.9 435.0 %copy-start.70 = (f32[6144,1]{0,1:T(1,128)}, f32[6144,1]{0,1:T(1,128)S(1)}, u32[]{:S(2)}) copy-start(f32[6144,1]{0,1:T(1,128)S(1)} %get-tuple-element.2071) | copy-start | bytes 73732
  37.0 414.2 %copy-start.58 = (f32[4,1,512]{2,1,0:T(1,128)}, f32[4,1,512]{2,1,0:T(1,128)S(1)}, u32[]{:S(2)}) copy-start(f32[4,1,512]{2,1,0:T(1,128)S(1)} %convert_element_type.473) | copy-start | bytes 24580
  37.8 413.3 %copy-start.82 = (f32[256]{0:T(256)}, f32[256]{0:T(256)S(1)}, u32[]{:S(2)}) copy-start(f32[256]{0:T(256)S(1)} %fusion.359) | copy-start | bytes 3076
  69.2 382.0 %copy-start.60 = (bf16[2048,16]{0,1:T(8,128)(2,1)}, bf16[2048,16]{0,1:T(8,128)(2,1)S(1)}, u32[]{:S(2)}) copy-start(bf16[2048,16]{0,1:T(8,128)(2,1)S(1)} %all_gather.32) | copy-start | bytes 196612
  69.2 390.7 %copy-start.85 = (f32[1,256]{1,0:T(1,128)}, f32[1,256]{1,0:T(1,128)S(1)}, u32[]{:S(2)}) copy-start(f32[1,256]{1,0:T(1,128)S(1)} %get-tuple-element.2072) | copy-start | bytes 3076
  69.2 390.7 %copy-start.87 = (f32[1,256]{1,0:T(1,128)}, f32[1,256]{1,0:T(1,128)S(1)}, u32[]{:S(2)}) copy-start(f32[1,256]{1,0:T(1,128)S(1)} %get-tuple-element.2073) | copy-start | bytes 3076
  69.2 390.7 %copy-start.89 = (f32[1,256]{1,0:T(1,128)}, f32[1,256]{1,0:T(1,128)S(1)}, u32[]{:S(2)}) copy-start(f32[1,256]{1,0:T(1,128)S(1)} %get-tuple-element.2074) | copy-start | bytes 3076
  69.2 390.7 %copy-start.91 = (f32[1,256]{1,0:T(1,128)}, f32[1,256]{1,0:T(1,128)S(1)}, u32[]{:S(2)}) copy-start(f32[1,256]{1,0:T(1,128)S(1)} %get-tuple-element.2075) | copy-start | bytes 3076
  69.7 385.9 %copy-start.78 = (f32[256,16]{0,1:T(8,128)}, f32[256,16]{0,1:T(8,128)S(1)}, u32[]{:S(2)}) copy-start(f32[256,16]{0,1:T(8,128)S(1)} %fusion.326) | copy-start | bytes 49156
  452.9 4.2 collective-permute-start
  1215.0 105.8 %copy-start.1 = (f32[1,16,128,128]{3,2,1,0:T(8,128)}, f32[1,16,128,128]{3,2,1,0:T(8,128)S(1)}, u32[]{:S(2)}) copy-start(f32[1,16,128,128]{3,2,1,0:T(8,128)S(1)} %get-tuple-element.1213) | copy-start | bytes 3145732
  1218.5 75.6 %collective-permute-start.1 = (bf16[1,16,128,128]{3,2,1,0:T(8,128)(2,1)}, bf16[1,16,128,128]{3,2,1,0:T(8,128)(2,1)}, u32[]{:S(2)}, u32[]{:S(2)}) collective-permute-start(bf16[1,16,128,128]{3,2,1,0:T(8,128)(2,1)} %fusion.323), channel_id=1, source_target_pairs={{0,1},{1,2},{2,3},{4,5},{5,6},{6,7},{8,9},{9,10},{10,11},{12,13},{... | collective-permute-start | bytes 1572872 | tf_op jit(solution)/shard_map/ppermute | solution.py:21
  1293.5 610.1 %copy-start.51 = (f32[4,1,512]{2,1,0:T(1,128)}, f32[4,1,512]{2,1,0:T(1,128)S(1)}, u32[]{:S(2)}) copy-start(f32[4,1,512]{2,1,0:T(1,128)S(1)} %convert_element_type.474) | copy-start | bytes 24580
  1296.1 24.7 collective-permute-start.2
  1322.8 33.8 collective-permute-start.3
  1931.6 1675.4 %reduce-scatter.18.cloned.1.call-start = ((), (), s32[]{:S(2)}) async-start(), calls=%async_computation.13 | async-start | bytes 41943040
  2410.6 26.8 collective-permute-start.4
  2438.5 13.1 collective-permute-start.5
  2453.4 12.0 collective-permute-start.6
  3005.1 9.5 collective-permute-start.7
  3053.1 1310.5 %reduce-scatter.12.cloned.1.call-start = ((), (), s32[]{:S(2)}) async-start(), calls=%async_computation.10 | async-start | bytes 57671680 | tf_op jit(solution)/shard_map/reduce_scatter | solution.py:293
  3077.0 1335.1 %reduce-scatter.16.cloned.1.call-start = ((), (), s32[]{:S(2)}) async-start(), calls=%async_computation.12 | async-start | bytes 1966080
  3079.8 1345.0 %reduce-scatter.10.cloned.1.call-start = ((), (), s32[]{:S(2)}) async-start(), calls=%async_computation.9 | async-start | bytes 81920 | tf_op jit(solution)/shard_map/reduce_scatter | solution.py:320
  3081.2 1660.3 %all-reduce.22.cloned.1.call-start = ((), (), s32[]{:S(2)}) async-start(), calls=%async_computation.14 | async-start | bytes 51380224 | tf_op jit(solution)/shard_map/psum | solution.py:336
  (179 other events, 1253.0 us)
Sparse Core Ops, SparseCore 0:
  9.6 428.9 all-gather.6
  440.1 147.8 all-gather.8
  589.6 796.9 all-gather.10
  1388.0 393.3 all-gather.12
  1931.7 397.0 reduce-scatter.13
  3053.2 553.6 reduce-scatter.17
  3609.3 754.1 reduce-scatter.11
  4366.5 37.0 reduce-scatter.15
  4406.5 18.2 reduce-scatter.9
  4428.9 312.5 all-reduce.21
where the time goes:
time: 4790 us; the launch traced here: 4780 us
  waiting for transfers between devices  2040 us (43%)
  other arithmetic  1770 us (37%)
  matrix products  565 us (12%)
  local copies, waits for them, and re-layouts  179 us (4%)
  blocking collectives  164 us (3%)
    another operation x88, other arithmetic, stretch_step(): jax.scipy.linalg.solve_triangular(identity + coupling, target, lower=True...  1620 us
    reduce_scatter x1, waiting for transfers between devices, body(): lax.psum_scatter(jnp.einsum('nr,nc->rc', flat_mid, flat_gate, preferred_e...  757 us
    unnamed x12, waiting for transfers between devices  528 us
    all_gather x1, waiting for transfers between devices, body(): lax.all_gather(qkv_weight, 'group', axis=0, tiled=True)  369 us
    psum x1, waiting for transfers between devices, body(): lax.psum(attn_sum, 'replica').astype(jnp.float32)  290 us
  transfers between devices with their start and end apart: 18, of which 11 were waited for; matrix products, arithmetic and copies ran while one was open for 50% of the time, Pallas kernels for 0%

commit v1 on v0

v1 whole, which is shorter than its diff:
```python
import functools

import jax
import jax.numpy as jnp
from jax import lax
from jax.experimental import pallas as pl
from jax.experimental.pallas import tpu as pltpu
from jax.sharding import PartitionSpec as P

D = 2048
HEADS = 16
HD = 128
FF = 5632
CONV = 4
EPS = 1e-06
RIM = 16
TP = 4
HT = HEADS // TP
DT = D // TP
FT = FF // TP
SCALE = HD**-0.5
VMEM = 56 * 1024 * 1024

BF = jnp.bfloat16
F32 = jnp.float32


def swap(x, bits):
    n = lax.axis_size("replica")
    return lax.ppermute(x, "replica", [(i, i ^ bits) for i in range(n)])


def plane_swap(x, j):
    return swap(x, 2 * j)


def core_swap(x):
    return swap(x, 1)


def far_sum(x):
    x = x.astype(F32)
    bits = 8
    while bits < lax.axis_size("replica"):
        x = x + swap(x.astype(BF), bits).astype(F32)
        bits *= 2
    return x


def z_shift(x, by):
    n = lax.axis_size("group")
    return lax.ppermute(x, "group", [(i, i + by) for i in range(n) if 0 <= i + by < n])


def z_turn(x, by):
    n = lax.axis_size("group")
    return lax.ppermute(x, "group", [(i, (i + by) % n) for i in range(n)])


def plane_copies(x):
    a, b = plane_swap(x, 1), plane_swap(x, 2)
    h = x.shape[0] // 32 * 16 if x.shape[0] >= 32 else x.shape[0] // 2
    d = jnp.concatenate([plane_swap(a[:h], 2), plane_swap(b[h:], 1)], axis=0)
    return [x, a, b, d]


def plane_sum(parts):
    got = [plane_swap(parts[j].astype(BF), j) for j in (1, 2, 3)]
    return parts[0].astype(F32) + got[0].astype(F32) + got[1].astype(F32) + got[2].astype(F32)


def plane_trade(parts):
    return [parts[0]] + [plane_swap(parts[j], j) for j in (1, 2, 3)]


def place(pieces, count, axis=0):
    shape = list(pieces[0][1].shape)
    shape.insert(axis, count)
    buf = jnp.zeros(shape, pieces[0][1].dtype)
    for index, piece in pieces:
        buf = lax.dynamic_update_index_in_dim(buf, piece, index, axis)
    return buf


def pick(x, index, axis=0):
    return lax.dynamic_index_in_dim(x, index, axis, keepdims=False)


def dot(a, b, dims=((1,), (0,))):
    return lax.dot_general(a, b, (dims, ((), ())), preferred_element_type=F32)


NT = ((1,), (1,))
TN = ((0,), (0,))


def dot3(a, b):
    ah, bh = a.astype(BF), b.astype(BF)
    al, bl = (a - ah.astype(F32)).astype(BF), (b - bh.astype(F32)).astype(BF)
    return dot(ah, bh) + (dot(ah, bl) + dot(al, bh))


def iotas(rows, cols):
    return (
        lax.broadcasted_iota(jnp.int32, (rows, cols), 0),
        lax.broadcasted_iota(jnp.int32, (rows, cols), 1),
    )


def unit_lower_inverse(a):
    n = a.shape[0]
    base = 16
    ri, ci = iotas(n, n)
    same = (ri // base) == (ci // base)
    compact = jnp.sum(jnp.where(same, a, 0.0).reshape(n // base, base, n), axis=0)
    lane = lax.broadcasted_iota(jnp.int32, (base, n), 1) % base
    rows = lax.broadcasted_iota(jnp.int32, (base, n), 0)
    spread = jnp.concatenate(
        [jnp.where(lane == j, compact, 0.0) for j in range(base)], axis=0
    )
    ones = same.astype(BF)
    hi = spread.astype(BF)
    lo = (spread - hi.astype(F32)).astype(BF)
    wide = dot(hi, ones) + dot(lo, ones)
    x = (lane == rows).astype(F32)
    for j in range(base - 1):
        x = x - wide[j * base : (j + 1) * base] * x[j : j + 1]
    full = jnp.where(same, jnp.concatenate([x] * (n // base), axis=0), 0.0)
    size = base
    while size < n:
        part = (
            ((ri // (2 * size)) == (ci // (2 * size)))
            & ((ri // size) % 2 == 1)
            & ((ci // size) % 2 == 0)
        )
        full = full - dot3(full, dot3(jnp.where(part, a, 0.0), full))
        size *= 2
    return full


def conv_rows(ext, taps, doc, length):
    pos = lax.broadcasted_iota(jnp.int32, (length, 1), 0)
    total = None
    for i in range(CONV):
        valid = (pos - (CONV - 1) + i >= doc).astype(F32)
        first = RIM - (CONV - 1) + i
        term = ext[first : first + length] * taps[i : i + 1] * valid
        total = term if total is None else total + term
    return total


def masks(doc, length):
    ri, ci = iotas(length, length)
    same = (doc <= ci) & (ri >= ci)
    return same.astype(F32), (same & (ri > ci)).astype(F32)


def ends(doc, length):
    last = doc[length - 1 : length]
    pos = lax.broadcasted_iota(jnp.int32, (length, 1), 0)
    return (pos >= last).astype(F32), (last < 0).astype(F32), (doc < 0).astype(F32)


def front_kernel(q_ref, taps_ref, doc_ref, rate_ref, qo, ko, vo, t_ref, u0_ref, w_ref, m_ref, b_ref):
    length = doc_ref.shape[1]
    doc = doc_ref[0]
    same, strict = masks(doc, length)
    tail, keep, carried = ends(doc, length)
    eye = (iotas(HD, HD)[0] == iotas(HD, HD)[1]).astype(F32)
    for h in range(HT):
        lanes = slice(h * HD, (h + 1) * HD)
        acts = []
        for part in range(3):
            cols = slice(part * DT + h * HD, part * DT + (h + 1) * HD)
            mixed = conv_rows(q_ref[0, :, cols].astype(F32), taps_ref[part, :, lanes], doc, length)
            acts.append(mixed * jax.nn.sigmoid(mixed))
        qa, ka, va = acts
        q = (qa * (lax.rsqrt(jnp.sum(qa * qa, axis=-1, keepdims=True) + EPS) * SCALE)).astype(BF)
        k = (ka * lax.rsqrt(jnp.sum(ka * ka, axis=-1, keepdims=True) + EPS)).astype(BF)
        v = va.astype(BF)
        rate = rate_ref[0, :, h : h + 1]
        inv = unit_lower_inverse(dot(k, k, NT) * (strict * rate)).astype(BF)
        kf = k.astype(F32)
        u0 = dot(inv, (v.astype(F32) * rate).astype(BF))
        w = dot(inv, (kf * (rate * carried)).astype(BF)).astype(BF)
        kl = (kf * tail).astype(BF)
        m_ref[0, h] = eye * keep - dot(kl, w, TN)
        b_ref[0, h] = dot(kl, u0.astype(BF), TN)
        qo[0, :, lanes] = q
        ko[0, :, lanes] = k
        vo[0, :, lanes] = v
        t_ref[0, h] = inv
        u0_ref[0, :, lanes] = u0
        w_ref[0, :, lanes] = w


def out_kernel(q_ref, k_ref, u0_ref, w_ref, s_ref, doc_ref, gain_ref, n_ref, o_ref, u_ref):
    length = doc_ref.shape[1]
    doc = doc_ref[0]
    same, _ = masks(doc, length)
    carried = (doc < 0).astype(F32)
    gain = gain_ref[...]
    for h in range(HT):
        lanes = slice(h * HD, (h + 1) * HD)
        q, k, state = q_ref[0, :, lanes], k_ref[0, :, lanes], s_ref[0, h]
        u = (u0_ref[0, :, lanes] - dot(w_ref[0, :, lanes], state)).astype(BF)
        scores = (dot(q, k, NT) * same).astype(BF)
        o = dot(scores, u) + dot(q, state) * carried
        r = lax.rsqrt(jnp.mean(o * o, axis=-1, keepdims=True) + EPS)
        n_ref[0, :, lanes] = (o * r * gain).astype(BF)
        o_ref[0, :, lanes] = o
        u_ref[0, :, lanes] = u


def back_kernel(
    dn_ref, o_ref, gain_ref, q_ref, k_ref, t_ref, rate_ref, doc_ref, g_ref, y_ref, z_ref, l_ref, hg_ref
):
    length = doc_ref.shape[1]
    doc = doc_ref[0]
    same, _ = masks(doc, length)
    tail, _, carried = ends(doc, length)
    gain = gain_ref[...]

    @pl.when(pl.program_id(0) == 0)
    def _():
        hg_ref[...] = jnp.zeros_like(hg_ref)

    total = jnp.zeros((1, HD), F32)
    for h in range(HT):
        lanes = slice(h * HD, (h + 1) * HD)
        o, dy = o_ref[0, :, lanes], dn_ref[0, :, lanes].astype(F32)
        r = lax.rsqrt(jnp.mean(o * o, axis=-1, keepdims=True) + EPS)
        total = total + jnp.sum(o * r * dy, axis=0, keepdims=True)
        gy = gain * dy
        gf = r * gy - o * (r * r * r * jnp.mean(o * gy, axis=-1, keepdims=True))
        g = gf.astype(BF)
        q, k = q_ref[0, :, lanes], k_ref[0, :, lanes]
        inv = t_ref[0, h]
        scores = (dot(q, k, NT) * same).astype(BF)
        kf = k.astype(F32)
        y = dot(inv, dot(scores, g, TN).astype(BF), TN)
        z_ref[0, :, lanes] = dot(inv, (kf * tail).astype(BF), TN).astype(BF)
        rate = rate_ref[0, :, h : h + 1]
        l_ref[0, h] = dot((q.astype(F32) * carried).astype(BF), g, TN) - dot(
            (kf * (rate * carried)).astype(BF), y.astype(BF), TN
        )
        g_ref[0, :, lanes] = g
        y_ref[0, :, lanes] = y
    hg_ref[0:1] += total


def unit_back(act, dy, scale):
    r = lax.rsqrt(jnp.sum(act * act, axis=-1, keepdims=True) + EPS)
    inner = jnp.sum(act * dy, axis=-1, keepdims=True)
    return (r * scale) * dy - act * (r * r * r * scale * inner)


def grad_kernel(
    p_ref, taps_ref, doc_ref, rate_ref, q_ref, k_ref, v_ref, s_ref, u_ref, g_ref, y_ref, z_ref, a_ref,
    gp_ref, gl_ref, cg_ref,
):
    length = doc_ref.shape[1]
    doc = doc_ref[0]
    same, strict = masks(doc, length)
    tail, _, carried = ends(doc, length)
    pos = lax.broadcasted_iota(jnp.int32, (length, 1), 0)

    @pl.when(pl.program_id(0) == 0)
    def _():
        cg_ref[...] = jnp.zeros_like(cg_ref)

    logits = []
    for h in range(HT):
        lanes = slice(h * HD, (h + 1) * HD)
        q, k, v = q_ref[0, :, lanes], k_ref[0, :, lanes], v_ref[0, :, lanes]
        state, u, g, adj = s_ref[0, h], u_ref[0, :, lanes], g_ref[0, :, lanes], a_ref[0, h]
        rate = rate_ref[0, :, h : h + 1]
        yf = y_ref[0, :, lanes] + dot(z_ref[0, :, lanes], adj)
        y = yf.astype(BF)
        dv = rate * yf
        d1 = dot(y, u, NT) * strict
        gram = dot(k, k, NT)
        e = v.astype(F32) - dot(k, state) * carried
        drate = jnp.sum(yf * e, axis=-1, keepdims=True) - jnp.sum(d1 * gram, axis=-1, keepdims=True)
        dgram = (d1 * (-rate)).astype(BF)
        dscore = (dot(g, u, NT) * same).astype(BF)
        dq = dot(dscore, k) + dot(g, state, NT) * carried
        dk = dot(dscore, q, TN) + dot(dgram, k) + dot(dgram, k, TN)
        dk = dk - dot(y, state, NT) * (rate * carried) + dot(u, adj, NT) * tail
        logits.append(drate * rate * (1.0 - rate))
        for part, grad in enumerate((dq, dk, dv)):
            cols = slice(part * DT + h * HD, part * DT + (h + 1) * HD)
            ext = p_ref[0, :, cols].astype(F32)
            taps = taps_ref[part, :, lanes]
            mixed = conv_rows(ext, taps, doc, length)
            s = jax.nn.sigmoid(mixed)
            if part < 2:
                grad = unit_back(mixed * s, grad, SCALE if part == 0 else 1.0)
            gm = grad * (s * (1.0 + mixed * (1.0 - s)))
            total = jnp.zeros((length + RIM, HD), F32)
            for i in range(CONV):
                valid = (pos - (CONV - 1) + i >= doc).astype(F32)
                gv = gm * valid
                first = RIM - (CONV - 1) + i
                cg_ref[part, i : i + 1, lanes] += jnp.sum(
                    gv * ext[first : first + length], axis=0, keepdims=True
                )
                gv = gv * taps[i : i + 1]
                pads = [jnp.zeros((first, HD), F32), gv]
                if RIM - first > 0:
                    pads.append(jnp.zeros((RIM - first, HD), F32))
                total = total + jnp.concatenate(pads, axis=0)
            gp_ref[0, :, cols] = total.astype(BF)
    gl_ref[0] = jnp.concatenate(logits, axis=1)


def block(shape, fixed=False):
    zeros = (0,) * len(shape)
    if fixed:
        return pl.BlockSpec(tuple(shape), lambda i: zeros)
    return pl.BlockSpec((1,) + tuple(shape[1:]), lambda i: (i,) + zeros[1:])


def call(kernel, ins, fixed_ins, outs, fixed_outs=(), flops=0):
    count = ins[0].shape[0]
    size = sum(x.size * x.dtype.itemsize for x in ins)
    for shape, dtype in outs:
        n = 1
        for extent in shape:
            n *= extent
        size += n * jnp.dtype(dtype).itemsize
    return pl.pallas_call(
        kernel,
        grid=(count,),
        in_specs=[block(x.shape, i in fixed_ins) for i, x in enumerate(ins)],
        out_specs=[block(s, i in fixed_outs) for i, (s, _) in enumerate(outs)],
        out_shape=[jax.ShapeDtypeStruct(s, d) for s, d in outs],
        compiler_params=pltpu.CompilerParams(vmem_limit_bytes=VMEM),
        cost_estimate=pl.CostEstimate(flops=flops, bytes_accessed=size, transcendentals=0),
    )(*ins)


def norm_back(x, gain, dy):
    r = lax.rsqrt(jnp.mean(x * x, axis=-1, keepdims=True) + EPS)
    gy = gain * dy
    dx = r * gy - x * (r * r * r * jnp.mean(x * gy, axis=-1, keepdims=True))
    return dx, jnp.sum((x * r * dy).reshape(-1, x.shape[-1]), axis=0)


def norm_rows(x, gain):
    return (x * lax.rsqrt(jnp.mean(x * x, axis=-1, keepdims=True) + EPS) * gain).astype(BF)


def mm(a, b, dims=((1,), (0,))):
    return lax.dot_general(a, b, (dims, ((), ())), preferred_element_type=F32)


def body(
    tokens,
    cotangent,
    doc_start,
    norm_gain,
    qkv_weight,
    conv_weight,
    beta_weight,
    head_gain,
    out_weight,
    ffn_gain,
    gate_up_weight,
    down_weight,
):
    groups = lax.axis_size("group")
    r = lax.axis_index("replica") % 8
    g = lax.axis_index("group")
    c, t = r % 2, r // 2
    batch, length, _ = tokens.shape
    rows = batch * length
    seqs = TP * batch
    ext_len = length + RIM
    shard = D // groups
    half = shard // 2
    ff_shard = FF // groups
    col = D // 8

    def z_pieces(x):
        return [(g, x)] + [((g - s) % groups, z_turn(x, s)) for s in range(1, groups)]

    gain_in = place(z_pieces(norm_gain.reshape(1, shard)), groups).reshape(D).astype(F32)
    small = jnp.concatenate(
        [ffn_gain.reshape(-1), beta_weight.reshape(-1), conv_weight.reshape(-1)]
    ).reshape(-1, 128)
    small = place(z_pieces(small), groups).reshape(groups, -1)
    gain_mid = small[:, :shard].reshape(D).astype(F32)
    beta_full = small[:, shard : shard * (1 + HEADS)].reshape(D, HEADS)
    conv_full = small[:, shard * (1 + HEADS) :].reshape(3, TP, DT, CONV)
    beta_t = lax.dynamic_slice(beta_full, (0, t * HT), (D, HT))
    taps = jnp.swapaxes(pick(conv_full, t, 1), 1, 2).astype(F32)
    gain_head = head_gain.astype(F32).reshape(1, HD)

    rim = z_shift(tokens[:, length - RIM :], 1)
    inputs = tokens.astype(F32)
    ext = jnp.concatenate([rim, tokens], axis=1).astype(F32)
    normed_ext = norm_rows(ext, gain_in)
    normed_all = jnp.concatenate(plane_copies(normed_ext.reshape(batch * ext_len, D)), axis=0)
    doc_rel = doc_start - g * length
    docs = jnp.concatenate(
        [doc_rel] + [plane_swap(doc_rel, j) for j in (1, 2, 3)], axis=0
    ).reshape(seqs, length, 1)

    piece = jnp.concatenate(
        [lax.dynamic_slice(qkv_weight, (c * half, j * D + t * DT), (half, DT)) for j in range(3)], axis=1
    )
    qkv = jnp.zeros((groups, 2, half, 3 * DT), BF)
    for index, part in z_pieces(piece):
        qkv = lax.dynamic_update_slice(qkv, part[None, None], (index, c, 0, 0))
        qkv = lax.dynamic_update_slice(qkv, core_swap(part)[None, None], (index, 1 - c, 0, 0))
    qkv = qkv.reshape(D, 3 * DT)

    projected = mm(normed_all, qkv).astype(BF).reshape(seqs, ext_len, 3 * DT)
    logits = mm(normed_all, beta_t).reshape(seqs, ext_len, HT)[:, RIM:]
    rates = jax.nn.sigmoid(logits)

    piece = lax.dynamic_slice(down_weight, (0, r * col), (ff_shard, col))
    piece = lax.all_gather(piece, "group", axis=0, tiled=True).reshape(TP, FT, col)
    got = plane_trade([pick(piece, t ^ j) for j in range(TP)])
    other = core_swap(jnp.stack(got))
    down = place(
        [((t ^ j) * 2 + c, got[j]) for j in range(TP)]
        + [((t ^ j) * 2 + 1 - c, other[j]) for j in range(TP)],
        8,
    )
    down = jnp.swapaxes(down, 0, 1).reshape(FT, D)

    piece = jnp.concatenate(
        [
            lax.dynamic_slice(gate_up_weight, (c * half, j * FF + t * FT), (half, FT))
            for j in range(2)
        ],
        axis=1,
    )
    piece = lax.all_gather(piece, "group", axis=0)
    gate_up_w = place([(c, piece), (1 - c, core_swap(piece))], 2, 1).reshape(D, 2 * FT)

    piece = lax.dynamic_slice(out_weight, (r * (shard // 8), 0), (shard // 8, D))
    piece = place(z_pieces(piece), groups)
    got = plane_copies(piece)
    other = core_swap(jnp.stack(got))
    out_w = place(
        [((t ^ j) * 2 + c, got[j]) for j in range(TP)]
        + [((t ^ j) * 2 + 1 - c, other[j]) for j in range(TP)],
        8,
        1,
    ).reshape(TP, DT, D)
    out_rel = jnp.concatenate([pick(out_w, t ^ j) for j in range(TP)], axis=0)

    cot = cotangent.reshape(rows, D)
    cot_all = jnp.concatenate(plane_copies(cot), axis=0)

    wide = (seqs, length, DT)
    square = (seqs, HT, HD, HD)
    queries, key_rows, value_rows, inverse, u0, w, move, free = call(
        front_kernel,
        [projected, taps, docs, rates],
        (1,),
        [
            (wide, BF),
            (wide, BF),
            (wide, BF),
            ((seqs, HT, length, length), BF),
            (wide, F32),
            (wide, BF),
            (square, F32),
            (square, F32),
        ],
        flops=seqs * HT * length * length * (24 * 2 * length + 3 * 2 * HD),
    )
    state = jnp.zeros(square, BF)
    for _ in range(groups - 1):
        leaving = (
            jnp.einsum("shij,shjk->shik", move.astype(BF), state, preferred_element_type=F32) + free
        )
        state = z_shift(leaving.astype(BF), 1)
    normed, head_out, update = call(
        out_kernel,
        [queries, key_rows, u0, w, state, docs, gain_head],
        (6,),
        [(wide, BF), (wide, F32), (wide, BF)],
        flops=seqs * HT * length * 2 * HD * (2 * length + 2 * HD),
    )
    got = plane_trade([normed[j * batch : (j + 1) * batch].reshape(rows, DT) for j in range(TP)])
    normed_rel = jnp.concatenate(got, axis=1)
    normed_abs = jnp.swapaxes(place([(t ^ j, got[j]) for j in range(TP)], TP), 0, 1).reshape(rows, D)
    middle = inputs.reshape(rows, D) + mm(normed_rel, out_rel)
    normed_mid = norm_rows(middle, gain_mid)
    mid_all = jnp.concatenate(plane_copies(normed_mid), axis=0)

    gate_up = mm(mid_all, gate_up_w)
    grad_hidden = mm(cot_all, down, NT)
    gate, up = gate_up[:, :FT], gate_up[:, FT:]
    sg = jax.nn.sigmoid(gate)
    hidden = (gate * sg * up).astype(BF)
    grad_gate_up = jnp.concatenate(
        [
            (grad_hidden * up * (sg * (1.0 + gate * (1.0 - sg)))).astype(BF),
            (grad_hidden * gate * sg).astype(BF),
        ],
        axis=1,
    )
    mid_part = mm(grad_gate_up, gate_up_w, NT).astype(BF).reshape(TP, rows, D)
    grad_mid = plane_sum([mid_part[j] for j in range(TP)])
    out_part = mm(hidden, down).astype(BF).reshape(TP, rows, D)
    output = (middle + plane_sum([out_part[j] for j in range(TP)])).astype(BF)

    dx, ffn_gain_part = norm_back(middle, gain_mid, grad_mid)
    grad_middle = cot.astype(F32) + dx
    branch = grad_middle.astype(BF)
    dnormed = mm(branch, out_rel, NT).astype(BF)
    got = plane_trade([dnormed[:, j * DT : (j + 1) * DT] for j in range(TP)])
    dnormed = jnp.concatenate(got, axis=0).reshape(wide)

    grad_out, y0, z, local, head_part = call(
        back_kernel,
        [dnormed, head_out, gain_head, queries, key_rows, inverse, rates, docs],
        (2,),
        [(wide, BF), (wide, F32), (wide, BF), (square, F32), ((8, HD), F32)],
        (4,),
        flops=seqs * HT * length * 2 * HD * (4 * length + 2 * HD),
    )
    later = jnp.zeros(square, BF)
    for _ in range(groups - 1):
        leaving = (
            jnp.einsum("shji,shjk->shik", move.astype(BF), later, preferred_element_type=F32) + local
        )
        later = z_shift(leaving.astype(BF), -1)
    grad_proj, grad_logit, conv_part = call(
        grad_kernel,
        [
            projected, taps, docs, rates, queries, key_rows, value_rows, state, update, grad_out, y0, z, later,
        ],
        (1,),
        [((seqs, ext_len, 3 * DT), BF), ((seqs, length, HT), F32), ((3, CONV, DT), F32)],
        (2,),
        flops=seqs * HT * length * 2 * HD * (7 * length + 5 * HD),
    )
    grad_proj = grad_proj.reshape(seqs * ext_len, 3 * DT)

    logit_ext = jnp.pad(grad_logit, ((0, 0), (RIM, 0), (0, 0))).reshape(seqs * ext_len, HT).astype(BF)
    in_part = mm(grad_proj, qkv, NT) + mm(logit_ext, beta_t, NT)
    in_part = in_part.astype(BF).reshape(TP, batch, ext_len, D)
    grad_in = plane_sum([in_part[j] for j in range(TP)])
    back_rim = z_shift(grad_in[:, :RIM].astype(BF), -1).astype(F32)
    grad_in = grad_in[:, RIM:]
    grad_in = jnp.concatenate(
        [grad_in[:, : length - RIM], grad_in[:, length - RIM :] + back_rim], axis=1
    )
    dx, norm_gain_part = norm_back(inputs, gain_in, grad_in)
    input_grad = grad_middle.reshape(batch, length, D) + dx

    def two_halves(left, right):
        parts = left.reshape(-1, groups, 2, half)
        away = mm(pick(parts, 1 - c, 2).reshape(-1, groups * half), right, TN).astype(BF)
        mine = mm(pick(parts, c, 2).reshape(-1, groups * half), right, TN)
        return (mine + core_swap(away).astype(F32)).astype(BF).reshape(groups, half, -1)

    def columns(x, core):
        parts = x.reshape(-1, TP, 2, col)
        return jnp.concatenate([pick(pick(parts, t ^ j, 1), core, 1) for j in range(TP)], axis=1)

    def two_columns(left, right):
        away = mm(left, columns(right, 1 - c), TN).astype(BF)
        mine = mm(left, columns(right, c), TN)
        return (mine + core_swap(away).astype(F32)).astype(BF)

    def spread(x):
        got = plane_copies(x)
        mine = jnp.stack(got)
        other = core_swap(mine)
        return place(
            [((t ^ j) * 2 + c, got[j]) for j in range(TP)]
            + [((t ^ j) * 2 + 1 - c, other[j]) for j in range(TP)],
            8,
        )

    gate_sum = two_halves(mid_all, grad_gate_up)
    gate_sum = far_sum(lax.psum_scatter(gate_sum, "group", scatter_dimension=0)).astype(BF)
    gate_sum = spread(gate_sum).reshape(TP, 2, half, 2, FT)
    gate_up_grad = gate_sum.transpose(1, 2, 3, 0, 4).reshape(shard, 2 * FF).astype(F32)

    down_sum = two_columns(hidden, cot_all)
    got = plane_trade([down_sum[:, j * col : (j + 1) * col] for j in range(TP)])
    down_sum = place([(t ^ j, got[j]) for j in range(TP)], TP).reshape(groups, ff_shard, col)
    down_sum = far_sum(lax.psum_scatter(down_sum, "group", scatter_dimension=0)).astype(BF)
    down_grad = jnp.swapaxes(spread(down_sum), 0, 1).reshape(ff_shard, D).astype(F32)

    out_sum = two_columns(normed_abs, branch)
    out_sum = plane_sum([out_sum[:, j * col : (j + 1) * col] for j in range(TP)]).astype(BF)

    def z_sum(x):
        total = pick(x, g).astype(F32)
        for s in range(1, groups):
            total = total + z_turn(pick(x, (g + s) % groups), s).astype(F32)
        return total

    out_sum = far_sum(z_sum(out_sum.reshape(groups, shard, col))).astype(BF)
    out_grad = jnp.swapaxes(spread(out_sum), 0, 1).reshape(shard, D).astype(F32)

    qkv_sum = far_sum(z_sum(two_halves(normed_all, grad_proj))).astype(BF)
    qkv_sum = spread(qkv_sum).reshape(TP, 2, half, 3, DT)
    qkv_grad = qkv_sum.transpose(1, 2, 3, 0, 4).reshape(shard, 3 * D).astype(F32)

    beta_part = mm(normed_all, logit_ext, TN)
    beta_all = lax.dynamic_update_slice(jnp.zeros((D, HEADS), F32), beta_part, (0, t * HT))
    conv_all = place([(t, jnp.swapaxes(conv_part, 1, 2))], TP, 1)
    pack = jnp.concatenate(
        [
            norm_gain_part.reshape(groups, -1),
            ffn_gain_part.reshape(groups, -1),
            jnp.broadcast_to(head_part[:1], (groups, HD)),
            beta_all.reshape(groups, -1),
            conv_all.reshape(groups, -1),
        ],
        axis=1,
    ).reshape(groups, -1, 128)
    total = far_sum(z_sum(pack))
    total = total + core_swap(total)
    total = total + plane_swap(total, 1)
    total = (total + plane_swap(total, 2)).reshape(-1)
    sizes = [shard, shard, HD, shard * HEADS, 3 * D // groups * CONV]
    at = [0]
    for size in sizes:
        at.append(at[-1] + size)
    norm_gain_grad, ffn_gain_grad, head_gain_grad, beta_grad, conv_grad = [
        total[at[i] : at[i + 1]] for i in range(5)
    ]
    return (
        output.reshape(batch, length, D),
        input_grad,
        norm_gain_grad,
        qkv_grad,
        conv_grad.reshape(-1, CONV),
        beta_grad.reshape(-1, HEADS),
        head_gain_grad,
        out_grad,
        ffn_gain_grad,
        gate_up_grad,
        down_grad,
    )


def solution(mesh):
    rows = P("replica", "group", None)
    shard = P("group", None)
    return jax.shard_map(
        body,
        mesh=mesh,
        in_specs=(
            rows, rows, P("replica", "group"), P("group"), shard, shard, shard, P(), shard, P("group"), shard, shard,
        ),
        out_specs=(
            rows, rows, P("group"), shard, shard, shard, P(), shard, P("group"), shard, shard,
        ),
        check_vma=False,
    )
```

time: 4790 us -> 1550 us (0.32)
  other arithmetic: 1770 us -> 98.3 us
  waiting for transfers between devices: 2040 us -> 371 us
  matrix products: 565 us -> 157 us
  local copies, waits for them, and re-layouts: 179 us -> 585 us
  starting transfers between devices: 27.5 us -> 200 us
  blocking collectives: 164 us -> 0 us
  Pallas kernels: 0 us -> 107 us
    another operation x97 -> x7, other arithmetic: 1620 us -> 19.2 us  [the longest x4 11.3 us: spread(): mine = jnp.stack(got)]
    reduce_scatter x3 -> x2, waiting for transfers between devices: 768 us -> 0.01 us  [the longest x1 0.01 us: body(): lax.psum_scatter(down_sum, 'group', scatter_dimension=0)]
    unnamed x12 -> x4, waiting for transfers between devices: 528 us -> 0.07 us
    all_gather x4 -> x2, waiting for transfers between devices: 369 us -> 0.01 us  [the longest x1 0.01 us: body(): lax.all_gather(piece, 'group', axis=0, tiled=True).reshape(TP, FT, col)]
    dot_general x173 -> x25, matrix products: 504 us -> 157 us  [the longest x19 149 us: mm(): return lax.dot_general(a, b, (dims, ((), ())), preferred_element_type=F32)]
    psum x1 -> x0, waiting for transfers between devices: 290 us -> none  [body(): lax.psum(attn_sum, 'replica').astype(jnp.float32)]
    ppermute x8 -> x106, waiting for transfers between devices: 81.6 us -> 370 us  [the longest x77 216 us: swap(): return lax.ppermute(x, 'replica', [(i, i ^ bits) for i in range(n)])]
    ppermute x8 -> x106, starting transfers between devices: 27.1 us -> 200 us  [the longest x77 72 us: swap(): return lax.ppermute(x, 'replica', [(i, i ^ bits) for i in range(n)])]
  transfers between devices with their start and end apart: 18 -> 110, of which waited for: 11 -> 35; matrix products, arithmetic and copies ran while one was open for 50% -> 45% of each run, Pallas kernels for 0% -> 7%
where the time goes in v1:
time: 1550 us; the launch traced here: 1530 us
  local copies, waits for them, and re-layouts  585 us (38%)
  waiting for transfers between devices  371 us (24%)
  starting transfers between devices  200 us (13%)
  matrix products  157 us (10%)
  Pallas kernels  107 us (7%)
  other arithmetic  98.3 us (6%)
  between operations  16.1 us (1%)
    ppermute x77, waiting for transfers between devices, swap(): return lax.ppermute(x, 'replica', [(i, i ^ bits) for i in range(n)])  216 us
    dynamic_update_slice x67, local copies, waits for them, and re-layouts, place(): buf = lax.dynamic_update_index_in_dim(buf, piece, index, axis)  161 us
    dot_general x19, matrix products, mm(): return lax.dot_general(a, b, (dims, ((), ())), preferred_element_type=F32)  149 us
    ppermute x21, waiting for transfers between devices, z_turn(): return lax.ppermute(x, 'group', [(i, (i + by) % n) for i in range(n)])  124 us
    pallas_call x4, Pallas kernels, call(): pl.pallas_call(kernel, grid=(count,), in_specs=[block(x.shape, i in fixed...  107 us
    unnamed x249, local copies, waits for them, and re-layouts  83.3 us
    ppermute x77, starting transfers between devices, swap(): return lax.ppermute(x, 'replica', [(i, i ^ bits) for i in range(n)])  72 us
    ppermute x21, starting transfers between devices, z_turn(): return lax.ppermute(x, 'group', [(i, (i + by) % n) for i in range(n)])  66.1 us
  transfers between devices with their start and end apart: 110, of which 35 were waited for; matrix products, arithmetic and copies ran while one was open for 45% of the time, Pallas kernels for 7%

profile of v1, /device:TPU:0, one launch (start us, length us, event | category | flops | bytes accessed | tf_op | source)
XLA Modules:
  0.0 1534.6 jit_solution(11339821711075299553)
XLA Ops:
  64.7 10.5 collective-permute-done.15
  115.5 12.2 collective-permute-done.9
  141.0 48.2 %collective-permute-done.11 = bf16[256,1536]{1,0:T(8,128)(2,1)} collective-permute-done((bf16[256,1536]{1,0:T(8,128)(2,1)}, bf16[256,1536]{1,0:T(8,128)(2,1)}, u32[]{:S(2)}, u32[]{:S(2)}) %collective-permute-start.11) | collective-permute-done | bytes 786464 | tf_op jit(solution)/shard_map/ppermute | solution.py:57
  247.9 12.1 convolution_convert_fusion
  266.4 59.9 %shard_map.203 = (bf16[4,256,512]{2,1,0:T(8,128)(2,1)}, bf16[4,256,512]{2,1,0:T(8,128)(2,1)}, bf16[4,256,512]{2,1,0:T(8,128)(2,1)}, bf16[4,4,256,256]{3,2,1,0:T(...) custom-call(bf16[4,272,1536]{2,1,0:T(8,128)(2,1)} %bitcast.368, ...), custom_call_target="tpu_custom_call" | custom-call | flops 13690208256 | bytes 13873152 | tf_op jit(solution)/shard_map/pallas_call | solution.py:332
  330.2 45.3 %collective-permute-start.21 = (bf16[4,4,128,128]{3,2,1,0:T(8,128)(2,1)}, bf16[4,4,128,128]{3,2,1,0:T(8,128)(2,1)}, u32[]{:S(2)}, u32[]{:S(2)}) collective-permute-start(bf16[4,4,128,128]{3,2,1,0:T(8,128)(2,1)} %fusion.30), channel_id=1, source_target_pairs={{0,1},{1,2},{2,3},{4,5},{5,6},{6,7},{8,9},{9,10},{10,11},{12,13},{... | collective-permute-start | bytes 1572872 | tf_op jit(solution)/shard_map/ppermute | solution.py:52
  496.1 10.5 collective-permute-done.41
  561.3 11.8 constant_dynamic-slice_fusion.9
  573.1 10.6 copy.209
  583.7 10.5 copy.208
  624.2 17.2 %fusion.103 = f32[1024,2816]{1,0:T(8,128)S(1)} fusion(bf16[1024,2048]{1,0:T(8,128)(2,1)} %constant_dynamic-update-slice_fusion.7, bf16[2048,2816]{1,0:T(8,128)(2,1)} %bitcast.344), kind=kOutput, calls=%fused_computation.333 | convolution fusion | flops 11811160064 | bytes 27262976 | tf_op jit(solution)/shard_map/dot_general | solution.py:355
  641.4 14.1 multiply_convert_fusion.1
  655.5 16.9 %convolution_convert_fusion.2 = bf16[1024,2048]{1,0:T(8,128)(2,1)S(1)} fusion(bf16[2048,2816]{1,0:T(8,128)(2,1)} %bitcast.345, bf16[1024,1408]{1,0:T(8,128)(2,1)} %get-tuple-element.88, bf16[1024,1408]{1,0:T(8,128)(2,1)S(1)} %get-tuple-element.87), kind=kOutput, calls=%fused_computation.24 | convolution fusion | flops 11824791552 | bytes 21495808 | tf_op jit(solution)/shard_map/dot_general | solution.py:355
  687.8 12.1 collective-permute-done.53
  705.5 16.8 %collective-permute-done.52 = bf16[256,2048]{1,0:T(8,128)(2,1)S(1)} collective-permute-done((bf16[256,2048]{1,0:T(8,128)(2,1)S(1)}, bf16[256,2048]{1,0:T(8,128)(2,1)S(1)}, u32[]{:S(2)}, u32[]{:S(2)}) %collective-permute-start.52) | collective-permute-done | bytes 1048608 | tf_op jit(solution)/shard_map/ppermute | solution.py:30
  723.6 21.3 %collective-permute-done.46 = bf16[256,2048]{1,0:T(8,128)(2,1)S(1)} collective-permute-done((bf16[256,2048]{1,0:T(8,128)(2,1)S(1)}, bf16[256,2048]{1,0:T(8,128)(2,1)S(1)}, u32[]{:S(2)}, u32[]{:S(2)}) %collective-permute-start.46) | collective-permute-done | bytes 1048608 | tf_op jit(solution)/shard_map/ppermute | solution.py:30
  744.8 19.8 %collective-permute-done.45 = bf16[256,2048]{1,0:T(8,128)(2,1)S(1)} collective-permute-done((bf16[256,2048]{1,0:T(8,128)(2,1)S(1)}, bf16[256,2048]{1,0:T(8,128)(2,1)S(1)}, u32[]{:S(2)}, u32[]{:S(2)}) %collective-permute-start.45) | collective-permute-done | bytes 1048608 | tf_op jit(solution)/shard_map/ppermute | solution.py:30
  796.3 12.9 shard_map.205
  814.4 12.1 collective-permute-done.57
  859.5 28.1 %shard_map.206 = (bf16[4,272,1536]{2,1,0:T(8,128)(2,1)}, f32[4,256,4]{2,1,0:T(8,128)}, f32[3,4,512]{2,1,0:T(4,128)}) custom-call(bf16[4,272,1536]{2,1,0:T(8,128)(2,1)} %bitcast.369, f32[3,4,512]{2,1,0:T(4,128)} %bitcast_bitcast_fusion.taps_ref, s32[4,256,1]{2,1,0:T(8,128)} %copy.104.doc_ref, f32[4,256,4]{2,1,0:T(8,128)} %fusion.50.rate_ref, ...), custom_call_target="tpu_custom_call" | custom-call | flops 2550136832 | bytes 16207872 | tf_op jit(solution)/shard_map/pallas_call | solution.py:332
  951.0 17.9 %collective-permute-done.61 = bf16[1,272,2048]{2,1,0:T(8,128)(2,1)} collective-permute-done((bf16[1,272,2048]{2,1,0:T(8,128)(2,1)}, bf16[1,272,2048]{2,1,0:T(8,128)(2,1)}, u32[]{:S(2)}, u32[]{:S(2)}) %collective-permute-start.61) | collective-permute-done | bytes 1114144 | tf_op jit(solution)/shard_map/ppermute | solution.py:30
  1037.4 21.5 %collective-permute-done.81 = bf16[2048,256]{1,0:T(8,128)(2,1)} collective-permute-done((bf16[2048,256]{1,0:T(8,128)(2,1)}, bf16[2048,256]{1,0:T(8,128)(2,1)}, u32[]{:S(2)}, u32[]{:S(2)}) %collective-permute-start.81) | collective-permute-done | bytes 1048608 | tf_op jit(solution)/shard_map/ppermute | solution.py:30
  1077.0 44.4 %collective-permute-done.85 = bf16[512,256]{1,0:T(8,128)(2,1)S(1)} collective-permute-done((bf16[512,256]{1,0:T(8,128)(2,1)S(1)}, bf16[512,256]{1,0:T(8,128)(2,1)S(1)}, u32[]{:S(2)}, u32[]{:S(2)}) %collective-permute-start.85) | collective-permute-done | bytes 262176 | tf_op jit(solution)/shard_map/ppermute | solution.py:57
  1121.4 33.9 %collective-permute-start.83 = (bf16[512,256]{1,0:T(8,128)(2,1)S(1)}, bf16[512,256]{1,0:T(8,128)(2,1)}, u32[]{:S(2)}, u32[]{:S(2)}) collective-permute-start(bf16[512,256]{1,0:T(8,128)(2,1)S(1)} %get-tuple-element.144), channel_id=1, source_target_pairs={{0,1},{1,2},{2,3},{3,0},{4,5},{5,6},{6,7},{7,4},{8,9},{9,10},{10,1... | collective-permute-start | bytes 786440 | tf_op jit(solution)/shard_map/ppermute | solution.py:57
  1181.9 10.8 collective-permute-done.75
  1322.9 23.8 %collective-permute-done.93 = bf16[256,2816]{0,1:T(8,128)(2,1)S(1)} collective-permute-done((bf16[256,2816]{0,1:T(8,128)(2,1)}, bf16[256,2816]{0,1:T(8,128)(2,1)S(1)}, u32[]{:S(2)}, u32[]{:S(2)}) %collective-permute-start.93) | collective-permute-done | bytes 1441824 | tf_op jit(solution)/shard_map/ppermute | solution.py:30
  1381.4 15.3 copy.139
  1396.6 15.4 %reshape.596 = f32[512,6144]{1,0:T(8,128)} reshape(f32[2,256,3,4,512]{4,3,2,1,0:T(4,128)} %copy.139) | data formatting | bytes 25165824 | tf_op jit(solution)/shard_map/convert_element_type | solution.py:609
  1428.0 11.9 copy.186
  1460.1 13.2 convert_bitcast_fusion
  1473.3 26.5 %copy.163 = f32[2,256,2,4,1408]{4,3,2,1,0:T(4,128)} copy(f32[2,256,2,4,1408]{1,4,2,0,3:T(8,128)} %convert_bitcast_fusion) | data formatting | bytes 46137344 | tf_op jit(solution)/shard_map/convert_element_type | solution.py:587
  1499.8 28.1 %reshape.599 = f32[512,11264]{1,0:T(8,128)} reshape(f32[2,256,2,4,1408]{4,3,2,1,0:T(4,128)} %copy.163) | data formatting | bytes 46137344 | tf_op jit(solution)/shard_map/convert_element_type | solution.py:587
  (749 shorter events, 853.0 us)
Async XLA Ops:
  7.2 462.3 %all-gather.4.cloned.1.call-start = ((), (), s32[]{:S(2)}) async-start(), calls=%async_computation.2 | async-start | bytes 3604480 | tf_op jit(solution)/shard_map/all_gather | solution.py:424
  9.3 484.1 %all-gather.6.cloned.1.call-start = ((), (), s32[]{:S(2)}) async-start(), calls=%async_computation.5 | async-start | bytes 7208960 | tf_op jit(solution)/shard_map/all_gather | solution.py:441
  11.3 89.9 %collective-permute-start.27 = (bf16[64,2048]{1,0:T(8,128)(2,1)}, bf16[64,2048]{1,0:T(8,128)(2,1)}, u32[]{:S(2)}, u32[]{:S(2)}) collective-permute-start(bf16[64,2048]{1,0:T(8,128)(2,1)} %get-tuple-element.86), channel_id=1, source_target_pairs={{0,1},{1,2},{2,3},{3,0},{4,5},{5,6},{6,7},{7,4},{8,9},{9,10},{10,1... | collective-permute-start | bytes 786440 | tf_op jit(solution)/shard_map/ppermute | solution.py:57
  14.3 87.9 %collective-permute-start.28 = (bf16[64,2048]{1,0:T(8,128)(2,1)}, bf16[64,2048]{1,0:T(8,128)(2,1)}, u32[]{:S(2)}, u32[]{:S(2)}) collective-permute-start(bf16[64,2048]{1,0:T(8,128)(2,1)} %get-tuple-element.86), channel_id=1, source_target_pairs={{0,2},{1,3},{2,0},{3,1},{4,6},{5,7},{6,4},{7,5},{8,10},{9,11},{10,... | collective-permute-start | bytes 786440 | tf_op jit(solution)/shard_map/ppermute | solution.py:57
  24.7 1220.3 %reduce-scatter.5.cloned.1.call-start = ((), (), s32[]{:S(2)}) async-start(), calls=%async_computation.4 | async-start | bytes 3604480 | tf_op jit(solution)/shard_map/reduce_scatter | solution.py:592
  101.2 88.0 %collective-permute-start.11 = (bf16[256,1536]{1,0:T(8,128)(2,1)}, bf16[256,1536]{1,0:T(8,128)(2,1)}, u32[]{:S(2)}, u32[]{:S(2)}) collective-permute-start(bf16[256,1536]{1,0:T(8,128)(2,1)} %pad_maximum_fusion.18), channel_id=1, source_target_pairs={{0,2},{1,3},{2,0},{3,1},{4,6},{5,7},{6,4},{7,5},{8,10},{9,11},{10,... | collective-permute-start | bytes 2359304 | tf_op jit(solution)/shard_map/ppermute | solution.py:57
  112.4 86.9 %collective-permute-start.4 = (bf16[272,2048]{1,0:T(8,128)(2,1)}, bf16[272,2048]{1,0:T(8,128)(2,1)}, u32[]{:S(2)}, u32[]{:S(2)}) collective-permute-start(bf16[272,2048]{1,0:T(8,128)(2,1)} %get-tuple-element.84), channel_id=1, source_target_pairs={{0,8},{4,12},{8,0},{12,4},{16,24},{20,28},{24,16},{28,20},{1,9},{5... | collective-permute-start | bytes 3342344 | tf_op jit(solution)/shard_map/ppermute | solution.py:30
  127.6 80.2 %collective-permute-start.5 = (bf16[272,2048]{1,0:T(8,128)(2,1)}, bf16[272,2048]{1,0:T(8,128)(2,1)}, u32[]{:S(2)}, u32[]{:S(2)}) collective-permute-start(bf16[272,2048]{1,0:T(8,128)(2,1)} %get-tuple-element.84), channel_id=1, source_target_pairs={{0,16},{4,20},{8,24},{12,28},{16,0},{20,4},{24,8},{28,12},{1,17},{... | collective-permute-start | bytes 3342344 | tf_op jit(solution)/shard_map/ppermute | solution.py:30
  132.3 75.1 %collective-permute-start.13 = (bf16[256,1536]{1,0:T(8,128)(2,1)}, bf16[256,1536]{1,0:T(8,128)(2,1)}, u32[]{:S(2)}, u32[]{:S(2)}) collective-permute-start(bf16[256,1536]{1,0:T(8,128)(2,1)} %pad_maximum_fusion.18), channel_id=1, source_target_pairs={{0,3},{1,0},{2,1},{3,2},{4,7},{5,4},{6,5},{7,6},{8,11},{9,8},{10,9... | collective-permute-start | bytes 2359304 | tf_op jit(solution)/shard_map/ppermute | solution.py:57
  136.0 82.2 %collective-permute-start.30 = (bf16[4,64,2048]{2,1,0:T(8,128)(2,1)S(1)}, bf16[4,64,2048]{2,1,0:T(8,128)(2,1)}, u32[]{:S(2)}, u32[]{:S(2)}) collective-permute-start(bf16[4,64,2048]{2,1,0:T(8,128)(2,1)S(1)} %bitcast_dynamic-update-slice_fusion.13), channel_id=1, source_target_pairs={{0,8},{4,12},{8,0},{12,4},{16,24},{20,28},{24,16},{28,20},{1,9},{5... | collective-permute-start | bytes 3145736 | tf_op jit(solution)/shard_map/ppermute | solution.py:30
  218.2 159.6 %collective-permute-start.49 = (bf16[128,2048]{1,0:T(8,128)(2,1)S(1)}, bf16[128,2048]{1,0:T(8,128)(2,1)S(1)}, u32[]{:S(2)}, u32[]{:S(2)}) collective-permute-start(bf16[128,2048]{1,0:T(8,128)(2,1)S(1)} %copy-done.67), channel_id=1, source_target_pairs={{0,16},{4,20},{8,24},{12,28},{16,0},{20,4},{24,8},{28,12},{1,17},{... | collective-permute-start | bytes 1572872 | tf_op jit(solution)/shard_map/ppermute | solution.py:30
  219.7 159.1 %collective-permute-start.50 = (bf16[128,2048]{1,0:T(8,128)(2,1)}, bf16[128,2048]{1,0:T(8,128)(2,1)}, u32[]{:S(2)}, u32[]{:S(2)}) collective-permute-start(bf16[128,2048]{1,0:T(8,128)(2,1)} %slice.391), channel_id=1, source_target_pairs={{0,8},{4,12},{8,0},{12,4},{16,24},{20,28},{24,16},{28,20},{1,9},{5... | collective-permute-start | bytes 1572872 | tf_op jit(solution)/shard_map/ppermute | solution.py:30
  266.4 209.9 %collective-permute-start.34 = (bf16[4,4,64,2048]{3,2,1,0:T(8,128)(2,1)}, bf16[4,4,64,2048]{3,2,1,0:T(8,128)(2,1)}, u32[]{:S(2)}, u32[]{:S(2)}) collective-permute-start(bf16[4,4,64,2048]{3,2,1,0:T(8,128)(2,1)} %pad_maximum_fusion.3), channel_id=1, source_target_pairs={{0,4},{4,0},{8,12},{12,8},{16,20},{20,16},{24,28},{28,24},{1,5},{5... | collective-permute-start | bytes 12582920 | tf_op jit(solution)/shard_map/ppermute | solution.py:30
  493.4 125.2 %collective-permute-start.39 = (bf16[4,256,2816]{2,1,0:T(8,128)(2,1)}, bf16[4,256,2816]{2,1,0:T(8,128)(2,1)}, u32[]{:S(2)}, u32[]{:S(2)}) collective-permute-start(bf16[4,256,2816]{2,1,0:T(8,128)(2,1)} %bitcast.352), channel_id=1, source_target_pairs={{0,4},{4,0},{8,12},{12,8},{16,20},{20,16},{24,28},{28,24},{1,5},{5... | collective-permute-start | bytes 17301512 | tf_op jit(solution)/shard_map/ppermute | solution.py:30
  511.4 82.9 %collective-permute-start.43 = (bf16[4,1408,256]{2,1,0:T(8,128)(2,1)}, bf16[4,1408,256]{2,1,0:T(8,128)(2,1)}, u32[]{:S(2)}, u32[]{:S(2)}) collective-permute-start(bf16[4,1408,256]{2,1,0:T(8,128)(2,1)} %pad_maximum_fusion.5), channel_id=1, source_target_pairs={{0,4},{4,0},{8,12},{12,8},{16,20},{20,16},{24,28},{28,24},{1,5},{5... | collective-permute-start | bytes 8650760 | tf_op jit(solution)/shard_map/ppermute | solution.py:30
  685.5 59.3 %collective-permute-start.46 = (bf16[256,2048]{1,0:T(8,128)(2,1)S(1)}, bf16[256,2048]{1,0:T(8,128)(2,1)S(1)}, u32[]{:S(2)}, u32[]{:S(2)}) collective-permute-start(bf16[256,2048]{1,0:T(8,128)(2,1)S(1)} %get-tuple-element.121), channel_id=1, source_target_pairs={{0,24},{4,28},{8,16},{12,20},{16,8},{20,12},{24,0},{28,4},{1,25},{... | collective-permute-start | bytes 3145736 | tf_op jit(solution)/shard_map/ppermute | solution.py:30
  686.9 77.7 %collective-permute-start.45 = (bf16[256,2048]{1,0:T(8,128)(2,1)S(1)}, bf16[256,2048]{1,0:T(8,128)(2,1)S(1)}, u32[]{:S(2)}, u32[]{:S(2)}) collective-permute-start(bf16[256,2048]{1,0:T(8,128)(2,1)S(1)} %get-tuple-element.122), channel_id=1, source_target_pairs={{0,16},{4,20},{8,24},{12,28},{16,0},{20,4},{24,8},{28,12},{1,17},{... | collective-permute-start | bytes 3145736 | tf_op jit(solution)/shard_map/ppermute | solution.py:30
  699.9 64.8 %collective-permute-start.44 = (bf16[256,2048]{1,0:T(8,128)(2,1)S(1)}, bf16[256,2048]{1,0:T(8,128)(2,1)S(1)}, u32[]{:S(2)}, u32[]{:S(2)}) collective-permute-start(bf16[256,2048]{1,0:T(8,128)(2,1)S(1)} %get-tuple-element.120), channel_id=1, source_target_pairs={{0,8},{4,12},{8,0},{12,4},{16,24},{20,28},{24,16},{28,20},{1,9},{5... | collective-permute-start | bytes 3145736 | tf_op jit(solution)/shard_map/ppermute | solution.py:30
  722.4 121.7 %collective-permute-start.97 = (bf16[1408,1024]{1,0:T(8,128)(2,1)}, bf16[1408,1024]{1,0:T(8,128)(2,1)}, u32[]{:S(2)}, u32[]{:S(2)}) collective-permute-start(bf16[1408,1024]{1,0:T(8,128)(2,1)} %convolution_convert_fusion.5), channel_id=1, source_target_pairs={{0,4},{4,0},{8,12},{12,8},{16,20},{20,16},{24,28},{28,24},{1,5},{5... | collective-permute-start | bytes 8650760 | tf_op jit(solution)/shard_map/ppermute | solution.py:30
  790.9 141.9 %collective-permute-start.91 = (bf16[1024,2816]{1,0:T(8,128)(2,1)}, bf16[1024,2816]{1,0:T(8,128)(2,1)}, u32[]{:S(2)}, u32[]{:S(2)}) collective-permute-start(bf16[1024,2816]{1,0:T(8,128)(2,1)} %convolution_convert_fusion.1), channel_id=1, source_target_pairs={{0,4},{4,0},{8,12},{12,8},{16,20},{20,16},{24,28},{28,24},{1,5},{5... | collective-permute-start | bytes 17301512 | tf_op jit(solution)/shard_map/ppermute | solution.py:30
  858.7 145.1 %collective-permute-start.79 = (bf16[2048,1024]{1,0:T(8,128)(2,1)}, bf16[2048,1024]{1,0:T(8,128)(2,1)}, u32[]{:S(2)}, u32[]{:S(2)}) collective-permute-start(bf16[2048,1024]{1,0:T(8,128)(2,1)} %convolution_convert_fusion.3), channel_id=1, source_target_pairs={{0,4},{4,0},{8,12},{12,8},{16,20},{20,16},{24,28},{28,24},{1,5},{5... | collective-permute-start | bytes 12582920 | tf_op jit(solution)/shard_map/ppermute | solution.py:30
  901.4 405.1 %reduce-scatter.3.cloned.1.call-start = ((), (), s32[]{:S(2)}) async-start(), calls=%async_computation.3 | async-start | bytes 7208960 | tf_op jit(solution)/shard_map/reduce_scatter | solution.py:585
  997.5 69.1 %collective-permute-start.66 = (f32[121,128]{1,0:T(8,128)}, f32[121,128]{1,0:T(8,128)}, u32[]{:S(2)}, u32[]{:S(2)}) collective-permute-start(f32[121,128]{1,0:T(8,128)} %get-tuple-element.165), channel_id=1, source_target_pairs={{0,3},{1,0},{2,1},{3,2},{4,7},{5,4},{6,5},{7,6},{8,11},{9,8},{10,9... | collective-permute-start | bytes 185864 | tf_op jit(solution)/shard_map/ppermute | solution.py:57
  1003.8 64.2 %collective-permute-start.65 = (f32[121,128]{1,0:T(8,128)}, f32[121,128]{1,0:T(8,128)}, u32[]{:S(2)}, u32[]{:S(2)}) collective-permute-start(f32[121,128]{1,0:T(8,128)} %get-tuple-element.166), channel_id=1, source_target_pairs={{0,2},{1,3},{2,0},{3,1},{4,6},{5,7},{6,4},{7,5},{8,10},{9,11},{10,... | collective-permute-start | bytes 185864 | tf_op jit(solution)/shard_map/ppermute | solution.py:57
  1058.9 105.8 %collective-permute-start.73 = (bf16[256,1536]{0,1:T(8,128)(2,1)}, bf16[256,1536]{0,1:T(8,128)(2,1)}, u32[]{:S(2)}, u32[]{:S(2)}) collective-permute-start(bf16[256,1536]{0,1:T(8,128)(2,1)} %bitcast.388), channel_id=1, source_target_pairs={{0,3},{1,0},{2,1},{3,2},{4,7},{5,4},{6,5},{7,6},{8,11},{9,8},{10,9... | collective-permute-start | bytes 2359304 | tf_op jit(solution)/shard_map/ppermute | solution.py:57
  1059.6 105.8 %collective-permute-start.72 = (bf16[256,1536]{0,1:T(8,128)(2,1)}, bf16[256,1536]{0,1:T(8,128)(2,1)}, u32[]{:S(2)}, u32[]{:S(2)}) collective-permute-start(bf16[256,1536]{0,1:T(8,128)(2,1)} %bitcast.387), channel_id=1, source_target_pairs={{0,2},{1,3},{2,0},{3,1},{4,6},{5,7},{6,4},{7,5},{8,10},{9,11},{10,... | collective-permute-start | bytes 2359304 | tf_op jit(solution)/shard_map/ppermute | solution.py:57
  1066.6 98.8 %collective-permute-start.71 = (bf16[256,1536]{0,1:T(8,128)(2,1)}, bf16[256,1536]{0,1:T(8,128)(2,1)}, u32[]{:S(2)}, u32[]{:S(2)}) collective-permute-start(bf16[256,1536]{0,1:T(8,128)(2,1)} %bitcast.97), channel_id=1, source_target_pairs={{0,1},{1,2},{2,3},{3,0},{4,5},{5,6},{6,7},{7,4},{8,9},{9,10},{10,1... | collective-permute-start | bytes 2359304 | tf_op jit(solution)/shard_map/ppermute | solution.py:57
  1077.0 83.3 %collective-permute-start.84 = (bf16[512,256]{1,0:T(8,128)(2,1)}, bf16[512,256]{1,0:T(8,128)(2,1)S(1)}, u32[]{:S(2)}, u32[]{:S(2)}) collective-permute-start(bf16[512,256]{1,0:T(8,128)(2,1)} %get-tuple-element.146), channel_id=1, source_target_pairs={{0,2},{1,3},{2,0},{3,1},{4,6},{5,7},{6,4},{7,5},{8,10},{9,11},{10,... | collective-permute-start | bytes 786440 | tf_op jit(solution)/shard_map/ppermute | solution.py:57
  1240.4 108.4 %collective-permute-start.78 = (bf16[4,256,1536]{1,2,0:T(8,128)(2,1)}, bf16[4,256,1536]{1,2,0:T(8,128)(2,1)}, u32[]{:S(2)}, u32[]{:S(2)}) collective-permute-start(bf16[4,256,1536]{1,2,0:T(8,128)(2,1)} %pad_maximum_fusion.4), channel_id=1, source_target_pairs={{0,4},{4,0},{8,12},{12,8},{16,20},{20,16},{24,28},{28,24},{1,5},{5... | collective-permute-start | bytes 9437192 | tf_op jit(solution)/shard_map/ppermute | solution.py:30
  1245.0 59.6 %collective-permute-start.101 = (bf16[1408,256]{0,1:T(8,128)(2,1)}, bf16[1408,256]{0,1:T(8,128)(2,1)S(1)}, u32[]{:S(2)}, u32[]{:S(2)}) collective-permute-start(bf16[1408,256]{0,1:T(8,128)(2,1)} %bitcast.375), channel_id=1, source_target_pairs={{0,8},{4,12},{8,0},{12,4},{16,24},{20,28},{24,16},{28,20},{1,9},{5... | collective-permute-start | bytes 2162696 | tf_op jit(solution)/shard_map/ppermute | solution.py:30
  1322.9 89.2 %collective-permute-start.105 = (bf16[4,1408,256]{1,2,0:T(8,128)(2,1)}, bf16[4,1408,256]{1,2,0:T(8,128)(2,1)}, u32[]{:S(2)}, u32[]{:S(2)}) collective-permute-start(bf16[4,1408,256]{1,2,0:T(8,128)(2,1)} %pad_maximum_fusion.6), channel_id=1, source_target_pairs={{0,4},{4,0},{8,12},{12,8},{16,20},{20,16},{24,28},{28,24},{1,5},{5... | collective-permute-start | bytes 8650760 | tf_op jit(solution)/shard_map/ppermute | solution.py:30
  1368.1 81.6 %collective-permute-start.96 = (bf16[4,256,2816]{1,2,0:T(8,128)(2,1)}, bf16[4,256,2816]{1,2,0:T(8,128)(2,1)}, u32[]{:S(2)}, u32[]{:S(2)}) collective-permute-start(bf16[4,256,2816]{1,2,0:T(8,128)(2,1)} %pad_maximum_fusion.2), channel_id=1, source_target_pairs={{0,4},{4,0},{8,12},{12,8},{16,20},{20,16},{24,28},{28,24},{1,5},{5... | collective-permute-start | bytes 17301512 | tf_op jit(solution)/shard_map/ppermute | solution.py:30
  (185 other events, 3677.4 us)
Sparse Core Ops, SparseCore 0:
  9.6 79.8 all-gather.3
  91.1 168.3 all-gather.5
  901.5 57.6 reduce-scatter.4
  961.9 110.0 reduce-scatter.2

commit v2 on v1

v2 whole, which is shorter than its diff:
```python
import functools

import jax
import jax.numpy as jnp
from jax import lax
from jax.experimental import pallas as pl
from jax.experimental.pallas import tpu as pltpu
from jax.sharding import PartitionSpec as P

D = 2048
HEADS = 16
HD = 128
FF = 5632
CONV = 4
EPS = 1e-06
RIM = 16
TP = 4
HT = HEADS // TP
DT = D // TP
FT = FF // TP
SCALE = HD**-0.5
VMEM = 56 * 1024 * 1024

BF = jnp.bfloat16
F32 = jnp.float32


def swap(x, bits):
    n = lax.axis_size("replica")
    return lax.ppermute(x, "replica", [(i, i ^ bits) for i in range(n)])


def plane_swap(x, j):
    return swap(x, 2 * j)


def core_swap(x):
    return swap(x, 1)


def far_sum(x):
    x = x.astype(F32)
    bits = 8
    while bits < lax.axis_size("replica"):
        x = x + swap(x.astype(BF), bits).astype(F32)
        bits *= 2
    return x


def z_shift(x, by):
    n = lax.axis_size("group")
    return lax.ppermute(x, "group", [(i, i + by) for i in range(n) if 0 <= i + by < n])


def z_turn(x, by):
    n = lax.axis_size("group")
    return lax.ppermute(x, "group", [(i, (i + by) % n) for i in range(n)])


def plane_copies(x):
    a, b = plane_swap(x, 1), plane_swap(x, 2)
    h = split_at(x.shape[0])
    return [x, a, b, plane_swap(a[:h], 2), plane_swap(b[h:], 1)]


def plane_parts(parts):
    own, x, y, d = parts
    h = split_at(own.shape[0])
    via_x, via_y = plane_swap(d[:h], 1), plane_swap(d[h:], 2)
    y = jnp.concatenate([(y[:h].astype(F32) + via_x.astype(F32)).astype(BF), y[h:]], axis=0)
    x = jnp.concatenate([x[:h], (x[h:].astype(F32) + via_y.astype(F32)).astype(BF)], axis=0)
    return [own, plane_swap(x, 1), plane_swap(y, 2)]


def plane_sum(parts):
    own, x, y = plane_parts([p.astype(BF) for p in parts])
    return parts[0].astype(F32) + x.astype(F32) + y.astype(F32)


def after(x, *others):
    return lax.optimization_barrier((x, *others))[0]


def plane_trade(parts):
    return [parts[0]] + [plane_swap(parts[j], j) for j in (1, 2, 3)]


def place(pieces, count, axis=0):
    shape = list(pieces[0][1].shape)
    shape.insert(axis, count)
    buf = jnp.zeros(shape, pieces[0][1].dtype)
    for index, piece in pieces:
        buf = lax.dynamic_update_index_in_dim(buf, piece, index, axis)
    return buf


def pick(x, index, axis=0):
    return lax.dynamic_index_in_dim(x, index, axis, keepdims=False)


def dot(a, b, dims=((1,), (0,))):
    return lax.dot_general(a, b, (dims, ((), ())), preferred_element_type=F32)


NT = ((1,), (1,))
TN = ((0,), (0,))


def iotas(rows, cols):
    return (
        lax.broadcasted_iota(jnp.int32, (rows, cols), 0),
        lax.broadcasted_iota(jnp.int32, (rows, cols), 1),
    )


def unit_lower_inverses(mats):
    n = mats[0].shape[0]
    base, tile = 16, 128
    ri, ci = iotas(n, n)
    lane = lax.broadcasted_iota(jnp.int32, (base, tile), 1) % base
    rows = lax.broadcasted_iota(jnp.int32, (base, tile), 0)
    picks = [lane == j for j in range(base)]
    rt, ct = iotas(tile, tile)
    same = (rt // base) == (ct // base)
    ones = same.astype(BF)
    zero = jnp.zeros((), BF)
    lows = [a.astype(BF) for a in mats]
    spans = [slice(at, at + tile) for at in range(0, n, tile)]
    blocks = [(m, span) for m in range(len(mats)) for span in spans]
    wides = []
    for m, span in blocks:
        part = jnp.where(same, mats[m][span, span], 0.0)
        compact = jnp.sum(part.reshape(tile // base, base, tile), axis=0).astype(BF)
        spread = jnp.concatenate([jnp.where(p, compact, zero) for p in picks], axis=0)
        wides.append(dot(spread, ones))
    xs = [(lane == rows).astype(F32)] * len(blocks)
    for j in range(base - 1):
        xs = [x - w[j * base : (j + 1) * base] * x[j : j + 1] for x, w in zip(xs, wides)]
    fulls = [jnp.where(same, jnp.concatenate([x] * (tile // base), axis=0), 0.0) for x in xs]
    size = base
    while size < tile:
        part = (
            ((rt // (2 * size)) == (ct // (2 * size)))
            & ((rt // size) % 2 == 1)
            & ((ct // size) % 2 == 0)
        )
        halves = [full.astype(BF) for full in fulls]
        inner = [
            dot(jnp.where(part, lows[m][span, span], zero), h).astype(BF)
            for (m, span), h in zip(blocks, halves)
        ]
        fulls = [full - dot(h, i) for full, h, i in zip(fulls, halves, inner)]
        size *= 2
    fulls = [full.astype(BF) for full in fulls]
    if n == tile:
        return fulls
    inner = [dot(low[tile:, :tile], fulls[2 * m]).astype(BF) for m, low in enumerate(lows)]
    corners = [-dot(fulls[2 * m + 1], i) for m, i in enumerate(inner)]
    blank = jnp.zeros((tile, tile), BF)
    return [
        jnp.concatenate(
            [
                jnp.concatenate([fulls[2 * m], blank], axis=1),
                jnp.concatenate([corner.astype(BF), fulls[2 * m + 1]], axis=1),
            ],
            axis=0,
        )
        for m, corner in enumerate(corners)
    ]


def tap_masks(doc, length):
    pos = lax.broadcasted_iota(jnp.int32, (length, 1), 0)
    return [
        jnp.broadcast_to((pos - (CONV - 1) + i >= doc).astype(F32), (length, HD)) for i in range(CONV - 1)
    ]


def conv_rows(ext, taps, kept, length):
    total = ext[RIM : RIM + length] * taps[CONV - 1 : CONV]
    for i in range(CONV - 1):
        first = RIM - (CONV - 1) + i
        total = total + ext[first : first + length] * taps[i : i + 1] * kept[i]
    return total


def masks(doc, length):
    ri, ci = iotas(length, length)
    same = (doc <= ci) & (ri >= ci)
    return same.astype(F32), (same & (ri > ci)).astype(F32)


def ends(doc, length):
    last = doc[length - 1 : length]
    pos = lax.broadcasted_iota(jnp.int32, (length, 1), 0)
    return (pos >= last).astype(F32), (last < 0).astype(F32), (doc < 0).astype(F32)


def row_starts(n):
    return (0, n, 2 * n, 3 * n, 3 * n + split_at(n))


def row_copies(srcs, dst, sem):
    starts = row_starts(srcs[0].shape[0])
    return [
        pltpu.make_async_copy(src, dst.at[pl.ds(starts[i], src.shape[0])], sem.at[i])
        for i, src in enumerate(srcs)
    ]


def front_kernel(groups, *refs):
    idx_ref, xs, ws = refs[0], refs[1:6], refs[6 : 6 + 2 * groups]
    (
        beta_ref, taps_ref, doc_ref, qo, ko, vo, t_ref, u0_ref, wo_ref, m_ref, b_ref, p_ref, rate_ref,
        all_ref, w_ref, x_sem, w_sem,
    ) = refs[6 + 2 * groups :]
    length = doc_ref.shape[1]
    half = ws[0].shape[0]
    step = pl.program_id(0)

    @pl.when(step == 0)
    def _():
        copies = row_copies(xs, all_ref, x_sem)
        for cc in range(2):
            for s in range(groups):
                at = (cc * groups + (idx_ref[2] + groups - s) % groups) * half
                copies.append(
                    pltpu.make_async_copy(
                        ws[cc * groups + s],
                        w_ref.at[pl.ds(pl.multiple_of(at, 128), half)],
                        w_sem.at[cc * groups + s],
                    )
                )
        for copy in copies:
            copy.start()
        for copy in copies:
            copy.wait()

    rows = length + RIM
    here = pl.ds(pl.multiple_of(step * rows, 16), rows)
    doc = doc_ref[0]
    same, strict = masks(doc, length)
    tail, keep, carried = ends(doc, length)
    eye = (iotas(HD, HD)[0] == iotas(HD, HD)[1]).astype(F32)

    @pl.loop(0, 3 * DT // 256)
    def _(i):
        cols = pl.ds(pl.multiple_of(i * 256, 256), 256)
        p_ref[0, :, cols] = dot(all_ref[here], w_ref[:, cols]).astype(BF)

    own = pl.ds(pl.multiple_of(step * rows + RIM, 16), length)
    rates = jax.nn.sigmoid(dot(all_ref[own], beta_ref[...]))
    rate_ref[0] = rates
    kept = tap_masks(doc, length)
    wide = (length, HD)
    tail, carried = jnp.broadcast_to(tail, wide), jnp.broadcast_to(carried, wide)
    head_rates = [jnp.broadcast_to(rates[:, h : h + 1], wide) for h in range(HT)]
    lanes = [slice(h * HD, (h + 1) * HD) for h in range(HT)]
    mats = []
    for h in range(HT):
        acts = []
        for part in range(3):
            cols = slice(part * DT + h * HD, part * DT + (h + 1) * HD)
            mixed = conv_rows(p_ref[0, :, cols].astype(F32), taps_ref[part, :, lanes[h]], kept, length)
            acts.append(mixed * jax.nn.sigmoid(mixed))
        qa, ka, va = acts
        q = (qa * (lax.rsqrt(jnp.sum(qa * qa, axis=-1, keepdims=True) + EPS) * SCALE)).astype(BF)
        k = (ka * lax.rsqrt(jnp.sum(ka * ka, axis=-1, keepdims=True) + EPS)).astype(BF)
        qo[0, :, lanes[h]] = q
        ko[0, :, lanes[h]] = k
        vo[0, :, lanes[h]] = va.astype(BF)
        mats.append(dot(k, k, NT) * (strict * rates[:, h : h + 1]))
    invs = unit_lower_inverses(mats)
    for h in range(HT):
        inv, rate = invs[h], head_rates[h]
        kf = ko[0, :, lanes[h]].astype(F32)
        u0 = dot(inv, (vo[0, :, lanes[h]].astype(F32) * rate).astype(BF))
        w = dot(inv, (kf * (rate * carried)).astype(BF)).astype(BF)
        kl = (kf * tail).astype(BF)
        m_ref[0, h] = (eye * keep - dot(kl, w, TN)).astype(BF)
        b_ref[0, h] = dot(kl, u0.astype(BF), TN)
        t_ref[0, h] = inv
        u0_ref[0, :, lanes[h]] = u0
        wo_ref[0, :, lanes[h]] = w


def out_kernel(gain_ref, q_ref, k_ref, u0_ref, w_ref, s_ref, doc_ref, n_ref, o_ref, u_ref):
    length = doc_ref.shape[1]
    doc = doc_ref[0]
    same, _ = masks(doc, length)
    carried = (doc < 0).astype(F32)
    gain = gain_ref[...]
    for h in range(HT):
        lanes = slice(h * HD, (h + 1) * HD)
        q, k, state = q_ref[0, :, lanes], k_ref[0, :, lanes], s_ref[0, h]
        u = (u0_ref[0, :, lanes] - dot(w_ref[0, :, lanes], state)).astype(BF)
        scores = (dot(q, k, NT) * same).astype(BF)
        o = dot(scores, u) + dot(q, state) * carried
        r = lax.rsqrt(jnp.mean(o * o, axis=-1, keepdims=True) + EPS)
        n_ref[0, :, lanes] = (o * r * gain).astype(BF)
        o_ref[0, :, lanes] = o
        u_ref[0, :, lanes] = u


def back_kernel(
    gain_ref, dn_ref, o_ref, q_ref, k_ref, t_ref, rate_ref, doc_ref, g_ref, y_ref, z_ref, l_ref, hg_ref
):
    length = doc_ref.shape[1]
    doc = doc_ref[0]
    same, _ = masks(doc, length)
    tail, _, carried = ends(doc, length)
    gain = gain_ref[...]

    @pl.when(pl.program_id(0) == 0)
    def _():
        hg_ref[...] = jnp.zeros_like(hg_ref)

    total = jnp.zeros((1, HD), F32)
    for h in range(HT):
        lanes = slice(h * HD, (h + 1) * HD)
        o, dy = o_ref[0, :, lanes], dn_ref[0, :, lanes].astype(F32)
        r = lax.rsqrt(jnp.mean(o * o, axis=-1, keepdims=True) + EPS)
        total = total + jnp.sum(o * r * dy, axis=0, keepdims=True)
        gy = gain * dy
        gf = r * gy - o * (r * r * r * jnp.mean(o * gy, axis=-1, keepdims=True))
        g = gf.astype(BF)
        q, k = q_ref[0, :, lanes], k_ref[0, :, lanes]
        inv = t_ref[0, h]
        scores = (dot(q, k, NT) * same).astype(BF)
        kf = k.astype(F32)
        y = dot(inv, dot(scores, g, TN).astype(BF), TN)
        z_ref[0, :, lanes] = dot(inv, (kf * tail).astype(BF), TN).astype(BF)
        rate = rate_ref[0, :, h : h + 1]
        l_ref[0, h] = dot((q.astype(F32) * carried).astype(BF), g, TN) - dot(
            (kf * (rate * carried)).astype(BF), y.astype(BF), TN
        )
        g_ref[0, :, lanes] = g
        y_ref[0, :, lanes] = y
    hg_ref[0:1] += total


def unit_back(act, dy, scale):
    r = lax.rsqrt(jnp.sum(act * act, axis=-1, keepdims=True) + EPS)
    inner = jnp.sum(act * dy, axis=-1, keepdims=True)
    return (r * scale) * dy - act * (r * r * r * scale * inner)


def grad_kernel(
    taps_ref, w_ref, beta_ref, p_ref, doc_ref, rate_ref, q_ref, k_ref, v_ref, s_ref, u_ref, g_ref, y_ref,
    z_ref, a_ref, gp_ref, gl_ref, in_ref, cg_ref,
):
    length = doc_ref.shape[1]
    doc = doc_ref[0]
    same, strict = masks(doc, length)
    tail, _, carried = ends(doc, length)

    @pl.when(pl.program_id(0) == 0)
    def _():
        cg_ref[...] = jnp.zeros_like(cg_ref)

    logits = []
    kept = tap_masks(doc, length)
    tail, carried = jnp.broadcast_to(tail, (length, HD)), jnp.broadcast_to(carried, (length, HD))
    for h in range(HT):
        lanes = slice(h * HD, (h + 1) * HD)
        q, k, v = q_ref[0, :, lanes], k_ref[0, :, lanes], v_ref[0, :, lanes]
        state, u, g, adj = s_ref[0, h], u_ref[0, :, lanes], g_ref[0, :, lanes], a_ref[0, h]
        rate = rate_ref[0, :, h : h + 1]
        yf = y_ref[0, :, lanes] + dot(z_ref[0, :, lanes], adj)
        y = yf.astype(BF)
        dv = rate * yf
        d1 = dot(y, u, NT) * strict
        gram = dot(k, k, NT)
        e = v.astype(F32) - dot(k, state) * carried
        drate = jnp.sum(yf * e, axis=-1, keepdims=True) - jnp.sum(d1 * gram, axis=-1, keepdims=True)
        dgram = (d1 * (-rate)).astype(BF)
        dscore = (dot(g, u, NT) * same).astype(BF)
        dq = dot(dscore, k) + dot(g, state, NT) * carried
        dk = dot(dscore, q, TN) + dot(dgram, k) + dot(dgram, k, TN)
        dk = dk - dot(y, state, NT) * (rate * carried) + dot(u, adj, NT) * tail
        logits.append(drate * rate * (1.0 - rate))
        for part, grad in enumerate((dq, dk, dv)):
            cols = slice(part * DT + h * HD, part * DT + (h + 1) * HD)
            ext = p_ref[0, :, cols].astype(F32)
            taps = taps_ref[part, :, lanes]
            mixed = conv_rows(ext, taps, kept, length)
            s = jax.nn.sigmoid(mixed)
            if part < 2:
                grad = unit_back(mixed * s, grad, SCALE if part == 0 else 1.0)
            gm = grad * (s * (1.0 + mixed * (1.0 - s)))
            total = jnp.zeros((length + RIM, HD), F32)
            for i in range(CONV):
                gv = gm * kept[i] if i < CONV - 1 else gm
                first = RIM - (CONV - 1) + i
                cg_ref[part, i : i + 1, lanes] += jnp.sum(
                    gv * ext[first : first + length], axis=0, keepdims=True
                )
                gv = gv * taps[i : i + 1]
                pads = [jnp.zeros((first, HD), F32), gv]
                if RIM - first > 0:
                    pads.append(jnp.zeros((RIM - first, HD), F32))
                total = total + jnp.concatenate(pads, axis=0)
            gp_ref[0, :, cols] = total.astype(BF)
    lane = lax.broadcasted_iota(jnp.int32, (length, HD), 1)
    wide = jnp.zeros((length, HD), F32)
    for h in range(HT):
        wide = jnp.where(lane == h, logits[h], wide)
    gl_ref[0, :RIM] = jnp.zeros((RIM, HD), BF)
    gl_ref[0, RIM:] = wide.astype(BF)

    @pl.loop(0, D // 256)
    def _(i):
        span = pl.ds(pl.multiple_of(i * 256, 256), 256)
        total = dot(gp_ref[0], w_ref[span], NT) + dot(gl_ref[0], beta_ref[span], NT)
        in_ref[0, :, span] = total.astype(BF)


def to_rel(x, c, groups):
    half = D // groups // 2
    out = []
    for cc in range(2):
        for i in range(groups):
            at = i * 2 * half
            one, two = x[:, at : at + half], x[:, at + half : at + 2 * half]
            out.append(jnp.where(c == 0, one, two) if cc == 0 else jnp.where(c == 0, two, one))
    return jnp.concatenate(out, axis=1)


def from_rel(x, c, groups):
    half = D // groups // 2
    out = []
    for i in range(groups):
        one, two = x[:, i * half : (i + 1) * half], x[:, (groups + i) * half : (groups + i + 1) * half]
        out += [jnp.where(c == 0, one, two), jnp.where(c == 0, two, one)]
    return jnp.concatenate(out, axis=1)


def norm_kernel(groups, idx_ref, rim_ref, x_ref, gain_ref, n_ref):
    c = idx_ref[0]
    for src, span in ((rim_ref, slice(0, RIM)), (x_ref, slice(RIM, RIM + x_ref.shape[0]))):
        x = src[...].astype(F32)
        r = lax.rsqrt(jnp.mean(x * x, axis=-1, keepdims=True) + EPS)
        n_ref[span] = to_rel(x * r * gain_ref[...], c, groups).astype(BF)


def mid_kernel(groups, idx_ref, n0, n1, n2, n3, w_ref, x_ref, gain_ref, mid_ref, n_ref):
    c = idx_ref[0]
    heads = (n0, n1, n2, n3)

    @pl.loop(0, D // 256)
    def _(i):
        span = pl.ds(pl.multiple_of(i * 256, 256), 256)
        total = x_ref[:, span].astype(F32)
        for j in range(TP):
            total = total + dot(heads[j][...], w_ref[j * DT : (j + 1) * DT, span])
        mid_ref[:, span] = total

    x = mid_ref[...]
    r = lax.rsqrt(jnp.mean(x * x, axis=-1, keepdims=True) + EPS)
    n_ref[...] = to_rel(x * r * gain_ref[...], c, groups).astype(BF)


def norm_back_rows(groups, c, parts, x, gain):
    dy = parts[0].astype(F32)
    for part in parts[1:]:
        dy = dy + part.astype(F32)
    dy = from_rel(dy, c, groups)
    r = lax.rsqrt(jnp.mean(x * x, axis=-1, keepdims=True) + EPS)
    gy = gain * dy
    dx = r * gy - x * (r * r * r * jnp.mean(x * gy, axis=-1, keepdims=True))
    return dx, jnp.sum(x * r * dy, axis=0, keepdims=True)


def mid_back_kernel(
    groups, idx_ref, p0, p1, p2, x_ref, cot_ref, gain_ref, w_ref, gm_ref, away_ref, mine_ref, d0, d1, d2, d3,
    gg_ref, br_ref,
):
    parts = [p[...] for p in (p0, p1, p2)]
    dx, gain_part = norm_back_rows(groups, idx_ref[0], parts, x_ref[...], gain_ref[...])
    grad = cot_ref[...].astype(F32) + dx
    gm_ref[...] = grad
    br_ref[...] = grad.astype(BF)
    gg_ref[...] = gain_part
    col = D // 8
    for j in range(TP):
        for cc, ref in ((1, away_ref), (0, mine_ref)):
            at = (jnp.bitwise_xor(idx_ref[1], j) * 2 + jnp.bitwise_xor(idx_ref[0], cc)) * col
            ref[:, j * col : (j + 1) * col] = br_ref[:, pl.ds(pl.multiple_of(at, 128), col)]
    for j, d_ref in enumerate((d0, d1, d2, d3)):

        @pl.loop(0, DT // 256)
        def _(i):
            at = pl.multiple_of(i * 256, 256)
            d_ref[:, pl.ds(at, 256)] = dot(br_ref[...], w_ref[pl.ds(j * DT + at, 256)], NT).astype(BF)


def in_back_kernel(groups, idx_ref, p0, p1, p2, x_ref, base_ref, gain_ref, out_ref, gg_ref):
    parts = [p[...] for p in (p0, p1, p2)]
    dx, gain_part = norm_back_rows(groups, idx_ref[0], parts, x_ref[...].astype(F32), gain_ref[...])
    out_ref[...] = base_ref[...] + dx
    gg_ref[...] = gain_part


def ffn_kernel(*refs):
    idx_ref, xs, cs, gus, downs = refs[0], refs[1:6], refs[6:11], refs[11:13], refs[13:21]
    hid_ref, gg_ref, part_ref, away_ref, mine_ref, x_ref, d_ref, c_ref, w_ref = refs[22:31]
    x_sem, c_sem, w_sem, d_sem = refs[31:]
    length = hid_ref.shape[1]
    c, t = idx_ref[0], idx_ref[1]
    step = pl.program_id(0)
    depth = gus[0].shape[0]
    col = downs[0].shape[1]

    def x_copies():
        return row_copies(xs, x_ref, x_sem)

    def c_copies():
        return row_copies(cs, c_ref, c_sem)

    def w_copies():
        return [
            pltpu.make_async_copy(gus[i], w_ref.at[pl.ds(i * depth, depth)], w_sem.at[i]) for i in range(2)
        ]

    def d_copies():
        out = []
        for cc in range(2):
            for j in range(TP):
                at = (jnp.bitwise_xor(t, j) * 2 + jnp.bitwise_xor(c, cc)) * col
                n = cc * TP + j
                out.append(
                    pltpu.make_async_copy(
                        downs[n], d_ref.at[:, pl.ds(pl.multiple_of(at, 128), col)], d_sem.at[n]
                    )
                )
        return out

    @pl.when(step == 0)
    def _():
        first = w_copies() + x_copies()
        for copy in first + c_copies() + d_copies():
            copy.start()
        for copy in first:
            copy.wait()

    here = pl.ds(pl.multiple_of(step * length, 16), length)

    def hidden_tile(at, width):
        cols = pl.ds(at, width)
        ups = pl.ds(pl.multiple_of(FT + at, 128), width)
        x = x_ref[here]
        gate, up = dot(x, w_ref[:, cols]), dot(x, w_ref[:, ups])
        grad = dot(c_ref[here], d_ref[cols], NT)
        sg = jax.nn.sigmoid(gate)
        act = gate * sg
        hid_ref[0, :, cols] = (act * up).astype(BF)
        gg_ref[0, :, cols] = (grad * up * (sg * (1.0 + gate * (1.0 - sg)))).astype(BF)
        gg_ref[0, :, ups] = (grad * act).astype(BF)

    @pl.when(step == 0)
    def _():
        for copy in c_copies() + d_copies():
            copy.wait()

    tiles = FT // 256

    @pl.loop(0, tiles)
    def _(i):
        hidden_tile(pl.multiple_of(i * 256, 256), 256)

    if FT % 256:
        hidden_tile(tiles * 256, FT % 256)

    @pl.loop(0, D // 256)
    def _(i):
        span = pl.ds(pl.multiple_of(i * 256, 256), 256)
        part_ref[0, :, span] = dot(gg_ref[0], w_ref[span], NT).astype(BF)

    for j in range(TP):
        for cc, ref in ((1, away_ref), (0, mine_ref)):
            at = (jnp.bitwise_xor(t, j) * 2 + jnp.bitwise_xor(c, cc)) * col
            ref[0, :, j * col : (j + 1) * col] = c_ref[here, pl.ds(pl.multiple_of(at, 128), col)]


def whole_call(kernel, idx, ins, outs, us=5, scratch=()):
    return pl.pallas_call(
        kernel,
        in_specs=[pl.BlockSpec(memory_space=pltpu.SMEM)]
        + [pl.BlockSpec(memory_space=pltpu.VMEM)] * len(ins),
        out_specs=[pl.BlockSpec(memory_space=pltpu.VMEM)] * len(outs),
        out_shape=[jax.ShapeDtypeStruct(s, d) for s, d in outs],
        scratch_shapes=list(scratch),
        compiler_params=pltpu.CompilerParams(vmem_limit_bytes=VMEM),
        cost_estimate=cost(us),
    )(idx, *ins)


def assemble(idx, pieces, plan, shape, us=5):
    count = len(plan([0, 0, 0]))

    def kernel(idx_ref, *refs):
        srcs, out, sem = refs[: len(pieces)], refs[-2], refs[-1]
        copies = [
            pltpu.make_async_copy(srcs[p].at[src], out.at[dst], sem.at[n])
            for n, (p, src, dst) in enumerate(plan(idx_ref))
        ]
        for copy in copies:
            copy.start()
        for copy in copies:
            copy.wait()

    dtype = pieces[0].dtype
    return pl.pallas_call(
        kernel,
        in_specs=[pl.BlockSpec(memory_space=pltpu.SMEM)] + [pl.BlockSpec(memory_space=pl.ANY)] * len(pieces),
        out_specs=pl.BlockSpec(memory_space=pltpu.VMEM),
        out_shape=jax.ShapeDtypeStruct(shape, dtype),
        scratch_shapes=[pltpu.SemaphoreType.DMA((count,))],
        compiler_params=pltpu.CompilerParams(vmem_limit_bytes=VMEM),
        cost_estimate=cost(us),
    )(idx, *pieces)


def split_at(rows):
    return rows // 32 * 16


def chunk_of(rows, cap):
    best = 16
    for q in range(16, cap + 1, 16):
        if rows % q == 0:
            best = q
    return best


def join_kernel(groups, idx_ref, g0, g1, g2, g3, out_ref):
    t = idx_ref[1]
    got = (g0, g1, g2, g3)
    shard, ff_shard = D // groups, FF // groups
    for i in range(groups):
        span = slice(i * shard, (i + 1) * shard)
        total = got[0][span].astype(F32)
        for x in got[1:]:
            total = total + x[span].astype(F32)
        out_ref[i, :shard] = total.astype(BF)
    per = groups // TP
    for j in range(TP):
        chip = jnp.bitwise_xor(t, j)
        for i in range(per):
            out_ref[chip * per + i, shard:] = got[j][D + i * ff_shard : D + (i + 1) * ff_shard]


def spread_first(x):
    return [x, plane_swap(x, 1), plane_swap(x, 2)]


def spread_pieces(first):
    x, a, b = first
    h = split_at(x.shape[0])
    mine = [x, a, b, plane_swap(a[:h], 2), plane_swap(b[h:], 1)]
    return mine + [core_swap(p) for p in mine]


def spread_out(idx, first, parts, heights=None):
    pieces = first if len(first) == 10 else spread_pieces(first)
    rows, cols = pieces[0].shape
    h = split_at(rows)
    width = cols // parts if parts else cols
    outs = []
    start = 0
    for height in heights or (rows,):
        edges = [start, start + height] + ([h] if start < h < start + height else [])
        q = 16
        for n in range(16, (64 if parts else 256) + 1, 16):
            if all((e - start) % n == 0 for e in edges) and start % n == 0 and h % n == 0:
                q = n
        outs.append(spread_part(idx, pieces, parts, width, start, height, h, q))
        start += height
    return outs


def gather_eight(x):
    n = lax.axis_size("replica")
    blocks = [list(range(i, i + 8)) for i in range(0, n, 8)]
    return lax.all_gather(x, "replica", axis=0, axis_index_groups=blocks if n > 8 else None)


def spread_abs(x, parts, start, height):
    _, rows, cols = x.shape
    width = cols // parts if parts else cols
    q = 16
    for n in range(16, (64 if parts else 128) + 1, 16):
        if height % n == 0 and start % n == 0:
            q = n
    base = start // q

    def kernel(x_ref, out):
        for r in range(8):
            chip, core = r // 2, r % 2
            if parts:
                for p in range(parts):
                    at = (p * TP + chip) * width
                    out[core, :, at : at + width] = x_ref[r, :, p * width : (p + 1) * width].astype(F32)
            else:
                out[:, r * width : (r + 1) * width] = x_ref[r].astype(F32)

    if parts:
        shape, out_spec = (2, height, TP * cols), pl.BlockSpec((2, q, TP * cols), lambda i: (0, i, 0))
    else:
        shape, out_spec = (height, 8 * cols), pl.BlockSpec((q, 8 * cols), lambda i: (i, 0))
    out = pl.pallas_call(
        kernel,
        grid=(height // q,),
        in_specs=[pl.BlockSpec((8, q, cols), lambda i: (0, i + base, 0))],
        out_specs=out_spec,
        out_shape=jax.ShapeDtypeStruct(shape, F32),
        compiler_params=pltpu.CompilerParams(vmem_limit_bytes=VMEM),
        cost_estimate=cost(height * cols * 16e-6),
    )(x)
    return out.reshape(-1, out.shape[-1])


def spread_part(idx, pieces, parts, width, start, height, h, q):
    cols = pieces[0].shape[1]
    rows = pieces[0].shape[0]
    cut, base = h // q, start // q

    def kernel(idx_ref, *refs):
        srcs, out = refs[:-1], refs[-1]
        c, t = idx_ref[0], idx_ref[1]
        i = pl.program_id(0) + base
        for cc in range(2):
            core = jnp.bitwise_xor(c, cc)

            def put(j, value):
                chip = jnp.bitwise_xor(t, j)
                if parts:
                    for p in range(parts):
                        at = pl.multiple_of((p * TP + chip) * width, 128)
                        out[core, :, pl.ds(at, width)] = value[:, p * width : (p + 1) * width].astype(F32)
                else:
                    at = pl.multiple_of((chip * 2 + core) * width, 128)
                    out[:, pl.ds(at, width)] = value.astype(F32)

            for j in range(3):
                put(j, srcs[5 * cc + j][...])

            @pl.when(i < cut)
            def _():
                put(3, srcs[5 * cc + 3][...])

            @pl.when(i >= cut)
            def _():
                put(3, srcs[5 * cc + 4][...])

    most = (rows - h) // q - 1
    full = pl.BlockSpec((q, cols), lambda i: (i + base, 0))
    low = pl.BlockSpec((q, cols), lambda i: (jnp.minimum(i + base, cut - 1), 0))
    high = pl.BlockSpec((q, cols), lambda i: (jnp.clip(i + base - cut, 0, most), 0))
    if parts:
        shape, out_spec = (2, height, TP * cols), pl.BlockSpec((2, q, TP * cols), lambda i: (0, i, 0))
    else:
        shape, out_spec = (height, 8 * cols), pl.BlockSpec((q, 8 * cols), lambda i: (i, 0))
    out = pl.pallas_call(
        kernel,
        grid=(height // q,),
        in_specs=[pl.BlockSpec(memory_space=pltpu.SMEM)] + [full, full, full, low, high] * 2,
        out_specs=out_spec,
        out_shape=jax.ShapeDtypeStruct(shape, F32),
        compiler_params=pltpu.CompilerParams(vmem_limit_bytes=VMEM),
        cost_estimate=cost(0.05),
    )(idx, *pieces)
    return out.reshape(-1, out.shape[-1])


def cost(us):
    return pl.CostEstimate(flops=int(us * 1.1e9), bytes_accessed=0, transcendentals=0)


def block(shape, fixed=False):
    zeros = (0,) * len(shape)
    if fixed:
        return pl.BlockSpec(tuple(shape), lambda i: zeros, pipeline_mode=pl.Buffered(1))
    return pl.BlockSpec((1,) + tuple(shape[1:]), lambda i: (i,) + zeros[1:])


def call(kernel, ins, fixed_ins, outs, fixed_outs=(), us=10, extra=(), scratch=(), held_outs=()):
    count = ins[-1].shape[0]
    out_specs = []
    for i, (shape, _) in enumerate(outs):
        zeros = (0,) * len(shape)
        if i in held_outs:
            spec = pl.BlockSpec(shape, lambda i, z=zeros: z, pipeline_mode=pl.Buffered(1))
        elif i in fixed_outs:
            spec = pl.BlockSpec(shape, lambda i, z=zeros: z)
        else:
            spec = block(shape)
        out_specs.append(spec)
    lead = [pl.BlockSpec(memory_space=pltpu.SMEM)] + [pl.BlockSpec(memory_space=pl.ANY)] * (len(extra) - 1)
    return pl.pallas_call(
        kernel,
        grid=(count,),
        in_specs=(lead if extra else []) + [block(x.shape, i in fixed_ins) for i, x in enumerate(ins)],
        out_specs=out_specs,
        out_shape=[jax.ShapeDtypeStruct(s, d) for s, d in outs],
        scratch_shapes=list(scratch),
        compiler_params=pltpu.CompilerParams(vmem_limit_bytes=VMEM),
        cost_estimate=cost(us),
    )(*extra, *ins)


def mm(a, b, dims=((1,), (0,))):
    return lax.dot_general(a, b, (dims, ((), ())), preferred_element_type=F32)


def body(
    tokens,
    cotangent,
    doc_start,
    norm_gain,
    qkv_weight,
    conv_weight,
    beta_weight,
    head_gain,
    out_weight,
    ffn_gain,
    gate_up_weight,
    down_weight,
):
    groups = lax.axis_size("group")
    r = lax.axis_index("replica") % 8
    g = lax.axis_index("group")
    c, t = r % 2, r // 2
    idx = jnp.stack([c, t, g]).astype(jnp.int32)
    _, length, _ = tokens.shape
    seqs = TP
    ext_len = length + RIM
    shard = D // groups
    half = shard // 2
    ff_shard = FF // groups
    col = D // 8
    tokens = tokens.reshape(length, D)
    cot = cotangent.reshape(length, D)

    def z_pieces(x):
        return [x] + [z_turn(x, s) for s in range(1, groups)]

    def z_abs(x):
        pieces = z_pieces(x)
        return place([((g - s) % groups, piece) for s, piece in enumerate(pieces)], groups)

    def rel(x):
        x = x.reshape(x.shape[:-1] + (groups, 2, half))
        x = jnp.where(c == 0, x, jnp.flip(x, -2))
        return jnp.swapaxes(x, -3, -2).reshape(x.shape[:-3] + (D,))

    def unrel(x):
        x = jnp.swapaxes(x.reshape(x.shape[:-1] + (2, groups, half)), -3, -2)
        x = jnp.where(c == 0, x, jnp.flip(x, -2))
        return x.reshape(x.shape[:-3] + (D,))

    small = jnp.concatenate(
        [
            beta_weight.T,
            jnp.swapaxes(conv_weight.reshape(3, shard, CONV), 1, 2).reshape(3 * CONV, shard),
            ffn_gain.reshape(1, shard),
            norm_gain.reshape(1, shard),
            jnp.zeros((2, shard), BF),
        ],
        axis=0,
    )
    rim = z_shift(tokens[length - RIM :], 1)
    small = z_abs(small)
    gain_in = small[:, HEADS + 3 * CONV + 1].reshape(1, D).astype(F32)
    gain_mid = small[:, HEADS + 3 * CONV].reshape(1, D).astype(F32)
    beta_full = jnp.swapaxes(small[:, :HEADS], 0, 1).reshape(HEADS, D)
    beta_t = jnp.pad(rel(lax.dynamic_slice(beta_full, (t * HT, 0), (HT, D))).T, ((0, 0), (0, HD - HT)))
    conv_full = small[:, HEADS : HEADS + 3 * CONV].reshape(groups * 3, CONV, shard)
    conv_full = jnp.swapaxes(conv_full, 0, 1).reshape(CONV, 3, TP, DT)
    taps = jnp.swapaxes(pick(conv_full, t, 2), 0, 1).astype(F32)
    gain_head = head_gain.astype(F32).reshape(1, HD)
    doc_rel = doc_start.reshape(1, length) - g * length
    docs = jnp.concatenate(
        [doc_rel] + [plane_swap(doc_rel, j) for j in (1, 2, 3)], axis=0
    ).reshape(seqs, length, 1)
    cot_x, cot_y = plane_swap(cot, 1), plane_swap(cot, 2)
    qkv_weight, small, rim = lax.optimization_barrier((qkv_weight, small, rim))

    (normed_ext,) = whole_call(
        functools.partial(norm_kernel, groups), idx, [rim, tokens, gain_in], [((ext_len, D), BF)]
    )
    normed_pieces = plane_copies(normed_ext)

    piece = jnp.concatenate(
        [lax.dynamic_slice(qkv_weight, (c * half, j * D + t * DT), (half, DT)) for j in range(3)], axis=1
    )
    qkv_pieces = z_pieces(piece)
    qkv_late = qkv_pieces
    qkv_pieces = qkv_pieces + [core_swap(p) for p in qkv_pieces]

    h = split_at(length)
    cot_pieces = [cot, cot_x, cot_y, plane_swap(cot_x[:h], 2), plane_swap(cot_y[h:], 1)]

    piece = jnp.concatenate(
        [
            lax.dynamic_slice(out_weight, (0, r * col), (shard, col)),
            lax.dynamic_slice(down_weight, (0, r * col), (ff_shard, col)),
        ],
        axis=0,
    )
    both = lax.all_gather(after(piece, *qkv_late), "group", axis=0)

    normed_pieces[0] = after(normed_pieces[0], *cot_pieces[:3])

    wide = (seqs, length, DT)
    square = (seqs, HT, HD, HD)
    (
        queries, key_rows, value_rows, inverse, u0, w, move, free, projected, rates, normed_all, qkv,
    ) = call(
        functools.partial(front_kernel, groups),
        [beta_t, taps, docs],
        (0, 1),
        [
            (wide, BF),
            (wide, BF),
            (wide, BF),
            ((seqs, HT, length, length), BF),
            (wide, F32),
            (wide, BF),
            (square, BF),
            (square, F32),
            ((seqs, ext_len, 3 * DT), BF),
            ((seqs, length, HD), F32),
            ((seqs * ext_len, D), BF),
            ((D, 3 * DT), BF),
        ],
        us=40,
        extra=[idx, *normed_pieces, *qkv_pieces],
        scratch=[pltpu.SemaphoreType.DMA((5,)), pltpu.SemaphoreType.DMA((2 * groups,))],
        held_outs=(10, 11),
    )
    piece = jnp.concatenate(
        [
            lax.dynamic_slice(gate_up_weight, (c * half, j * FF + t * FT), (half, FT))
            for j in range(2)
        ],
        axis=1,
    )
    gate_up = lax.all_gather(after(piece, free), "group", axis=0, tiled=True)

    state = jnp.zeros(square, BF)
    for hop in range(groups - 1):
        leaving = jnp.einsum("shij,shjk->shik", move, state, preferred_element_type=F32) + free
        if hop == groups - 2:
            leaving = after(leaving, *downs, *outs)
        state = z_shift(leaving.astype(BF), 1)
        if hop == 0:
            both = after(both, free)
            part = both[:, shard:].reshape(TP, FT, col)
            downs = plane_trade([pick(part, t ^ j) for j in range(TP)])
            outs = both[:, :shard].reshape(D, col)
            outs = plane_copies(outs)
    outs = outs + [core_swap(p) for p in outs]
    downs = downs + [core_swap(p) for p in downs]
    normed, head_out, update = call(
        out_kernel,
        [gain_head, queries, key_rows, u0, w, state, docs],
        (0,),
        [(wide, BF), (wide, F32), (wide, BF)],
        us=6,
    )

    def plan(ref):
        moves = []
        for cc in range(2):
            for j in range(TP):
                at = ((ref[1] ^ j) * 2 + (ref[0] ^ cc)) * col
                for b in range(TP):
                    n, first = (j, b) if j < 3 else ((3, b) if b < 2 else (4, b - 2))
                    moves.append(
                        (
                            5 * cc + n,
                            pl.ds(first * DT, DT),
                            (
                                pl.ds(pl.multiple_of((ref[1] ^ b) * DT, DT), DT),
                                pl.ds(pl.multiple_of(at, 128), col),
                            ),
                        )
                    )
        return moves

    out_w = assemble(idx, outs, plan, (D, D))

    heads = plane_trade([normed[j] for j in range(TP)])
    middle, normed_mid = whole_call(
        functools.partial(mid_kernel, groups),
        idx,
        heads + [out_w, tokens, gain_mid],
        [((length, D), F32), ((length, D), BF)],
        us=10,
    )
    mid_pieces = plane_copies(normed_mid)
    gate_ups = [gate_up, core_swap(after(gate_up, mid_pieces[1], mid_pieces[2]))]

    hidden, grad_gate_up, mid_part, cot_away, cot_mine, mid_all, down = call(
        ffn_kernel,
        [docs],
        (),
        [
            ((seqs, length, FT), BF),
            ((seqs, length, 2 * FT), BF),
            ((seqs, length, D), BF),
            ((seqs, length, D // 2), BF),
            ((seqs, length, D // 2), BF),
            ((seqs * length, D), BF),
            ((FT, D), BF),
        ],
        us=45,
        extra=[idx, *mid_pieces, *cot_pieces, *gate_ups, *downs],
        scratch=[pltpu.VMEM((seqs * length, D), BF), pltpu.VMEM((D, 2 * FT), BF)]
        + [pltpu.SemaphoreType.DMA((n,)) for n in (5, 5, 2, 8)],
        held_outs=(5, 6),
    )
    hidden = hidden.reshape(-1, FT)
    grad_gate_up = grad_gate_up.reshape(-1, 2 * FT)
    def two_halves(left, right):
        away = mm(left[:, groups * half :], right, TN).astype(BF)
        mine = mm(left[:, : groups * half], right, TN)
        return (mine + core_swap(away).astype(F32)).astype(BF).reshape(groups, half, -1)

    def two_columns(left, away, mine):
        away = mm(left, away, TN).astype(BF)
        mine = mm(left, mine, TN)
        return (mine + core_swap(away).astype(F32)).astype(BF)

    def z_sum(x, *others):
        total = pick(x, g).astype(F32)
        for s in range(1, groups):
            total = total + after(z_turn(pick(x, (g + s) % groups), s), *others).astype(F32)
        return total

    parts = plane_parts([mid_part[j] for j in range(TP)])
    gate_sums = [two_halves(mid_all, grad_gate_up[:, i * FT : (i + 1) * FT]) for i in range(2)]
    down_sum = two_columns(hidden, cot_away.reshape(-1, D // 2), cot_mine.reshape(-1, D // 2))
    first_sum = far_sum(lax.psum_scatter(gate_sums[0], "group", scatter_dimension=0)).astype(BF)
    parts, second_sum, down_sum = lax.optimization_barrier((parts, gate_sums[1], down_sum))
    second_sum = far_sum(lax.psum_scatter(second_sum, "group", scatter_dimension=0)).astype(BF)
    grad_middle, branch_away, branch_mine, *dheads, ffn_gain_part = whole_call(
        functools.partial(mid_back_kernel, groups),
        idx,
        parts + [middle.reshape(length, D), cot, gain_mid, out_w],
        [((length, D), F32)]
        + [((length, D // 2), BF)] * 2
        + [((length, DT), BF)] * TP
        + [((1, D), F32)],
        us=13,
        scratch=[pltpu.VMEM((length, D), BF)],
    )
    dnormed = jnp.stack(plane_trade(dheads))

    normed_abs = jnp.swapaxes(
        place([(t ^ j, heads[j]) for j in range(TP)], TP), 0, 1
    ).reshape(length, D)
    out_sum = two_columns(normed_abs, branch_away, branch_mine)
    both = [
        jnp.concatenate([x[:, j * col : (j + 1) * col] for x in (out_sum, down_sum)], axis=0)
        for j in range(TP)
    ]
    dnormed = after(dnormed, first_sum, *both)
    both = plane_trade(both)

    grad_out, y0, z, local, head_part = call(
        back_kernel,
        [gain_head, dnormed, head_out, queries, key_rows, inverse, rates, docs],
        (0,),
        [(wide, BF), (wide, F32), (wide, BF), (square, F32), ((8, HD), F32)],
        (4,),
        us=12,
    )

    out_part = mm(hidden, down).astype(BF).reshape(TP, length, D)

    later = jnp.zeros(square, BF)
    for hop in range(groups - 1):
        leaving = jnp.einsum("shji,shjk->shik", move, later, preferred_element_type=F32) + local
        if hop == 1:
            leaving = after(leaving, out_part)
        later = z_shift(leaving.astype(BF), -1)

    (both_sum,) = whole_call(
        functools.partial(join_kernel, groups), idx, both, [((groups, shard + ff_shard, col), BF)]
    )
    later = after(later, both_sum, second_sum)
    gate_sum = jnp.concatenate([first_sum, second_sum], axis=1)
    both_sum = lax.psum_scatter(both_sum, "group", scatter_dimension=0)
    gate_pieces = spread_first(gate_sum)
    grad_proj, grad_logit, in_part, conv_part = call(
        grad_kernel,
        [
            taps, qkv, beta_t, projected, docs, rates, queries, key_rows, value_rows, state, update, grad_out,
            y0, z, later,
        ],
        (0, 1, 2),
        [
            ((seqs, ext_len, 3 * DT), BF),
            ((seqs, ext_len, HD), BF),
            ((seqs, ext_len, D), BF),
            ((3, CONV, DT), F32),
        ],
        (3,),
        us=44,
    )
    qkv_sum = two_halves(normed_all, grad_proj.reshape(-1, 3 * DT))
    gate_pieces = spread_pieces([after(p, qkv_sum) for p in gate_pieces])
    rim = z_shift(in_part[:, :RIM], -1)
    in_part = after(in_part[:, RIM:], qkv_sum)
    qkv_sum = z_sum(qkv_sum)
    ends_in = (in_part[:, length - RIM :].astype(F32) + rim.astype(F32)).astype(BF)
    in_part = jnp.concatenate([in_part[:, : length - RIM], ends_in], axis=1)
    parts = plane_parts([in_part[j] for j in range(TP)])
    parts[0] = after(parts[0], qkv_sum)
    input_grad, norm_gain_part = whole_call(
        functools.partial(in_back_kernel, groups),
        idx,
        parts + [tokens, grad_middle, gain_in],
        [((length, D), F32), ((1, D), F32)],
        us=0.05,
    )
    output = (middle + plane_sum([out_part[j] for j in range(TP)])).astype(BF)

    beta_part = mm(grad_logit.reshape(-1, HD), normed_all, TN)[:HT]
    beta_all = lax.dynamic_update_slice(jnp.zeros((HEADS, D), F32), unrel(beta_part), (t * HT, 0))
    conv_all = lax.dynamic_update_slice(
        jnp.zeros((CONV, 3, TP, DT), F32), jnp.swapaxes(conv_part, 0, 1)[:, :, None], (0, 0, t, 0)
    )
    conv_all = jnp.swapaxes(conv_all.reshape(CONV, groups * 3, shard), 0, 1)
    pack = jnp.concatenate(
        [
            jnp.swapaxes(beta_all.reshape(HEADS, groups, shard), 0, 1),
            conv_all.reshape(groups, 3 * CONV, shard),
            norm_gain_part.reshape(groups, 1, shard),
            ffn_gain_part.reshape(groups, 1, shard),
            jnp.broadcast_to(jnp.pad(head_part[:1], ((0, 0), (0, shard - HD))), (groups, 1, shard)),
            jnp.zeros((groups, 1, shard), F32),
        ],
        axis=1,
    )
    pack = pack + core_swap(pack)
    pack = pack + plane_swap(pack, 1)
    pack = pack + plane_swap(pack, 2)

    (gate_up_grad,) = spread_out(idx, gate_pieces, 2)

    total = far_sum(z_sum(after(pack, qkv_sum)))
    both_pieces = [after(p, qkv_sum) for p in spread_first(far_sum(both_sum).astype(BF))]
    qkv_pieces = [after(p, gate_up_grad, output) for p in spread_first(far_sum(qkv_sum).astype(BF))]
    qkv_pieces = spread_pieces(qkv_pieces)
    out_grad, down_grad = spread_out(idx, both_pieces, 0, (shard, ff_shard))
    qkv_pieces[0] = after(qkv_pieces[0], total, out_grad, down_grad)
    (qkv_grad,) = spread_out(idx, qkv_pieces, 3)
    beta_grad = total[:HEADS].T
    conv_grad = jnp.swapaxes(total[HEADS : HEADS + 3 * CONV].reshape(3, CONV, shard), 1, 2)
    at = HEADS + 3 * CONV
    return (
        output.reshape(1, length, D),
        input_grad.reshape(1, length, D),
        total[at],
        qkv_grad,
        conv_grad.reshape(-1, CONV),
        beta_grad,
        total[at + 2, :HD],
        out_grad,
        total[at + 1],
        gate_up_grad,
        down_grad,
    )


def solution(mesh):
    rows = P("replica", "group", None)
    shard = P("group", None)
    return jax.shard_map(
        body,
        mesh=mesh,
        in_specs=(
            rows, rows, P("replica", "group"), P("group"), shard, shard, shard, P(), shard, P("group"), shard, shard,
        ),
        out_specs=(
            rows, rows, P("group"), shard, shard, shard, P(), shard, P("group"), shard, shard,
        ),
        check_vma=False,
    )
```

time: 1550 us -> 1020 us (0.66)
  local copies, waits for them, and re-layouts: 585 us -> 63.5 us
  Pallas kernels: 107 us -> 242 us
  matrix products: 157 us -> 74.8 us
  waiting for transfers between devices: 371 us -> 450 us
  starting transfers between devices: 200 us -> 122 us
  other arithmetic: 98.3 us -> 36.1 us
    dynamic_update_slice x67 -> x8, local copies, waits for them, and re-layouts: 161 us -> 0.13 us  [place(): buf = lax.dynamic_update_index_in_dim(buf, piece, index, axis)]
    pallas_call x4 -> x15, Pallas kernels: 107 us -> 242 us  [the longest x5 156 us: call(): pl.pallas_call(kernel, grid=(count,), in_specs=(lead if extra else []) +...]
    ppermute x8, waiting for transfers between devices: 29.9 us -> 126 us  [z_shift(): lax.ppermute(x, 'group', [(i, i + by) for i in range(n) if 0 <= i + by < n])]
    convert_element_type x5 -> x0, local copies, waits for them, and re-layouts: 85.9 us -> none  [the longest x2 54.6 us: body(): gate_sum.transpose(1, 2, 3, 0, 4).reshape(shard, 2 * FF).astype(F32)]
    dot_general x19 -> x12, matrix products: 149 us -> 68.1 us  [mm(): return lax.dot_general(a, b, (dims, ((), ())), preferred_element_type=F32)]
    unnamed x249 -> x159, local copies, waits for them, and re-layouts: 83.3 us -> 11.8 us
    ppermute x21 -> x12, starting transfers between devices: 66.1 us -> 11.6 us  [z_turn(): return lax.ppermute(x, 'group', [(i, (i + by) % n) for i in range(n)])]
    concatenate x24 -> x2, local copies, waits for them, and re-layouts: 48.1 us -> 0.75 us  [the longest x1 0.75 us: body(): jnp.concatenate([beta_weight.T, jnp.swapaxes(conv_weight.reshape(3, shard...]
  transfers between devices with their start and end apart: 110 -> 117, of which waited for: 35 -> 50; matrix products, arithmetic and copies ran while one was open for 45% -> 15% of each run, Pallas kernels for 7% -> 13%
where the time goes in v2:
time: 1020 us; the launch traced here: 1000 us
  waiting for transfers between devices  450 us (44%)
  Pallas kernels  242 us (24%)
  starting transfers between devices  122 us (12%)
  matrix products  74.8 us (7%)
  local copies, waits for them, and re-layouts  63.5 us (6%)
  other arithmetic  36.1 us (4%)
  between operations  15.9 us (2%)
    ppermute x92, waiting for transfers between devices, swap(): return lax.ppermute(x, 'replica', [(i, i ^ bits) for i in range(n)])  197 us
    pallas_call x5, Pallas kernels, call(): pl.pallas_call(kernel, grid=(count,), in_specs=(lead if extra else []) +...  156 us
    ppermute x8, waiting for transfers between devices, z_shift(): lax.ppermute(x, 'group', [(i, i + by) for i in range(n) if 0 <= i + by < n])  126 us
    ppermute x12, waiting for transfers between devices, z_turn(): return lax.ppermute(x, 'group', [(i, (i + by) % n) for i in range(n)])  121 us
    ppermute x92, starting transfers between devices, swap(): return lax.ppermute(x, 'replica', [(i, i ^ bits) for i in range(n)])  68.1 us
    dot_general x12, matrix products, mm(): return lax.dot_general(a, b, (dims, ((), ())), preferred_element_type=F32)  68.1 us
    ppermute x8, starting transfers between devices, z_shift(): lax.ppermute(x, 'group', [(i, i + by) for i in range(n) if 0 <= i + by < n])  42.2 us
    pallas_call x4, Pallas kernels, spread_part(): pl.pallas_call(kernel, grid=(height // q,), in_specs=[pl.BlockSpec(memory...  40.3 us
  transfers between devices with their start and end apart: 117, of which 50 were waited for; matrix products, arithmetic and copies ran while one was open for 15% of the time, Pallas kernels for 13%

profile of v2, /device:TPU:0, one launch (start us, length us, event | category | flops | bytes accessed | tf_op | source)
XLA Modules:
  0.0 1004.0 jit_solution(1845794703730404250)
XLA Ops:
  35.0 13.5 %collective-permute-done.10.refs_7_ = bf16[256,1536]{1,0:T(8,128)(2,1)} collective-permute-done((bf16[256,1536]{1,0:T(8,128)(2,1)}, bf16[256,1536]{1,0:T(8,128)(2,1)}, u32[]{:S(2)}, u32[]{:S(2)}) %collective-permute-start.10) | collective-permute-done | bytes 786464 | tf_op jit(solution)/shard_map/ppermute | solution.py:57
  51.1 28.5 %collective-permute-done.11.refs_8_ = bf16[256,1536]{1,0:T(8,128)(2,1)S(1)} collective-permute-done((bf16[256,1536]{1,0:T(8,128)(2,1)}, bf16[256,1536]{1,0:T(8,128)(2,1)S(1)}, u32[]{:S(2)}, u32[]{:S(2)}) %collective-permute-start.11) | collective-permute-done | bytes 786464 | tf_op jit(solution)/shard_map/ppermute | solution.py:57
  86.3 18.6 %collective-permute-done.18 = s32[1,256]{1,0:T(1,128)S(1)} collective-permute-done((s32[1,256]{1,0:T(1,128)S(1)}, s32[1,256]{1,0:T(1,128)S(1)}, u32[]{:S(2)}, u32[]{:S(2)}) %collective-permute-start.18) | collective-permute-done | bytes 1056 | tf_op jit(solution)/shard_map/ppermute | solution.py:30
  119.8 10.1 %collective-permute-done.8.refs_4_ = bf16[128,2048]{1,0:T(8,128)(2,1)} collective-permute-done((bf16[128,2048]{1,0:T(8,128)(2,1)S(1)}, bf16[128,2048]{1,0:T(8,128)(2,1)}, u32[]{:S(2)}, u32[]{:S(2)}) %collective-permute-start.8) | collective-permute-done | bytes 524320 | tf_op jit(solution)/shard_map/ppermute | solution.py:30
  129.9 37.6 %shard_map.204 = (bf16[4,256,512]{2,1,0:T(8,128)(2,1)}, bf16[4,256,512]{2,1,0:T(8,128)(2,1)}, bf16[4,256,512]{2,1,0:T(8,128)(2,1)}, bf16[4,4,256,256]{3,2,1,0:T(...) custom-call(s32[3]{0:T(128)} %pad_add_fusion.idx_ref.refs_0_, ...), custom_call_target="tpu_custom_call" | custom-call | flops 44000002048 | tf_op jit(solution)/shard_map/pallas_call | solution.py:800
  170.1 15.6 %collective-permute-start.20 = (bf16[4,4,128,128]{3,2,1,0:T(8,128)(2,1)}, bf16[4,4,128,128]{3,2,1,0:T(8,128)(2,1)S(1)}, u32[]{:S(2)}, u32[]{:S(2)}) collective-permute-start(bf16[4,4,128,128]{3,2,1,0:T(8,128)(2,1)} %fusion.13), channel_id=1, source_target_pairs={{0,1},{1,2},{2,3},{4,5},{5,6},{6,7},{8,9},{9,10},{10,11},{12,13},{... | collective-permute-start | bytes 1572872 | tf_op jit(solution)/shard_map/ppermute | solution.py:52
  189.3 17.4 %collective-permute-done.20 = bf16[4,4,128,128]{3,2,1,0:T(8,128)(2,1)S(1)} collective-permute-done((bf16[4,4,128,128]{3,2,1,0:T(8,128)(2,1)}, bf16[4,4,128,128]{3,2,1,0:T(8,128)(2,1)S(1)}, u32[]{:S(2)}, u32[]{:S(2)}) %collective-permute-start.20) | collective-permute-done | bytes 524320 | tf_op jit(solution)/shard_map/ppermute | solution.py:52
  225.7 9.7 collective-permute-done.21
  237.8 9.2 collective-permute-done.23.refs_15_
  253.5 10.4 %collective-permute-start.29 = (bf16[4,4,128,128]{3,2,1,0:T(8,128)(2,1)S(1)}, bf16[4,4,128,128]{3,2,1,0:T(8,128)(2,1)S(1)}, u32[]{:S(2)}, u32[]{:S(2)}) collective-permute-start(bf16[4,4,128,128]{3,2,1,0:T(8,128)(2,1)S(1)} %convolution_add_fusion.3), channel_id=1, source_target_pairs={{0,1},{1,2},{2,3},{4,5},{5,6},{6,7},{8,9},{9,10},{10,11},{12,13},{... | collective-permute-start | bytes 1572872 | tf_op jit(solution)/shard_map/ppermute | solution.py:52
  266.1 16.9 %collective-permute-done.29.s_ref = bf16[4,4,128,128]{3,2,1,0:T(8,128)(2,1)S(1)} collective-permute-done((bf16[4,4,128,128]{3,2,1,0:T(8,128)(2,1)S(1)}, bf16[4,4,128,128]{3,2,1,0:T(8,128)(2,1)S(1)}, u32[]{:S(2)}, u32[]{:S(2)}) %collective-permute-start.29) | collective-permute-done | bytes 524320 | tf_op jit(solution)/shard_map/ppermute | solution.py:52
  307.8 9.6 shard_map.207
  319.8 21.7 %collective-permute-done.38.refs_2_ = bf16[256,2048]{1,0:T(8,128)(2,1)S(1)} collective-permute-done((bf16[256,2048]{1,0:T(8,128)(2,1)}, bf16[256,2048]{1,0:T(8,128)(2,1)S(1)}, u32[]{:S(2)}, u32[]{:S(2)}) %collective-permute-start.38) | collective-permute-done | bytes 1048608 | tf_op jit(solution)/shard_map/ppermute | solution.py:30
  346.7 11.3 %collective-permute-done.42.refs_9_ = bf16[128,2048]{1,0:T(8,128)(2,1)S(1)} collective-permute-done((bf16[128,2048]{1,0:T(8,128)(2,1)S(1)}, bf16[128,2048]{1,0:T(8,128)(2,1)S(1)}, u32[]{:S(2)}, u32[]{:S(2)}) %collective-permute-start.42) | collective-permute-done | bytes 524320 | tf_op jit(solution)/shard_map/ppermute | solution.py:30
  367.5 10.3 %collective-permute-done.40.refs_4_ = bf16[128,2048]{1,0:T(8,128)(2,1)S(1)} collective-permute-done((bf16[128,2048]{1,0:T(8,128)(2,1)}, bf16[128,2048]{1,0:T(8,128)(2,1)S(1)}, u32[]{:S(2)}, u32[]{:S(2)}) %collective-permute-start.40) | collective-permute-done | bytes 524320 | tf_op jit(solution)/shard_map/ppermute | solution.py:30
  379.0 58.4 %shard_map.208 = (bf16[4,256,1408]{2,1,0:T(8,128)(2,1)}, bf16[4,256,2816]{2,1,0:T(8,128)(2,1)}, bf16[4,256,2048]{2,1,0:T(8,128)(2,1)}, bf16[4,256,1024]{2,1,0:T(...) custom-call(s32[3]{0:T(128)} %pad_add_fusion.idx_ref.refs_0_, ...), custom_call_target="tpu_custom_call" | custom-call | flops 49500000256 | tf_op jit(solution)/shard_map/pallas_call | solution.py:800
  487.4 13.3 %shard_map.209 = (f32[256,2048]{1,0:T(8,128)}, bf16[256,1024]{1,0:T(8,128)(2,1)}, bf16[256,1024]{1,0:T(8,128)(2,1)}, bf16[256,512]{1,0:T(8,128)(2,1)}, bf16[256,...) custom-call(s32[3]{0:T(128)} %pad_add_fusion.idx_ref.refs_0_, ...), custom_call_target="tpu_custom_call" | custom-call | flops 14300000256 | tf_op jit(solution)/shard_map/pallas_call | solution.py:586
  541.5 12.4 %shard_map.210 = (bf16[4,256,512]{2,1,0:T(8,128)(2,1)}, f32[4,256,512]{2,1,0:T(8,128)}, bf16[4,256,512]{2,1,0:T(8,128)(2,1)}, f32[4,4,128,128]{3,2,1,0:T(8,128)}, f32[8,128]{1,0:T(8,128)}) custom-call(f32[1,128]{1,0:T(1,128)} %bitcast_convert_fusion.1.gain_ref, bf16[4,256,512]{2,1,0:T(8,128)(2,1)} %pad_maximum_fusion.10.dn_ref, ...), custom_call_target="tpu_custom_call" | custom-call | flops 13200000000 | tf_op jit(solution)/shard_map/pallas_call | solution.py:800
  556.9 49.5 %collective-permute-done.64 = bf16[4,4,128,128]{3,2,1,0:T(8,128)(2,1)S(1)} collective-permute-done((bf16[4,4,128,128]{3,2,1,0:T(8,128)(2,1)S(1)}, bf16[4,4,128,128]{3,2,1,0:T(8,128)(2,1)S(1)}, u32[]{:S(2)}, u32[]{:S(2)}) %collective-permute-start.64) | collective-permute-done | bytes 524320 | tf_op jit(solution)/shard_map/ppermute | solution.py:52
  609.3 14.1 %collective-permute-done.65 = bf16[4,4,128,128]{3,2,1,0:T(8,128)(2,1)S(1)} collective-permute-done((bf16[4,4,128,128]{3,2,1,0:T(8,128)(2,1)S(1)}, bf16[4,4,128,128]{3,2,1,0:T(8,128)(2,1)S(1)}, u32[]{:S(2)}, u32[]{:S(2)}) %collective-permute-start.65) | collective-permute-done | bytes 524320 | tf_op jit(solution)/shard_map/ppermute | solution.py:52
  639.8 41.1 %shard_map.212 = (bf16[4,272,1536]{2,1,0:T(8,128)(2,1)}, bf16[4,272,128]{2,1,0:T(8,128)(2,1)}, bf16[4,272,2048]{2,1,0:T(8,128)(2,1)}, f32[3,4,512]{2,1,0:T(4,128)}) custom-call(f32[3,4,512]{2,1,0:T(4,128)} %convert_bitcast_fusion.refs_15_.taps_ref, bf16[2048,1536]{1,0:T(8,128)(2,1)} %get-tuple-element.101.w_ref, bf16[2048,128]{1,0:T(8,128)(2,1)} %pad.10.refs_14_.beta_ref, ...), custom_call_target="tpu_custom_call" | custom-call | flops 48399998976 | tf_op jit(solution)/shard_map/pallas_call | solution.py:800
  688.8 8.7 convolution_convert_fusion.1
  700.7 13.5 %collective-permute-done.49 = bf16[128,2048]{1,0:T(8,128)(2,1)S(1)} collective-permute-done((bf16[128,2048]{1,0:T(8,128)(2,1)S(1)}, bf16[128,2048]{1,0:T(8,128)(2,1)S(1)}, u32[]{:S(2)}, u32[]{:S(2)}) %collective-permute-start.49) | collective-permute-done | bytes 524320 | tf_op jit(solution)/shard_map/ppermute | solution.py:30
  743.5 9.9 collective-permute-done.71
  756.5 9.6 collective-permute-done.77
  766.2 17.9 %collective-permute-done.75 = bf16[128,2048]{1,0:T(8,128)(2,1)S(1)} collective-permute-done((bf16[128,2048]{1,0:T(8,128)(2,1)S(1)}, bf16[128,2048]{1,0:T(8,128)(2,1)S(1)}, u32[]{:S(2)}, u32[]{:S(2)}) %collective-permute-start.75) | collective-permute-done | bytes 524320 | tf_op jit(solution)/shard_map/ppermute | solution.py:30
  789.1 19.3 %collective-permute-done.74 = bf16[256,1536]{1,0:T(8,128)(2,1)} collective-permute-done((bf16[256,1536]{1,0:T(8,128)(2,1)S(1)}, bf16[256,1536]{1,0:T(8,128)(2,1)}, u32[]{:S(2)}, u32[]{:S(2)}) %collective-permute-start.74) | collective-permute-done | bytes 786464 | tf_op jit(solution)/shard_map/ppermute | solution.py:57
  809.2 37.8 %collective-permute-done.73 = bf16[256,1536]{1,0:T(8,128)(2,1)S(1)} collective-permute-done((bf16[256,1536]{1,0:T(8,128)(2,1)}, bf16[256,1536]{1,0:T(8,128)(2,1)S(1)}, u32[]{:S(2)}, u32[]{:S(2)}) %collective-permute-start.73) | collective-permute-done | bytes 786464 | tf_op jit(solution)/shard_map/ppermute | solution.py:57
  853.7 14.3 %collective-permute-done.72 = bf16[256,1536]{1,0:T(8,128)(2,1)} collective-permute-done((bf16[256,1536]{1,0:T(8,128)(2,1)}, bf16[256,1536]{1,0:T(8,128)(2,1)}, u32[]{:S(2)}, u32[]{:S(2)}) %collective-permute-start.72) | collective-permute-done | bytes 786464 | tf_op jit(solution)/shard_map/ppermute | solution.py:57
  906.5 12.1 %shard_map.214 = f32[2,256,11264]{2,1,0:T(8,128)} custom-call(s32[3]{0:T(128)} %pad_add_fusion.idx_ref.refs_0_, bf16[256,2816]{1,0:T(8,128)(2,1)} %copy-done.10, bf16[256,2816]{1,0:T(8,128)(2,1)} %collective-permute-done.85.refs_1_, bf16[256,2816]{1,0:T(8,128)(2,1)} %collective-permute-done.86.refs_2_, bf16[128,2816]{1,0:T(8,128)(2,1)} %collective-permute-done.87.refs_3_, ...), custom_call_target="tpu_custom_call" | custom-call | flops 55000000 | tf_op jit(solution)/shard_map/pallas_call | solution.py:764
  918.6 17.6 %collective-permute-done.103.refs_1_ = bf16[256,1536]{1,0:T(8,128)(2,1)} collective-permute-done((bf16[256,1536]{1,0:T(8,128)(2,1)}, bf16[256,1536]{1,0:T(8,128)(2,1)}, u32[]{:S(2)}, u32[]{:S(2)}) %collective-permute-start.103) | collective-permute-done | bytes 786464 | tf_op jit(solution)/shard_map/ppermute | solution.py:30
  973.5 14.2 %shard_map.216 = f32[1408,2048]{1,0:T(8,128)} custom-call(s32[3]{0:T(128)} %pad_add_fusion.idx_ref.refs_0_, bf16[1920,256]{1,0:T(8,128)(2,1)} %bitcast.213, bf16[1920,256]{1,0:T(8,128)(2,1)} %copy-done.8, bf16[1920,256]{1,0:T(8,128)(2,1)} %copy-done.9, bf16[960,256]{1,0:T(8,128)(2,1)} %copy-done.19, bf16[960,256]{1,0:T(8,128)(2,1)} %copy-done.20, ...), custom_call_target="tpu_custom_call" | custom-call | flops 55000000 | tf_op jit(solution)/shard_map/pallas_call | solution.py:764
  (525 shorter events, 384.0 us)
Async XLA Ops:
  7.2 178.5 %all-gather.6.cloned.1.call-start = ((), (), s32[]{:S(2)}) async-start(), calls=%async_computation.7 | async-start | bytes 4915200 | tf_op jit(solution)/shard_map/all_gather | solution.py:911
  20.6 93.2 %collective-permute-start.4 = (bf16[256,2048]{1,0:T(8,128)(2,1)}, bf16[256,2048]{1,0:T(8,128)(2,1)}, u32[]{:S(2)}, u32[]{:S(2)}) collective-permute-start(bf16[256,2048]{1,0:T(8,128)(2,1)} %bitcast.14.refs_6_.cot_ref), channel_id=1, source_target_pairs={{0,8},{4,12},{8,0},{12,4},{16,24},{20,28},{24,16},{28,20},{1,9},{5... | collective-permute-start | bytes 3145736 | tf_op jit(solution)/shard_map/ppermute | solution.py:30
  27.6 52.0 %collective-permute-start.11 = (bf16[256,1536]{1,0:T(8,128)(2,1)}, bf16[256,1536]{1,0:T(8,128)(2,1)S(1)}, u32[]{:S(2)}, u32[]{:S(2)}) collective-permute-start(bf16[256,1536]{1,0:T(8,128)(2,1)} %pad_maximum_fusion.14.refs_6_), channel_id=1, source_target_pairs={{0,2},{1,3},{2,0},{3,1},{4,6},{5,7},{6,4},{7,5},{8,10},{9,11},{10,... | collective-permute-start | bytes 2359304 | tf_op jit(solution)/shard_map/ppermute | solution.py:57
  27.9 53.2 %collective-permute-start.12 = (bf16[256,1536]{1,0:T(8,128)(2,1)}, bf16[256,1536]{1,0:T(8,128)(2,1)}, u32[]{:S(2)}, u32[]{:S(2)}) collective-permute-start(bf16[256,1536]{1,0:T(8,128)(2,1)} %pad_maximum_fusion.14.refs_6_), channel_id=1, source_target_pairs={{0,3},{1,0},{2,1},{3,2},{4,7},{5,4},{6,5},{7,6},{8,11},{9,8},{10,9... | collective-permute-start | bytes 2359304 | tf_op jit(solution)/shard_map/ppermute | solution.py:57
  33.6 80.8 %collective-permute-start.6 = (bf16[272,2048]{1,0:T(8,128)(2,1)}, bf16[272,2048]{1,0:T(8,128)(2,1)}, u32[]{:S(2)}, u32[]{:S(2)}) collective-permute-start(bf16[272,2048]{1,0:T(8,128)(2,1)} %shard_map.203.refs_1_), channel_id=1, source_target_pairs={{0,8},{4,12},{8,0},{12,4},{16,24},{20,28},{24,16},{28,20},{1,9},{5... | collective-permute-start | bytes 3342344 | tf_op jit(solution)/shard_map/ppermute | solution.py:30
  48.5 63.6 %collective-permute-start.7 = (bf16[272,2048]{1,0:T(8,128)(2,1)}, bf16[272,2048]{1,0:T(8,128)(2,1)}, u32[]{:S(2)}, u32[]{:S(2)}) collective-permute-start(bf16[272,2048]{1,0:T(8,128)(2,1)} %shard_map.203.refs_1_), channel_id=1, source_target_pairs={{0,16},{4,20},{8,24},{12,28},{16,0},{20,4},{24,8},{28,12},{1,17},{... | collective-permute-start | bytes 3342344 | tf_op jit(solution)/shard_map/ppermute | solution.py:30
  79.6 36.5 %collective-permute-start.5 = (bf16[256,2048]{1,0:T(8,128)(2,1)}, bf16[256,2048]{1,0:T(8,128)(2,1)}, u32[]{:S(2)}, u32[]{:S(2)}) collective-permute-start(bf16[256,2048]{1,0:T(8,128)(2,1)} %bitcast.14.refs_6_.cot_ref), channel_id=1, source_target_pairs={{0,16},{4,20},{8,24},{12,28},{16,0},{20,4},{24,8},{28,12},{1,17},{... | collective-permute-start | bytes 3145736 | tf_op jit(solution)/shard_map/ppermute | solution.py:30
  81.1 260.8 %all-gather.4.cloned.1.call-start = ((), (), s32[]{:S(2)}) async-start(), calls=%async_computation.3 | async-start | bytes 7208960 | tf_op jit(solution)/shard_map/all_gather | solution.py:949
  167.5 374.0 %reduce-scatter.4.cloned.1.call-start = ((), (), s32[]{:S(2)}) async-start(), calls=%async_computation.4 | async-start | bytes 3604480 | tf_op jit(solution)/shard_map/reduce_scatter | solution.py:1045
  170.1 36.6 %collective-permute-start.20 = (bf16[4,4,128,128]{3,2,1,0:T(8,128)(2,1)}, bf16[4,4,128,128]{3,2,1,0:T(8,128)(2,1)S(1)}, u32[]{:S(2)}, u32[]{:S(2)}) collective-permute-start(bf16[4,4,128,128]{3,2,1,0:T(8,128)(2,1)} %fusion.13), channel_id=1, source_target_pairs={{0,1},{1,2},{2,3},{4,5},{5,6},{6,7},{8,9},{9,10},{10,11},{12,13},{... | collective-permute-start | bytes 1572872 | tf_op jit(solution)/shard_map/ppermute | solution.py:52
  187.7 35.4 %collective-permute-start.26 = (bf16[2048,256]{1,0:T(8,128)(2,1)S(1)}, bf16[2048,256]{1,0:T(8,128)(2,1)}, u32[]{:S(2)}, u32[]{:S(2)}) collective-permute-start(bf16[2048,256]{1,0:T(8,128)(2,1)S(1)} %bitcast.224), channel_id=1, source_target_pairs={{0,16},{4,20},{8,24},{12,28},{16,0},{20,4},{24,8},{28,12},{1,17},{... | collective-permute-start | bytes 3145736 | tf_op jit(solution)/shard_map/ppermute | solution.py:30
  342.5 36.4 %collective-permute-start.44 = (bf16[1024,2816]{1,0:T(8,128)(2,1)}, bf16[1024,2816]{1,0:T(8,128)(2,1)}, u32[]{:S(2)}, u32[]{:S(2)}) collective-permute-start(bf16[1024,2816]{1,0:T(8,128)(2,1)} %all-gather.4.cloned.1.call-done.refs_11_), channel_id=1, source_target_pairs={{0,4},{4,0},{8,12},{12,8},{16,20},{20,16},{24,28},{28,24},{1,5},{5... | collective-permute-start | bytes 17301512 | tf_op jit(solution)/shard_map/ppermute | solution.py:30
  467.3 163.7 %reduce-scatter.6.cloned.1.call-start = ((), (), s32[]{:S(2)}) async-start(), calls=%async_computation.5 | async-start | bytes 3604480 | tf_op jit(solution)/shard_map/reduce_scatter | solution.py:1047
  510.0 381.3 %reduce-scatter.8.cloned.1.call-start = ((), (), s32[]{:S(2)}) async-start(), calls=%async_computation.6 | async-start | bytes 4915200 | tf_op jit(solution)/shard_map/reduce_scatter | solution.py:1095
  528.3 96.9 %collective-permute-start.67 = (bf16[3456,256]{1,0:T(8,128)(2,1)}, bf16[3456,256]{1,0:T(8,128)(2,1)}, u32[]{:S(2)}, u32[]{:S(2)}) collective-permute-start(bf16[3456,256]{1,0:T(8,128)(2,1)} %pad_maximum_fusion.1), channel_id=1, source_target_pairs={{0,8},{4,12},{8,0},{12,4},{16,24},{20,28},{24,16},{28,20},{1,9},{5... | collective-permute-start | bytes 5308424 | tf_op jit(solution)/shard_map/ppermute | solution.py:30
  530.9 94.3 %collective-permute-start.68 = (bf16[3456,256]{1,0:T(8,128)(2,1)}, bf16[3456,256]{1,0:T(8,128)(2,1)}, u32[]{:S(2)}, u32[]{:S(2)}) collective-permute-start(bf16[3456,256]{1,0:T(8,128)(2,1)} %pad_maximum_fusion.2), channel_id=1, source_target_pairs={{0,16},{4,20},{8,24},{12,28},{16,0},{20,4},{24,8},{28,12},{1,17},{... | collective-permute-start | bytes 5308424 | tf_op jit(solution)/shard_map/ppermute | solution.py:30
  532.8 92.4 %collective-permute-start.69 = (bf16[3456,256]{1,0:T(8,128)(2,1)}, bf16[3456,256]{1,0:T(8,128)(2,1)}, u32[]{:S(2)}, u32[]{:S(2)}) collective-permute-start(bf16[3456,256]{1,0:T(8,128)(2,1)} %pad_maximum_fusion.3), channel_id=1, source_target_pairs={{0,24},{4,28},{8,16},{12,20},{16,8},{20,12},{24,0},{28,4},{1,25},{... | collective-permute-start | bytes 5308424 | tf_op jit(solution)/shard_map/ppermute | solution.py:30
  555.6 50.8 %collective-permute-start.64 = (bf16[4,4,128,128]{3,2,1,0:T(8,128)(2,1)S(1)}, bf16[4,4,128,128]{3,2,1,0:T(8,128)(2,1)S(1)}, u32[]{:S(2)}, u32[]{:S(2)}) collective-permute-start(bf16[4,4,128,128]{3,2,1,0:T(8,128)(2,1)S(1)} %fusion.15), channel_id=1, source_target_pairs={{1,0},{2,1},{3,2},{5,4},{6,5},{7,6},{9,8},{10,9},{11,10},{13,12},{... | collective-permute-start | bytes 1572872 | tf_op jit(solution)/shard_map/ppermute | solution.py:52
  688.8 44.3 %collective-permute-start.70 = (bf16[1024,1536]{1,0:T(8,128)(2,1)}, bf16[1024,1536]{1,0:T(8,128)(2,1)}, u32[]{:S(2)}, u32[]{:S(2)}) collective-permute-start(bf16[1024,1536]{1,0:T(8,128)(2,1)} %convolution_convert_fusion.4), channel_id=1, source_target_pairs={{0,4},{4,0},{8,12},{12,8},{16,20},{20,16},{24,28},{28,24},{1,5},{5... | collective-permute-start | bytes 9437192 | tf_op jit(solution)/shard_map/ppermute | solution.py:30
  717.3 150.8 %collective-permute-start.52 = (bf16[256,2048]{1,0:T(8,128)(2,1)}, bf16[256,2048]{1,0:T(8,128)(2,1)}, u32[]{:S(2)}, u32[]{:S(2)}) collective-permute-start(bf16[256,2048]{1,0:T(8,128)(2,1)} %pad_maximum_fusion.7), channel_id=1, source_target_pairs={{0,16},{4,20},{8,24},{12,28},{16,0},{20,4},{24,8},{28,12},{1,17},{... | collective-permute-start | bytes 3145736 | tf_op jit(solution)/shard_map/ppermute | solution.py:30
  722.1 64.9 %collective-permute-start.85 = (bf16[256,2816]{1,0:T(8,128)(2,1)S(1)}, bf16[256,2816]{1,0:T(8,128)(2,1)}, u32[]{:S(2)}, u32[]{:S(2)}) collective-permute-start(bf16[256,2816]{1,0:T(8,128)(2,1)S(1)} %pad_maximum_fusion.5.refs_0_), channel_id=1, source_target_pairs={{0,8},{4,12},{8,0},{12,4},{16,24},{20,28},{24,16},{28,20},{1,9},{5... | collective-permute-start | bytes 4325384 | tf_op jit(solution)/shard_map/ppermute | solution.py:30
  723.0 64.7 %collective-permute-start.86 = (bf16[256,2816]{1,0:T(8,128)(2,1)S(1)}, bf16[256,2816]{1,0:T(8,128)(2,1)}, u32[]{:S(2)}, u32[]{:S(2)}) collective-permute-start(bf16[256,2816]{1,0:T(8,128)(2,1)S(1)} %pad_maximum_fusion.5.refs_0_), channel_id=1, source_target_pairs={{0,16},{4,20},{8,24},{12,28},{16,0},{20,4},{24,8},{28,12},{1,17},{... | collective-permute-start | bytes 4325384 | tf_op jit(solution)/shard_map/ppermute | solution.py:30
  766.1 42.3 %collective-permute-start.74 = (bf16[256,1536]{1,0:T(8,128)(2,1)S(1)}, bf16[256,1536]{1,0:T(8,128)(2,1)}, u32[]{:S(2)}, u32[]{:S(2)}) collective-permute-start(bf16[256,1536]{1,0:T(8,128)(2,1)S(1)} %get-tuple-element.179), channel_id=1, source_target_pairs={{0,3},{1,0},{2,1},{3,2},{4,7},{5,4},{6,5},{7,6},{8,11},{9,8},{10,9... | collective-permute-start | bytes 2359304 | tf_op jit(solution)/shard_map/ppermute | solution.py:57
  784.1 62.9 %collective-permute-start.73 = (bf16[256,1536]{1,0:T(8,128)(2,1)}, bf16[256,1536]{1,0:T(8,128)(2,1)S(1)}, u32[]{:S(2)}, u32[]{:S(2)}) collective-permute-start(bf16[256,1536]{1,0:T(8,128)(2,1)} %get-tuple-element.180), channel_id=1, source_target_pairs={{0,2},{1,3},{2,0},{3,1},{4,6},{5,7},{6,4},{7,5},{8,10},{9,11},{10,... | collective-permute-start | bytes 2359304 | tf_op jit(solution)/shard_map/ppermute | solution.py:57
  787.1 81.5 %collective-permute-start.50 = (bf16[256,2048]{1,0:T(8,128)(2,1)}, bf16[256,2048]{1,0:T(8,128)(2,1)}, u32[]{:S(2)}, u32[]{:S(2)}) collective-permute-start(bf16[256,2048]{1,0:T(8,128)(2,1)} %pad_maximum_fusion.6), channel_id=1, source_target_pairs={{0,8},{4,12},{8,0},{12,4},{16,24},{20,28},{24,16},{28,20},{1,9},{5... | collective-permute-start | bytes 3145736 | tf_op jit(solution)/shard_map/ppermute | solution.py:30
  787.7 82.6 %collective-permute-start.76 = (bf16[256,2048]{1,0:T(8,128)(2,1)}, bf16[256,2048]{1,0:T(8,128)(2,1)}, u32[]{:S(2)}, u32[]{:S(2)}) collective-permute-start(bf16[256,2048]{1,0:T(8,128)(2,1)} %pad_maximum_fusion.11), channel_id=1, source_target_pairs={{0,8},{4,12},{8,0},{12,4},{16,24},{20,28},{24,16},{28,20},{1,9},{5... | collective-permute-start | bytes 3145736 | tf_op jit(solution)/shard_map/ppermute | solution.py:30
  808.4 63.5 %collective-permute-start.78 = (bf16[256,2048]{1,0:T(8,128)(2,1)}, bf16[256,2048]{1,0:T(8,128)(2,1)}, u32[]{:S(2)}, u32[]{:S(2)}) collective-permute-start(bf16[256,2048]{1,0:T(8,128)(2,1)} %pad_maximum_fusion.12), channel_id=1, source_target_pairs={{0,16},{4,20},{8,24},{12,28},{16,0},{20,4},{24,8},{28,12},{1,17},{... | collective-permute-start | bytes 3145736 | tf_op jit(solution)/shard_map/ppermute | solution.py:30
  891.3 50.4 %collective-permute-start.94 = (bf16[1920,256]{1,0:T(8,128)(2,1)}, bf16[1920,256]{1,0:T(8,128)(2,1)S(1)}, u32[]{:S(2)}, u32[]{:S(2)}) collective-permute-start(bf16[1920,256]{1,0:T(8,128)(2,1)} %bitcast.210), channel_id=1, source_target_pairs={{0,8},{4,12},{8,0},{12,4},{16,24},{20,28},{24,16},{28,20},{1,9},{5... | collective-permute-start | bytes 2949128 | tf_op jit(solution)/shard_map/ppermute | solution.py:30
  891.7 50.1 %collective-permute-start.95 = (bf16[1920,256]{1,0:T(8,128)(2,1)}, bf16[1920,256]{1,0:T(8,128)(2,1)S(1)}, u32[]{:S(2)}, u32[]{:S(2)}) collective-permute-start(bf16[1920,256]{1,0:T(8,128)(2,1)} %bitcast.211), channel_id=1, source_target_pairs={{0,16},{4,20},{8,24},{12,28},{16,0},{20,4},{24,8},{28,12},{1,17},{... | collective-permute-start | bytes 2949128 | tf_op jit(solution)/shard_map/ppermute | solution.py:30
  893.2 43.1 %collective-permute-start.103 = (bf16[256,1536]{1,0:T(8,128)(2,1)}, bf16[256,1536]{1,0:T(8,128)(2,1)}, u32[]{:S(2)}, u32[]{:S(2)}) collective-permute-start(bf16[256,1536]{1,0:T(8,128)(2,1)} %fusion.12.refs_0_), channel_id=1, source_target_pairs={{0,8},{4,12},{8,0},{12,4},{16,24},{20,28},{24,16},{28,20},{1,9},{5... | collective-permute-start | bytes 2359304 | tf_op jit(solution)/shard_map/ppermute | solution.py:30
  899.2 39.9 %collective-permute-start.104 = (bf16[256,1536]{1,0:T(8,128)(2,1)}, bf16[256,1536]{1,0:T(8,128)(2,1)}, u32[]{:S(2)}, u32[]{:S(2)}) collective-permute-start(bf16[256,1536]{1,0:T(8,128)(2,1)} %fusion.12.refs_0_), channel_id=1, source_target_pairs={{0,16},{4,20},{8,24},{12,28},{16,0},{20,4},{24,8},{28,12},{1,17},{... | collective-permute-start | bytes 2359304 | tf_op jit(solution)/shard_map/ppermute | solution.py:30
  901.7 40.7 %collective-permute-start.81 = (f32[4,32,512]{2,0,1:T(4,128)S(1)}, f32[4,32,512]{2,0,1:T(4,128)S(1)}, u32[]{:S(2)}, u32[]{:S(2)}) collective-permute-start(f32[4,32,512]{2,0,1:T(4,128)S(1)} %add.296), channel_id=1, source_target_pairs={{0,16},{4,20},{8,24},{12,28},{16,0},{20,4},{24,8},{28,12},{1,17},{... | collective-permute-start | bytes 786440 | tf_op jit(solution)/shard_map/ppermute | solution.py:30
  (160 other events, 2616.2 us)
Sparse Core Ops, SparseCore 0:
  81.3 89.3 all-gather.5
  172.8 138.7 all-gather.3
  467.4 74.0 reduce-scatter.3
  543.6 67.1 reduce-scatter.5
  721.0 102.4 reduce-scatter.7

commit v3 on v2

--- a/solution.py
+++ b/solution.py
@@ -243,9 +243,8 @@
     tail, keep, carried = ends(doc, length)
     eye = (iotas(HD, HD)[0] == iotas(HD, HD)[1]).astype(F32)
 
-    @pl.loop(0, 3 * DT // 256)
-    def _(i):
-        cols = pl.ds(pl.multiple_of(i * 256, 256), 256)
+    for i in range(3 * DT // 256):
+        cols = slice(i * 256, (i + 1) * 256)
         p_ref[0, :, cols] = dot(all_ref[here], w_ref[:, cols]).astype(BF)
 
     own = pl.ds(pl.multiple_of(step * rows + RIM, 16), length)
@@ -408,9 +407,8 @@
     gl_ref[0, :RIM] = jnp.zeros((RIM, HD), BF)
     gl_ref[0, RIM:] = wide.astype(BF)
 
-    @pl.loop(0, D // 256)
-    def _(i):
-        span = pl.ds(pl.multiple_of(i * 256, 256), 256)
+    for i in range(D // 256):
+        span = slice(i * 256, (i + 1) * 256)
         total = dot(gp_ref[0], w_ref[span], NT) + dot(gl_ref[0], beta_ref[span], NT)
         in_ref[0, :, span] = total.astype(BF)
 
@@ -447,9 +445,8 @@
     c = idx_ref[0]
     heads = (n0, n1, n2, n3)
 
-    @pl.loop(0, D // 256)
-    def _(i):
-        span = pl.ds(pl.multiple_of(i * 256, 256), 256)
+    for i in range(D // 256):
+        span = slice(i * 256, (i + 1) * 256)
         total = x_ref[:, span].astype(F32)
         for j in range(TP):
             total = total + dot(heads[j][...], w_ref[j * DT : (j + 1) * DT, span])
@@ -487,11 +484,9 @@
             at = (jnp.bitwise_xor(idx_ref[1], j) * 2 + jnp.bitwise_xor(idx_ref[0], cc)) * col
             ref[:, j * col : (j + 1) * col] = br_ref[:, pl.ds(pl.multiple_of(at, 128), col)]
     for j, d_ref in enumerate((d0, d1, d2, d3)):
-
-        @pl.loop(0, DT // 256)
-        def _(i):
-            at = pl.multiple_of(i * 256, 256)
-            d_ref[:, pl.ds(at, 256)] = dot(br_ref[...], w_ref[pl.ds(j * DT + at, 256)], NT).astype(BF)
+        for i in range(DT // 256):
+            at = i * 256
+            d_ref[:, at : at + 256] = dot(br_ref[...], w_ref[j * DT + at : j * DT + at + 256], NT).astype(BF)
 
 
 def in_back_kernel(groups, idx_ref, p0, p1, p2, x_ref, base_ref, gain_ref, out_ref, gg_ref):
@@ -547,7 +542,7 @@
 
     def hidden_tile(at, width):
         cols = pl.ds(at, width)
-        ups = pl.ds(pl.multiple_of(FT + at, 128), width)
+        ups = pl.ds(FT + at, width)
         x = x_ref[here]
         gate, up = dot(x, w_ref[:, cols]), dot(x, w_ref[:, ups])
         grad = dot(c_ref[here], d_ref[cols], NT)
@@ -564,16 +559,14 @@
 
     tiles = FT // 256
 
-    @pl.loop(0, tiles)
-    def _(i):
-        hidden_tile(pl.multiple_of(i * 256, 256), 256)
+    for i in range(tiles):
+        hidden_tile(i * 256, 256)
 
     if FT % 256:
         hidden_tile(tiles * 256, FT % 256)
 
-    @pl.loop(0, D // 256)
-    def _(i):
-        span = pl.ds(pl.multiple_of(i * 256, 256), 256)
+    for i in range(D // 256):
+        span = slice(i * 256, (i + 1) * 256)
         part_ref[0, :, span] = dot(gg_ref[0], w_ref[span], NT).astype(BF)
 
     for j in range(TP):
@@ -622,7 +615,10 @@
 
 
 def split_at(rows):
-    return rows // 32 * 16
+    unit = 16
+    while unit < 128 and rows % (2 * unit) == 0:
+        unit *= 2
+    return (rows // unit + 1) // 2 * unit if unit >= 64 and rows // unit > 8 else rows // 32 * 16
 
 
 def chunk_of(rows, cap):
@@ -638,16 +634,16 @@
     got = (g0, g1, g2, g3)
     shard, ff_shard = D // groups, FF // groups
     for i in range(groups):
-        span = slice(i * shard, (i + 1) * shard)
+        span = slice(FT + i * shard, FT + (i + 1) * shard)
         total = got[0][span].astype(F32)
         for x in got[1:]:
             total = total + x[span].astype(F32)
-        out_ref[i, :shard] = total.astype(BF)
+        out_ref[i, ff_shard:] = total.astype(BF)
     per = groups // TP
     for j in range(TP):
         chip = jnp.bitwise_xor(t, j)
         for i in range(per):
-            out_ref[chip * per + i, shard:] = got[j][D + i * ff_shard : D + (i + 1) * ff_shard]
+            out_ref[chip * per + i, :ff_shard] = got[j][i * ff_shard : (i + 1) * ff_shard]
 
 
 def spread_first(x):
@@ -1063,7 +1059,7 @@
     ).reshape(length, D)
     out_sum = two_columns(normed_abs, branch_away, branch_mine)
     both = [
-        jnp.concatenate([x[:, j * col : (j + 1) * col] for x in (out_sum, down_sum)], axis=0)
+        jnp.concatenate([x[:, j * col : (j + 1) * col] for x in (down_sum, out_sum)], axis=0)
         for j in range(TP)
     ]
     dnormed = after(dnormed, first_sum, *both)
@@ -1155,7 +1151,7 @@
     both_pieces = [after(p, qkv_sum) for p in spread_first(far_sum(both_sum).astype(BF))]
     qkv_pieces = [after(p, gate_up_grad, output) for p in spread_first(far_sum(qkv_sum).astype(BF))]
     qkv_pieces = spread_pieces(qkv_pieces)
-    out_grad, down_grad = spread_out(idx, both_pieces, 0, (shard, ff_shard))
+    down_grad, out_grad = spread_out(idx, both_pieces, 0, (ff_shard, shard))
     qkv_pieces[0] = after(qkv_pieces[0], total, out_grad, down_grad)
     (qkv_grad,) = spread_out(idx, qkv_pieces, 3)
     beta_grad = total[:HEADS].T

time: 1020 us -> 991 us (0.972)
  Pallas kernels: 242 us -> 210 us
  starting transfers between devices: 122 us -> 140 us
    pallas_call x5, Pallas kernels: 156 us -> 135 us  [call(): pl.pallas_call(kernel, grid=(count,), in_specs=(lead if extra else []) +...]
    ppermute x8, waiting for transfers between devices: 126 us -> 109 us  [z_shift(): lax.ppermute(x, 'group', [(i, i + by) for i in range(n) if 0 <= i + by < n])]
    ppermute x8, starting transfers between devices: 42.2 us -> 54.6 us  [z_shift(): lax.ppermute(x, 'group', [(i, i + by) for i in range(n) if 0 <= i + by < n])]
  transfers between devices with their start and end apart: 117 -> 117, of which waited for: 50 -> 49; matrix products, arithmetic and copies ran while one was open for 15% -> 15% of each run, Pallas kernels for 13% -> 12%
where the time goes in v3:
time: 991 us; the launch traced here: 980 us
  waiting for transfers between devices  440 us (44%)
  Pallas kernels  210 us (21%)
  starting transfers between devices  140 us (14%)
  matrix products  75.4 us (8%)
  local copies, waits for them, and re-layouts  62.4 us (6%)
  other arithmetic  36.2 us (4%)
  between operations  15.7 us (2%)
    ppermute x92, waiting for transfers between devices, swap(): return lax.ppermute(x, 'replica', [(i, i ^ bits) for i in range(n)])  204 us
    pallas_call x5, Pallas kernels, call(): pl.pallas_call(kernel, grid=(count,), in_specs=(lead if extra else []) +...  135 us
    ppermute x12, waiting for transfers between devices, z_turn(): return lax.ppermute(x, 'group', [(i, (i + by) % n) for i in range(n)])  120 us
    ppermute x8, waiting for transfers between devices, z_shift(): lax.ppermute(x, 'group', [(i, i + by) for i in range(n) if 0 <= i + by < n])  109 us
    ppermute x92, starting transfers between devices, swap(): return lax.ppermute(x, 'replica', [(i, i ^ bits) for i in range(n)])  70 us
    dot_general x12, matrix products, mm(): return lax.dot_general(a, b, (dims, ((), ())), preferred_element_type=F32)  68.6 us
    ppermute x8, starting transfers between devices, z_shift(): lax.ppermute(x, 'group', [(i, i + by) for i in range(n) if 0 <= i + by < n])  54.6 us
    pallas_call x4, Pallas kernels, spread_part(): pl.pallas_call(kernel, grid=(height // q,), in_specs=[pl.BlockSpec(memory...  34.2 us
  transfers between devices with their start and end apart: 117, of which 49 were waited for; matrix products, arithmetic and copies ran while one was open for 15% of the time, Pallas kernels for 12%

profile of v3, /device:TPU:0, one launch (start us, length us, event | category | flops | bytes accessed | tf_op | source)
XLA Modules:
  0.0 980.0 jit_solution(3532711268940233556)
XLA Ops:
  35.0 13.5 %collective-permute-done.10.refs_7_ = bf16[256,1536]{1,0:T(8,128)(2,1)} collective-permute-done((bf16[256,1536]{1,0:T(8,128)(2,1)}, bf16[256,1536]{1,0:T(8,128)(2,1)}, u32[]{:S(2)}, u32[]{:S(2)}) %collective-permute-start.10) | collective-permute-done | bytes 786464 | tf_op jit(solution)/shard_map/ppermute | solution.py:57
  51.1 28.5 %collective-permute-done.11.refs_8_ = bf16[256,1536]{1,0:T(8,128)(2,1)S(1)} collective-permute-done((bf16[256,1536]{1,0:T(8,128)(2,1)}, bf16[256,1536]{1,0:T(8,128)(2,1)S(1)}, u32[]{:S(2)}, u32[]{:S(2)}) %collective-permute-start.11) | collective-permute-done | bytes 786464 | tf_op jit(solution)/shard_map/ppermute | solution.py:57
  86.3 18.6 %collective-permute-done.18 = s32[1,256]{1,0:T(1,128)S(1)} collective-permute-done((s32[1,256]{1,0:T(1,128)S(1)}, s32[1,256]{1,0:T(1,128)S(1)}, u32[]{:S(2)}, u32[]{:S(2)}) %collective-permute-start.18) | collective-permute-done | bytes 1056 | tf_op jit(solution)/shard_map/ppermute | solution.py:30
  119.8 10.1 %collective-permute-done.8.refs_4_ = bf16[128,2048]{1,0:T(8,128)(2,1)} collective-permute-done((bf16[128,2048]{1,0:T(8,128)(2,1)S(1)}, bf16[128,2048]{1,0:T(8,128)(2,1)}, u32[]{:S(2)}, u32[]{:S(2)}) %collective-permute-start.8) | collective-permute-done | bytes 524320 | tf_op jit(solution)/shard_map/ppermute | solution.py:30
  129.9 32.4 %shard_map.204 = (bf16[4,256,512]{2,1,0:T(8,128)(2,1)}, bf16[4,256,512]{2,1,0:T(8,128)(2,1)}, bf16[4,256,512]{2,1,0:T(8,128)(2,1)}, bf16[4,4,256,256]{3,2,1,0:T(...) custom-call(s32[3]{0:T(128)} %pad_add_fusion.idx_ref.refs_0_, ...), custom_call_target="tpu_custom_call" | custom-call | flops 44000002048 | tf_op jit(solution)/shard_map/pallas_call | solution.py:796
  164.9 15.6 %collective-permute-start.20 = (bf16[4,4,128,128]{3,2,1,0:T(8,128)(2,1)}, bf16[4,4,128,128]{3,2,1,0:T(8,128)(2,1)S(1)}, u32[]{:S(2)}, u32[]{:S(2)}) collective-permute-start(bf16[4,4,128,128]{3,2,1,0:T(8,128)(2,1)} %fusion.13), channel_id=1, source_target_pairs={{0,1},{1,2},{2,3},{4,5},{5,6},{6,7},{8,9},{9,10},{10,11},{12,13},{... | collective-permute-start | bytes 1572872 | tf_op jit(solution)/shard_map/ppermute | solution.py:52
  184.1 17.4 %collective-permute-done.20 = bf16[4,4,128,128]{3,2,1,0:T(8,128)(2,1)S(1)} collective-permute-done((bf16[4,4,128,128]{3,2,1,0:T(8,128)(2,1)}, bf16[4,4,128,128]{3,2,1,0:T(8,128)(2,1)S(1)}, u32[]{:S(2)}, u32[]{:S(2)}) %collective-permute-start.20) | collective-permute-done | bytes 524320 | tf_op jit(solution)/shard_map/ppermute | solution.py:52
  201.8 8.5 collective-permute-start.21
  220.5 9.7 collective-permute-done.21
  232.5 9.2 collective-permute-done.23.refs_15_
  248.3 22.6 %collective-permute-start.29 = (bf16[4,4,128,128]{3,2,1,0:T(8,128)(2,1)S(1)}, bf16[4,4,128,128]{3,2,1,0:T(8,128)(2,1)S(1)}, u32[]{:S(2)}, u32[]{:S(2)}) collective-permute-start(bf16[4,4,128,128]{3,2,1,0:T(8,128)(2,1)S(1)} %convolution_add_fusion.3), channel_id=1, source_target_pairs={{0,1},{1,2},{2,3},{4,5},{5,6},{6,7},{8,9},{9,10},{10,11},{12,13},{... | collective-permute-start | bytes 1572872 | tf_op jit(solution)/shard_map/ppermute | solution.py:52
  312.9 21.7 %collective-permute-done.38.refs_2_ = bf16[256,2048]{1,0:T(8,128)(2,1)S(1)} collective-permute-done((bf16[256,2048]{1,0:T(8,128)(2,1)}, bf16[256,2048]{1,0:T(8,128)(2,1)S(1)}, u32[]{:S(2)}, u32[]{:S(2)}) %collective-permute-start.38) | collective-permute-done | bytes 1048608 | tf_op jit(solution)/shard_map/ppermute | solution.py:30
  339.8 11.3 %collective-permute-done.42.refs_9_ = bf16[128,2048]{1,0:T(8,128)(2,1)S(1)} collective-permute-done((bf16[128,2048]{1,0:T(8,128)(2,1)S(1)}, bf16[128,2048]{1,0:T(8,128)(2,1)S(1)}, u32[]{:S(2)}, u32[]{:S(2)}) %collective-permute-start.42) | collective-permute-done | bytes 524320 | tf_op jit(solution)/shard_map/ppermute | solution.py:30
  360.6 10.3 %collective-permute-done.40.refs_4_ = bf16[128,2048]{1,0:T(8,128)(2,1)S(1)} collective-permute-done((bf16[128,2048]{1,0:T(8,128)(2,1)}, bf16[128,2048]{1,0:T(8,128)(2,1)S(1)}, u32[]{:S(2)}, u32[]{:S(2)}) %collective-permute-start.40) | collective-permute-done | bytes 524320 | tf_op jit(solution)/shard_map/ppermute | solution.py:30
  372.1 47.2 %shard_map.208 = (bf16[4,256,1408]{2,1,0:T(8,128)(2,1)}, bf16[4,256,2816]{2,1,0:T(8,128)(2,1)}, bf16[4,256,2048]{2,1,0:T(8,128)(2,1)}, bf16[4,256,1024]{2,1,0:T(...) custom-call(s32[3]{0:T(128)} %pad_add_fusion.idx_ref.refs_0_, ...), custom_call_target="tpu_custom_call" | custom-call | flops 49500000256 | tf_op jit(solution)/shard_map/pallas_call | solution.py:796
  449.4 8.5 add_convert_fusion.3
  469.9 10.2 %shard_map.209 = (f32[256,2048]{1,0:T(8,128)}, bf16[256,1024]{1,0:T(8,128)(2,1)}, bf16[256,1024]{1,0:T(8,128)(2,1)}, bf16[256,512]{1,0:T(8,128)(2,1)}, bf16[256,...) custom-call(s32[3]{0:T(128)} %pad_add_fusion.idx_ref.refs_0_, ...), custom_call_target="tpu_custom_call" | custom-call | flops 14300000256 | tf_op jit(solution)/shard_map/pallas_call | solution.py:579
  523.5 12.4 %shard_map.210 = (bf16[4,256,512]{2,1,0:T(8,128)(2,1)}, f32[4,256,512]{2,1,0:T(8,128)}, bf16[4,256,512]{2,1,0:T(8,128)(2,1)}, f32[4,4,128,128]{3,2,1,0:T(8,128)}, f32[8,128]{1,0:T(8,128)}) custom-call(f32[1,128]{1,0:T(1,128)} %bitcast_convert_fusion.1.gain_ref, bf16[4,256,512]{2,1,0:T(8,128)(2,1)} %pad_maximum_fusion.10.dn_ref, ...), custom_call_target="tpu_custom_call" | custom-call | flops 13200000000 | tf_op jit(solution)/shard_map/pallas_call | solution.py:796
  538.9 46.2 %collective-permute-done.64 = bf16[4,4,128,128]{3,2,1,0:T(8,128)(2,1)S(1)} collective-permute-done((bf16[4,4,128,128]{3,2,1,0:T(8,128)(2,1)S(1)}, bf16[4,4,128,128]{3,2,1,0:T(8,128)(2,1)S(1)}, u32[]{:S(2)}, u32[]{:S(2)}) %collective-permute-start.64) | collective-permute-done | bytes 524320 | tf_op jit(solution)/shard_map/ppermute | solution.py:52
  588.0 14.9 %collective-permute-done.65 = bf16[4,4,128,128]{3,2,1,0:T(8,128)(2,1)S(1)} collective-permute-done((bf16[4,4,128,128]{3,2,1,0:T(8,128)(2,1)S(1)}, bf16[4,4,128,128]{3,2,1,0:T(8,128)(2,1)S(1)}, u32[]{:S(2)}, u32[]{:S(2)}) %collective-permute-start.65) | collective-permute-done | bytes 524320 | tf_op jit(solution)/shard_map/ppermute | solution.py:52
  618.0 36.4 %shard_map.212 = (bf16[4,272,1536]{2,1,0:T(8,128)(2,1)}, bf16[4,272,128]{2,1,0:T(8,128)(2,1)}, bf16[4,272,2048]{2,1,0:T(8,128)(2,1)}, f32[3,4,512]{2,1,0:T(4,128)}) custom-call(f32[3,4,512]{2,1,0:T(4,128)} %convert_bitcast_fusion.refs_15_.taps_ref, bf16[2048,1536]{1,0:T(8,128)(2,1)} %get-tuple-element.101.w_ref, bf16[2048,128]{1,0:T(8,128)(2,1)} %pad.10.refs_14_.beta_ref, ...), custom_call_target="tpu_custom_call" | custom-call | flops 48399998976 | tf_op jit(solution)/shard_map/pallas_call | solution.py:796
  662.3 9.1 convolution_convert_fusion.1
  677.7 11.1 %collective-permute-done.49 = bf16[128,2048]{1,0:T(8,128)(2,1)S(1)} collective-permute-done((bf16[128,2048]{1,0:T(8,128)(2,1)S(1)}, bf16[128,2048]{1,0:T(8,128)(2,1)S(1)}, u32[]{:S(2)}, u32[]{:S(2)}) %collective-permute-start.49) | collective-permute-done | bytes 524320 | tf_op jit(solution)/shard_map/ppermute | solution.py:30
  718.5 9.2 collective-permute-done.71
  730.0 11.1 %collective-permute-done.77 = bf16[128,2048]{1,0:T(8,128)(2,1)S(1)} collective-permute-done((bf16[128,2048]{1,0:T(8,128)(2,1)S(1)}, bf16[128,2048]{1,0:T(8,128)(2,1)S(1)}, u32[]{:S(2)}, u32[]{:S(2)}) %collective-permute-start.77) | collective-permute-done | bytes 524320 | tf_op jit(solution)/shard_map/ppermute | solution.py:30
  743.0 16.7 %collective-permute-done.75 = bf16[128,2048]{1,0:T(8,128)(2,1)S(1)} collective-permute-done((bf16[128,2048]{1,0:T(8,128)(2,1)S(1)}, bf16[128,2048]{1,0:T(8,128)(2,1)S(1)}, u32[]{:S(2)}, u32[]{:S(2)}) %collective-permute-start.75) | collective-permute-done | bytes 524320 | tf_op jit(solution)/shard_map/ppermute | solution.py:30
  766.9 18.8 %collective-permute-done.74 = bf16[256,1536]{1,0:T(8,128)(2,1)} collective-permute-done((bf16[256,1536]{1,0:T(8,128)(2,1)S(1)}, bf16[256,1536]{1,0:T(8,128)(2,1)}, u32[]{:S(2)}, u32[]{:S(2)}) %collective-permute-start.74) | collective-permute-done | bytes 786464 | tf_op jit(solution)/shard_map/ppermute | solution.py:57
  787.0 37.7 %collective-permute-done.73 = bf16[256,1536]{1,0:T(8,128)(2,1)S(1)} collective-permute-done((bf16[256,1536]{1,0:T(8,128)(2,1)}, bf16[256,1536]{1,0:T(8,128)(2,1)S(1)}, u32[]{:S(2)}, u32[]{:S(2)}) %collective-permute-start.73) | collective-permute-done | bytes 786464 | tf_op jit(solution)/shard_map/ppermute | solution.py:57
  831.6 14.7 %collective-permute-done.72 = bf16[256,1536]{1,0:T(8,128)(2,1)} collective-permute-done((bf16[256,1536]{1,0:T(8,128)(2,1)}, bf16[256,1536]{1,0:T(8,128)(2,1)}, u32[]{:S(2)}, u32[]{:S(2)}) %collective-permute-start.72) | collective-permute-done | bytes 786464 | tf_op jit(solution)/shard_map/ppermute | solution.py:57
  884.5 11.9 %shard_map.214 = f32[2,256,11264]{2,1,0:T(8,128)} custom-call(s32[3]{0:T(128)} %pad_add_fusion.idx_ref.refs_0_, bf16[256,2816]{1,0:T(8,128)(2,1)} %copy-done.10, bf16[256,2816]{1,0:T(8,128)(2,1)} %collective-permute-done.85.refs_1_, bf16[256,2816]{1,0:T(8,128)(2,1)} %collective-permute-done.86.refs_2_, bf16[128,2816]{1,0:T(8,128)(2,1)} %collective-permute-done.87.refs_3_, ...), custom_call_target="tpu_custom_call" | custom-call | flops 55000000 | tf_op jit(solution)/shard_map/pallas_call | solution.py:760
  896.4 18.1 %collective-permute-done.103.refs_1_ = bf16[256,1536]{1,0:T(8,128)(2,1)} collective-permute-done((bf16[256,1536]{1,0:T(8,128)(2,1)}, bf16[256,1536]{1,0:T(8,128)(2,1)}, u32[]{:S(2)}, u32[]{:S(2)}) %collective-permute-start.103) | collective-permute-done | bytes 786464 | tf_op jit(solution)/shard_map/ppermute | solution.py:30
  954.1 9.9 %shard_map.216 = f32[1408,2048]{1,0:T(8,128)} custom-call(s32[3]{0:T(128)} %pad_add_fusion.idx_ref.refs_0_, bf16[1920,256]{1,0:T(8,128)(2,1)} %bitcast.213, bf16[1920,256]{1,0:T(8,128)(2,1)} %copy-done.8, bf16[1920,256]{1,0:T(8,128)(2,1)} %copy-done.9, bf16[1024,256]{1,0:T(8,128)(2,1)} %collective-permute-done.96.refs_3_, bf16[896,256]{1,0:T(8,128)(2,1)} %copy-done.20, ...), custom_call_target="tpu_custom_call" | custom-call | flops 55000000 | tf_op jit(solution)/shard_map/pallas_call | solution.py:760
  (523 shorter events, 390.8 us)
Async XLA Ops:
  7.2 173.3 %all-gather.6.cloned.1.call-start = ((), (), s32[]{:S(2)}) async-start(), calls=%async_computation.7 | async-start | bytes 4915200 | tf_op jit(solution)/shard_map/all_gather | solution.py:907
  20.6 93.2 %collective-permute-start.4 = (bf16[256,2048]{1,0:T(8,128)(2,1)}, bf16[256,2048]{1,0:T(8,128)(2,1)}, u32[]{:S(2)}, u32[]{:S(2)}) collective-permute-start(bf16[256,2048]{1,0:T(8,128)(2,1)} %bitcast.14.refs_6_.cot_ref), channel_id=1, source_target_pairs={{0,8},{4,12},{8,0},{12,4},{16,24},{20,28},{24,16},{28,20},{1,9},{5... | collective-permute-start | bytes 3145736 | tf_op jit(solution)/shard_map/ppermute | solution.py:30
  27.6 52.0 %collective-permute-start.11 = (bf16[256,1536]{1,0:T(8,128)(2,1)}, bf16[256,1536]{1,0:T(8,128)(2,1)S(1)}, u32[]{:S(2)}, u32[]{:S(2)}) collective-permute-start(bf16[256,1536]{1,0:T(8,128)(2,1)} %pad_maximum_fusion.14.refs_6_), channel_id=1, source_target_pairs={{0,2},{1,3},{2,0},{3,1},{4,6},{5,7},{6,4},{7,5},{8,10},{9,11},{10,... | collective-permute-start | bytes 2359304 | tf_op jit(solution)/shard_map/ppermute | solution.py:57
  27.9 53.2 %collective-permute-start.12 = (bf16[256,1536]{1,0:T(8,128)(2,1)}, bf16[256,1536]{1,0:T(8,128)(2,1)}, u32[]{:S(2)}, u32[]{:S(2)}) collective-permute-start(bf16[256,1536]{1,0:T(8,128)(2,1)} %pad_maximum_fusion.14.refs_6_), channel_id=1, source_target_pairs={{0,3},{1,0},{2,1},{3,2},{4,7},{5,4},{6,5},{7,6},{8,11},{9,8},{10,9... | collective-permute-start | bytes 2359304 | tf_op jit(solution)/shard_map/ppermute | solution.py:57
  33.6 80.8 %collective-permute-start.6 = (bf16[272,2048]{1,0:T(8,128)(2,1)}, bf16[272,2048]{1,0:T(8,128)(2,1)}, u32[]{:S(2)}, u32[]{:S(2)}) collective-permute-start(bf16[272,2048]{1,0:T(8,128)(2,1)} %shard_map.203.refs_1_), channel_id=1, source_target_pairs={{0,8},{4,12},{8,0},{12,4},{16,24},{20,28},{24,16},{28,20},{1,9},{5... | collective-permute-start | bytes 3342344 | tf_op jit(solution)/shard_map/ppermute | solution.py:30
  48.5 63.6 %collective-permute-start.7 = (bf16[272,2048]{1,0:T(8,128)(2,1)}, bf16[272,2048]{1,0:T(8,128)(2,1)}, u32[]{:S(2)}, u32[]{:S(2)}) collective-permute-start(bf16[272,2048]{1,0:T(8,128)(2,1)} %shard_map.203.refs_1_), channel_id=1, source_target_pairs={{0,16},{4,20},{8,24},{12,28},{16,0},{20,4},{24,8},{28,12},{1,17},{... | collective-permute-start | bytes 3342344 | tf_op jit(solution)/shard_map/ppermute | solution.py:30
  79.6 36.5 %collective-permute-start.5 = (bf16[256,2048]{1,0:T(8,128)(2,1)}, bf16[256,2048]{1,0:T(8,128)(2,1)}, u32[]{:S(2)}, u32[]{:S(2)}) collective-permute-start(bf16[256,2048]{1,0:T(8,128)(2,1)} %bitcast.14.refs_6_.cot_ref), channel_id=1, source_target_pairs={{0,16},{4,20},{8,24},{12,28},{16,0},{20,4},{24,8},{28,12},{1,17},{... | collective-permute-start | bytes 3145736 | tf_op jit(solution)/shard_map/ppermute | solution.py:30
  81.1 253.9 %all-gather.4.cloned.1.call-start = ((), (), s32[]{:S(2)}) async-start(), calls=%async_computation.3 | async-start | bytes 7208960 | tf_op jit(solution)/shard_map/all_gather | solution.py:945
  162.3 361.2 %reduce-scatter.4.cloned.1.call-start = ((), (), s32[]{:S(2)}) async-start(), calls=%async_computation.4 | async-start | bytes 3604480 | tf_op jit(solution)/shard_map/reduce_scatter | solution.py:1041
  164.9 36.6 %collective-permute-start.20 = (bf16[4,4,128,128]{3,2,1,0:T(8,128)(2,1)}, bf16[4,4,128,128]{3,2,1,0:T(8,128)(2,1)S(1)}, u32[]{:S(2)}, u32[]{:S(2)}) collective-permute-start(bf16[4,4,128,128]{3,2,1,0:T(8,128)(2,1)} %fusion.13), channel_id=1, source_target_pairs={{0,1},{1,2},{2,3},{4,5},{5,6},{6,7},{8,9},{9,10},{10,11},{12,13},{... | collective-permute-start | bytes 1572872 | tf_op jit(solution)/shard_map/ppermute | solution.py:52
  182.5 35.4 %collective-permute-start.26 = (bf16[2048,256]{1,0:T(8,128)(2,1)S(1)}, bf16[2048,256]{1,0:T(8,128)(2,1)}, u32[]{:S(2)}, u32[]{:S(2)}) collective-permute-start(bf16[2048,256]{1,0:T(8,128)(2,1)S(1)} %bitcast.224), channel_id=1, source_target_pairs={{0,16},{4,20},{8,24},{12,28},{16,0},{20,4},{24,8},{28,12},{1,17},{... | collective-permute-start | bytes 3145736 | tf_op jit(solution)/shard_map/ppermute | solution.py:30
  335.7 36.4 %collective-permute-start.44 = (bf16[1024,2816]{1,0:T(8,128)(2,1)}, bf16[1024,2816]{1,0:T(8,128)(2,1)}, u32[]{:S(2)}, u32[]{:S(2)}) collective-permute-start(bf16[1024,2816]{1,0:T(8,128)(2,1)} %all-gather.4.cloned.1.call-done.refs_11_), channel_id=1, source_target_pairs={{0,4},{4,0},{8,12},{12,8},{16,20},{20,16},{24,28},{28,24},{1,5},{5... | collective-permute-start | bytes 17301512 | tf_op jit(solution)/shard_map/ppermute | solution.py:30
  449.4 161.2 %reduce-scatter.6.cloned.1.call-start = ((), (), s32[]{:S(2)}) async-start(), calls=%async_computation.5 | async-start | bytes 3604480 | tf_op jit(solution)/shard_map/reduce_scatter | solution.py:1043
  489.4 379.9 %reduce-scatter.8.cloned.1.call-start = ((), (), s32[]{:S(2)}) async-start(), calls=%async_computation.6 | async-start | bytes 4915200 | tf_op jit(solution)/shard_map/reduce_scatter | solution.py:1091
  507.9 96.9 %collective-permute-start.67 = (bf16[3456,256]{1,0:T(8,128)(2,1)}, bf16[3456,256]{1,0:T(8,128)(2,1)}, u32[]{:S(2)}, u32[]{:S(2)}) collective-permute-start(bf16[3456,256]{1,0:T(8,128)(2,1)} %pad_maximum_fusion.1), channel_id=1, source_target_pairs={{0,8},{4,12},{8,0},{12,4},{16,24},{20,28},{24,16},{28,20},{1,9},{5... | collective-permute-start | bytes 5308424 | tf_op jit(solution)/shard_map/ppermute | solution.py:30
  510.4 94.3 %collective-permute-start.68 = (bf16[3456,256]{1,0:T(8,128)(2,1)}, bf16[3456,256]{1,0:T(8,128)(2,1)}, u32[]{:S(2)}, u32[]{:S(2)}) collective-permute-start(bf16[3456,256]{1,0:T(8,128)(2,1)} %pad_maximum_fusion.2), channel_id=1, source_target_pairs={{0,16},{4,20},{8,24},{12,28},{16,0},{20,4},{24,8},{28,12},{1,17},{... | collective-permute-start | bytes 5308424 | tf_op jit(solution)/shard_map/ppermute | solution.py:30
  512.4 92.3 %collective-permute-start.69 = (bf16[3456,256]{1,0:T(8,128)(2,1)}, bf16[3456,256]{1,0:T(8,128)(2,1)}, u32[]{:S(2)}, u32[]{:S(2)}) collective-permute-start(bf16[3456,256]{1,0:T(8,128)(2,1)} %pad_maximum_fusion.3), channel_id=1, source_target_pairs={{0,24},{4,28},{8,16},{12,20},{16,8},{20,12},{24,0},{28,4},{1,25},{... | collective-permute-start | bytes 5308424 | tf_op jit(solution)/shard_map/ppermute | solution.py:30
  537.6 47.5 %collective-permute-start.64 = (bf16[4,4,128,128]{3,2,1,0:T(8,128)(2,1)S(1)}, bf16[4,4,128,128]{3,2,1,0:T(8,128)(2,1)S(1)}, u32[]{:S(2)}, u32[]{:S(2)}) collective-permute-start(bf16[4,4,128,128]{3,2,1,0:T(8,128)(2,1)S(1)} %fusion.15), channel_id=1, source_target_pairs={{1,0},{2,1},{3,2},{5,4},{6,5},{7,6},{9,8},{10,9},{11,10},{13,12},{... | collective-permute-start | bytes 1572872 | tf_op jit(solution)/shard_map/ppermute | solution.py:52
  662.2 47.5 %collective-permute-start.70 = (bf16[1024,1536]{1,0:T(8,128)(2,1)}, bf16[1024,1536]{1,0:T(8,128)(2,1)}, u32[]{:S(2)}, u32[]{:S(2)}) collective-permute-start(bf16[1024,1536]{1,0:T(8,128)(2,1)} %convolution_convert_fusion.4), channel_id=1, source_target_pairs={{0,4},{4,0},{8,12},{12,8},{16,20},{20,16},{24,28},{28,24},{1,5},{5... | collective-permute-start | bytes 9437192 | tf_op jit(solution)/shard_map/ppermute | solution.py:30
  692.9 153.5 %collective-permute-start.52 = (bf16[256,2048]{1,0:T(8,128)(2,1)}, bf16[256,2048]{1,0:T(8,128)(2,1)}, u32[]{:S(2)}, u32[]{:S(2)}) collective-permute-start(bf16[256,2048]{1,0:T(8,128)(2,1)} %pad_maximum_fusion.7), channel_id=1, source_target_pairs={{0,16},{4,20},{8,24},{12,28},{16,0},{20,4},{24,8},{28,12},{1,17},{... | collective-permute-start | bytes 3145736 | tf_op jit(solution)/shard_map/ppermute | solution.py:30
  696.8 68.0 %collective-permute-start.85 = (bf16[256,2816]{1,0:T(8,128)(2,1)S(1)}, bf16[256,2816]{1,0:T(8,128)(2,1)}, u32[]{:S(2)}, u32[]{:S(2)}) collective-permute-start(bf16[256,2816]{1,0:T(8,128)(2,1)S(1)} %pad_maximum_fusion.5.refs_0_), channel_id=1, source_target_pairs={{0,8},{4,12},{8,0},{12,4},{16,24},{20,28},{24,16},{28,20},{1,9},{5... | collective-permute-start | bytes 4325384 | tf_op jit(solution)/shard_map/ppermute | solution.py:30
  698.6 67.9 %collective-permute-start.86 = (bf16[256,2816]{1,0:T(8,128)(2,1)S(1)}, bf16[256,2816]{1,0:T(8,128)(2,1)}, u32[]{:S(2)}, u32[]{:S(2)}) collective-permute-start(bf16[256,2816]{1,0:T(8,128)(2,1)S(1)} %pad_maximum_fusion.5.refs_0_), channel_id=1, source_target_pairs={{0,16},{4,20},{8,24},{12,28},{16,0},{20,4},{24,8},{28,12},{1,17},{... | collective-permute-start | bytes 4325384 | tf_op jit(solution)/shard_map/ppermute | solution.py:30
  741.1 44.6 %collective-permute-start.74 = (bf16[256,1536]{1,0:T(8,128)(2,1)S(1)}, bf16[256,1536]{1,0:T(8,128)(2,1)}, u32[]{:S(2)}, u32[]{:S(2)}) collective-permute-start(bf16[256,1536]{1,0:T(8,128)(2,1)S(1)} %get-tuple-element.179), channel_id=1, source_target_pairs={{0,3},{1,0},{2,1},{3,2},{4,7},{5,4},{6,5},{7,6},{8,11},{9,8},{10,9... | collective-permute-start | bytes 2359304 | tf_op jit(solution)/shard_map/ppermute | solution.py:57
  759.7 65.1 %collective-permute-start.73 = (bf16[256,1536]{1,0:T(8,128)(2,1)}, bf16[256,1536]{1,0:T(8,128)(2,1)S(1)}, u32[]{:S(2)}, u32[]{:S(2)}) collective-permute-start(bf16[256,1536]{1,0:T(8,128)(2,1)} %get-tuple-element.180), channel_id=1, source_target_pairs={{0,2},{1,3},{2,0},{3,1},{4,6},{5,7},{6,4},{7,5},{8,10},{9,11},{10,... | collective-permute-start | bytes 2359304 | tf_op jit(solution)/shard_map/ppermute | solution.py:57
  764.9 82.0 %collective-permute-start.50 = (bf16[256,2048]{1,0:T(8,128)(2,1)}, bf16[256,2048]{1,0:T(8,128)(2,1)}, u32[]{:S(2)}, u32[]{:S(2)}) collective-permute-start(bf16[256,2048]{1,0:T(8,128)(2,1)} %pad_maximum_fusion.6), channel_id=1, source_target_pairs={{0,8},{4,12},{8,0},{12,4},{16,24},{20,28},{24,16},{28,20},{1,9},{5... | collective-permute-start | bytes 3145736 | tf_op jit(solution)/shard_map/ppermute | solution.py:30
  766.5 81.8 %collective-permute-start.76 = (bf16[256,2048]{1,0:T(8,128)(2,1)}, bf16[256,2048]{1,0:T(8,128)(2,1)}, u32[]{:S(2)}, u32[]{:S(2)}) collective-permute-start(bf16[256,2048]{1,0:T(8,128)(2,1)} %pad_maximum_fusion.11), channel_id=1, source_target_pairs={{0,8},{4,12},{8,0},{12,4},{16,24},{20,28},{24,16},{28,20},{1,9},{5... | collective-permute-start | bytes 3145736 | tf_op jit(solution)/shard_map/ppermute | solution.py:30
  785.7 64.1 %collective-permute-start.78 = (bf16[256,2048]{1,0:T(8,128)(2,1)}, bf16[256,2048]{1,0:T(8,128)(2,1)}, u32[]{:S(2)}, u32[]{:S(2)}) collective-permute-start(bf16[256,2048]{1,0:T(8,128)(2,1)} %pad_maximum_fusion.12), channel_id=1, source_target_pairs={{0,16},{4,20},{8,24},{12,28},{16,0},{20,4},{24,8},{28,12},{1,17},{... | collective-permute-start | bytes 3145736 | tf_op jit(solution)/shard_map/ppermute | solution.py:30
  869.3 50.4 %collective-permute-start.94 = (bf16[1920,256]{1,0:T(8,128)(2,1)}, bf16[1920,256]{1,0:T(8,128)(2,1)S(1)}, u32[]{:S(2)}, u32[]{:S(2)}) collective-permute-start(bf16[1920,256]{1,0:T(8,128)(2,1)} %bitcast.210), channel_id=1, source_target_pairs={{0,8},{4,12},{8,0},{12,4},{16,24},{20,28},{24,16},{28,20},{1,9},{5... | collective-permute-start | bytes 2949128 | tf_op jit(solution)/shard_map/ppermute | solution.py:30
  869.8 49.9 %collective-permute-start.95 = (bf16[1920,256]{1,0:T(8,128)(2,1)}, bf16[1920,256]{1,0:T(8,128)(2,1)S(1)}, u32[]{:S(2)}, u32[]{:S(2)}) collective-permute-start(bf16[1920,256]{1,0:T(8,128)(2,1)} %bitcast.211), channel_id=1, source_target_pairs={{0,16},{4,20},{8,24},{12,28},{16,0},{20,4},{24,8},{28,12},{1,17},{... | collective-permute-start | bytes 2949128 | tf_op jit(solution)/shard_map/ppermute | solution.py:30
  871.2 43.4 %collective-permute-start.103 = (bf16[256,1536]{1,0:T(8,128)(2,1)}, bf16[256,1536]{1,0:T(8,128)(2,1)}, u32[]{:S(2)}, u32[]{:S(2)}) collective-permute-start(bf16[256,1536]{1,0:T(8,128)(2,1)} %fusion.12.refs_0_), channel_id=1, source_target_pairs={{0,8},{4,12},{8,0},{12,4},{16,24},{20,28},{24,16},{28,20},{1,9},{5... | collective-permute-start | bytes 2359304 | tf_op jit(solution)/shard_map/ppermute | solution.py:30
  877.2 37.4 %collective-permute-start.104 = (bf16[256,1536]{1,0:T(8,128)(2,1)}, bf16[256,1536]{1,0:T(8,128)(2,1)}, u32[]{:S(2)}, u32[]{:S(2)}) collective-permute-start(bf16[256,1536]{1,0:T(8,128)(2,1)} %fusion.12.refs_0_), channel_id=1, source_target_pairs={{0,16},{4,20},{8,24},{12,28},{16,0},{20,4},{24,8},{28,12},{1,17},{... | collective-permute-start | bytes 2359304 | tf_op jit(solution)/shard_map/ppermute | solution.py:30
  879.7 40.6 %collective-permute-start.81 = (f32[4,32,512]{2,0,1:T(4,128)S(1)}, f32[4,32,512]{2,0,1:T(4,128)S(1)}, u32[]{:S(2)}, u32[]{:S(2)}) collective-permute-start(f32[4,32,512]{2,0,1:T(4,128)S(1)} %add.296), channel_id=1, source_target_pairs={{0,16},{4,20},{8,24},{12,28},{16,0},{20,4},{24,8},{28,12},{1,17},{... | collective-permute-start | bytes 786440 | tf_op jit(solution)/shard_map/ppermute | solution.py:30
  (159 other events, 2571.9 us)
Sparse Core Ops, SparseCore 0:
  81.3 89.3 all-gather.5
  172.8 133.5 all-gather.3
  449.5 73.9 reduce-scatter.3
  525.7 67.8 reduce-scatter.5
  695.7 106.0 reduce-scatter.7

commit v4 on v3

--- a/solution.py
+++ b/solution.py
@@ -1074,13 +1074,10 @@
         us=12,
     )
 
-    out_part = mm(hidden, down).astype(BF).reshape(TP, length, D)
 
     later = jnp.zeros(square, BF)
     for hop in range(groups - 1):
         leaving = jnp.einsum("shji,shjk->shik", move, later, preferred_element_type=F32) + local
-        if hop == 1:
-            leaving = after(leaving, out_part)
         later = z_shift(leaving.astype(BF), -1)
 
     (both_sum,) = whole_call(
@@ -1107,6 +1104,7 @@
         us=44,
     )
     qkv_sum = two_halves(normed_all, grad_proj.reshape(-1, 3 * DT))
+    qkv_mine = qkv_sum
     gate_pieces = spread_pieces([after(p, qkv_sum) for p in gate_pieces])
     rim = z_shift(in_part[:, :RIM], -1)
     in_part = after(in_part[:, RIM:], qkv_sum)
@@ -1122,6 +1120,7 @@
         [((length, D), F32), ((1, D), F32)],
         us=0.05,
     )
+    out_part = mm(after(hidden, qkv_mine), down).astype(BF).reshape(TP, length, D)
     output = (middle + plane_sum([out_part[j] for j in range(TP)])).astype(BF)
 
     beta_part = mm(grad_logit.reshape(-1, HD), normed_all, TN)[:HT]

time: 991 us -> 988 us (level)
  starting transfers between devices: 140 us -> 129 us
  waiting for transfers between devices: 440 us -> 450 us
    ppermute x8, starting transfers between devices: 54.6 us -> 43.4 us  [z_shift(): lax.ppermute(x, 'group', [(i, i + by) for i in range(n) if 0 <= i + by < n])]
  transfers between devices with their start and end apart: 117 -> 117, of which waited for: 49 -> 45; matrix products, arithmetic and copies ran while one was open for 15% -> 16% of each run, Pallas kernels for 12% -> 12%
where the time goes in v4:
time: 988 us; the launch traced here: 983 us
  waiting for transfers between devices  450 us (46%)
  Pallas kernels  210 us (21%)
  starting transfers between devices  129 us (13%)
  matrix products  84.5 us (9%)
  local copies, waits for them, and re-layouts  65.8 us (7%)
  other arithmetic  29.1 us (3%)
  between operations  15.8 us (2%)
    ppermute x92, waiting for transfers between devices, swap(): return lax.ppermute(x, 'replica', [(i, i ^ bits) for i in range(n)])  204 us
    pallas_call x5, Pallas kernels, call(): pl.pallas_call(kernel, grid=(count,), in_specs=(lead if extra else []) +...  135 us
    ppermute x12, waiting for transfers between devices, z_turn(): return lax.ppermute(x, 'group', [(i, (i + by) % n) for i in range(n)])  126 us
    ppermute x8, waiting for transfers between devices, z_shift(): lax.ppermute(x, 'group', [(i, i + by) for i in range(n) if 0 <= i + by < n])  112 us
    dot_general x12, matrix products, mm(): return lax.dot_general(a, b, (dims, ((), ())), preferred_element_type=F32)  77.7 us
    ppermute x92, starting transfers between devices, swap(): return lax.ppermute(x, 'replica', [(i, i ^ bits) for i in range(n)])  69.4 us
    ppermute x8, starting transfers between devices, z_shift(): lax.ppermute(x, 'group', [(i, i + by) for i in range(n) if 0 <= i + by < n])  43.4 us
    pallas_call x4, Pallas kernels, spread_part(): pl.pallas_call(kernel, grid=(height // q,), in_specs=[pl.BlockSpec(memory...  34.1 us
  transfers between devices with their start and end apart: 117, of which 45 were waited for; matrix products, arithmetic and copies ran while one was open for 16% of the time, Pallas kernels for 12%

profile of v4, /device:TPU:0, one launch (start us, length us, event | category | flops | bytes accessed | tf_op | source)
XLA Modules:
  0.0 983.4 jit_solution(16318956592310616921)
XLA Ops:
  35.1 13.5 %collective-permute-done.10.refs_7_ = bf16[256,1536]{1,0:T(8,128)(2,1)} collective-permute-done((bf16[256,1536]{1,0:T(8,128)(2,1)}, bf16[256,1536]{1,0:T(8,128)(2,1)}, u32[]{:S(2)}, u32[]{:S(2)}) %collective-permute-start.10) | collective-permute-done | bytes 786464 | tf_op jit(solution)/shard_map/ppermute | solution.py:57
  51.1 28.5 %collective-permute-done.11.refs_8_ = bf16[256,1536]{1,0:T(8,128)(2,1)S(1)} collective-permute-done((bf16[256,1536]{1,0:T(8,128)(2,1)}, bf16[256,1536]{1,0:T(8,128)(2,1)S(1)}, u32[]{:S(2)}, u32[]{:S(2)}) %collective-permute-start.11) | collective-permute-done | bytes 786464 | tf_op jit(solution)/shard_map/ppermute | solution.py:57
  86.3 18.7 %collective-permute-done.18 = s32[1,256]{1,0:T(1,128)S(1)} collective-permute-done((s32[1,256]{1,0:T(1,128)S(1)}, s32[1,256]{1,0:T(1,128)S(1)}, u32[]{:S(2)}, u32[]{:S(2)}) %collective-permute-start.18) | collective-permute-done | bytes 1056 | tf_op jit(solution)/shard_map/ppermute | solution.py:30
  119.8 10.0 %collective-permute-done.8.refs_4_ = bf16[128,2048]{1,0:T(8,128)(2,1)S(1)} collective-permute-done((bf16[128,2048]{1,0:T(8,128)(2,1)S(1)}, bf16[128,2048]{1,0:T(8,128)(2,1)S(1)}, u32[]{:S(2)}, u32[]{:S(2)}) %collective-permute-start.8) | collective-permute-done | bytes 524320 | tf_op jit(solution)/shard_map/ppermute | solution.py:30
  130.6 32.4 %shard_map.204 = (bf16[4,256,512]{2,1,0:T(8,128)(2,1)}, bf16[4,256,512]{2,1,0:T(8,128)(2,1)}, bf16[4,256,512]{2,1,0:T(8,128)(2,1)}, bf16[4,4,256,256]{3,2,1,0:T(...) custom-call(s32[3]{0:T(128)} %pad_add_fusion.idx_ref.refs_0_, ...), custom_call_target="tpu_custom_call" | custom-call | flops 44000002048 | tf_op jit(solution)/shard_map/pallas_call | solution.py:796
  165.6 15.6 %collective-permute-start.20 = (bf16[4,4,128,128]{3,2,1,0:T(8,128)(2,1)}, bf16[4,4,128,128]{3,2,1,0:T(8,128)(2,1)S(1)}, u32[]{:S(2)}, u32[]{:S(2)}) collective-permute-start(bf16[4,4,128,128]{3,2,1,0:T(8,128)(2,1)} %fusion.13), channel_id=1, source_target_pairs={{0,1},{1,2},{2,3},{4,5},{5,6},{6,7},{8,9},{9,10},{10,11},{12,13},{... | collective-permute-start | bytes 1572872 | tf_op jit(solution)/shard_map/ppermute | solution.py:52
  184.8 17.5 %collective-permute-done.20 = bf16[4,4,128,128]{3,2,1,0:T(8,128)(2,1)S(1)} collective-permute-done((bf16[4,4,128,128]{3,2,1,0:T(8,128)(2,1)}, bf16[4,4,128,128]{3,2,1,0:T(8,128)(2,1)S(1)}, u32[]{:S(2)}, u32[]{:S(2)}) %collective-permute-start.20) | collective-permute-done | bytes 524320 | tf_op jit(solution)/shard_map/ppermute | solution.py:52
  202.6 8.5 collective-permute-start.21
  220.6 10.5 %collective-permute-done.21 = bf16[4,4,128,128]{3,2,1,0:T(8,128)(2,1)S(1)} collective-permute-done((bf16[4,4,128,128]{3,2,1,0:T(8,128)(2,1)S(1)}, bf16[4,4,128,128]{3,2,1,0:T(8,128)(2,1)S(1)}, u32[]{:S(2)}, u32[]{:S(2)}) %collective-permute-start.21) | collective-permute-done | bytes 524320 | tf_op jit(solution)/shard_map/ppermute | solution.py:52
  248.8 10.9 %collective-permute-start.29 = (bf16[4,4,128,128]{3,2,1,0:T(8,128)(2,1)S(1)}, bf16[4,4,128,128]{3,2,1,0:T(8,128)(2,1)S(1)}, u32[]{:S(2)}, u32[]{:S(2)}) collective-permute-start(bf16[4,4,128,128]{3,2,1,0:T(8,128)(2,1)S(1)} %convolution_add_fusion.3), channel_id=1, source_target_pairs={{0,1},{1,2},{2,3},{4,5},{5,6},{6,7},{8,9},{9,10},{10,11},{12,13},{... | collective-permute-start | bytes 1572872 | tf_op jit(solution)/shard_map/ppermute | solution.py:52
  261.9 16.5 %collective-permute-done.29.s_ref = bf16[4,4,128,128]{3,2,1,0:T(8,128)(2,1)S(1)} collective-permute-done((bf16[4,4,128,128]{3,2,1,0:T(8,128)(2,1)S(1)}, bf16[4,4,128,128]{3,2,1,0:T(8,128)(2,1)S(1)}, u32[]{:S(2)}, u32[]{:S(2)}) %collective-permute-start.29) | collective-permute-done | bytes 524320 | tf_op jit(solution)/shard_map/ppermute | solution.py:52
  302.9 8.1 shard_map.207
  313.5 21.7 %collective-permute-done.38.refs_2_ = bf16[256,2048]{1,0:T(8,128)(2,1)S(1)} collective-permute-done((bf16[256,2048]{1,0:T(8,128)(2,1)}, bf16[256,2048]{1,0:T(8,128)(2,1)S(1)}, u32[]{:S(2)}, u32[]{:S(2)}) %collective-permute-start.38) | collective-permute-done | bytes 1048608 | tf_op jit(solution)/shard_map/ppermute | solution.py:30
  340.4 11.3 %collective-permute-done.42.refs_9_ = bf16[128,2048]{1,0:T(8,128)(2,1)S(1)} collective-permute-done((bf16[128,2048]{1,0:T(8,128)(2,1)S(1)}, bf16[128,2048]{1,0:T(8,128)(2,1)S(1)}, u32[]{:S(2)}, u32[]{:S(2)}) %collective-permute-start.42) | collective-permute-done | bytes 524320 | tf_op jit(solution)/shard_map/ppermute | solution.py:30
  362.1 9.4 collective-permute-done.40.refs_4_
  372.6 47.2 %shard_map.208 = (bf16[4,256,1408]{2,1,0:T(8,128)(2,1)}, bf16[4,256,2816]{2,1,0:T(8,128)(2,1)}, bf16[4,256,2048]{2,1,0:T(8,128)(2,1)}, bf16[4,256,1024]{2,1,0:T(...) custom-call(s32[3]{0:T(128)} %pad_add_fusion.idx_ref.refs_0_, ...), custom_call_target="tpu_custom_call" | custom-call | flops 49500000256 | tf_op jit(solution)/shard_map/pallas_call | solution.py:796
  435.1 16.6 %bitcast_convert_fusion = bf16[1408,1024]{1,0:T(8,128)(2,1)} fusion(bf16[4,256,1408]{2,1,0:T(8,128)(2,1)S(1)} %copy-done.68, bf16[4,256,1024]{2,1,0:T(8,128)(2,1)S(1)} %copy-done.73), kind=kOutput, calls=%fused_computation.5 | convolution fusion | flops 2954231808 | bytes 7864320 | tf_op jit(solution)/shard_map/dot_general | solution.py:809
  461.6 8.5 add_convert_fusion.3
  482.1 10.3 %shard_map.209 = (f32[256,2048]{1,0:T(8,128)}, bf16[256,1024]{1,0:T(8,128)(2,1)}, bf16[256,1024]{1,0:T(8,128)(2,1)}, bf16[256,512]{1,0:T(8,128)(2,1)}, bf16[256,...) custom-call(s32[3]{0:T(128)} %pad_add_fusion.idx_ref.refs_0_, ...), custom_call_target="tpu_custom_call" | custom-call | flops 14300000256 | tf_op jit(solution)/shard_map/pallas_call | solution.py:579
  527.5 8.4 reduce-scatter.4.cloned.1.call-done
  535.9 12.4 %shard_map.210 = (bf16[4,256,512]{2,1,0:T(8,128)(2,1)}, f32[4,256,512]{2,1,0:T(8,128)}, bf16[4,256,512]{2,1,0:T(8,128)(2,1)}, f32[4,4,128,128]{3,2,1,0:T(8,128)}, f32[8,128]{1,0:T(8,128)}) custom-call(f32[1,128]{1,0:T(1,128)} %bitcast_convert_fusion.1.gain_ref, bf16[4,256,512]{2,1,0:T(8,128)(2,1)} %pad_maximum_fusion.8.dn_ref, ...), custom_call_target="tpu_custom_call" | custom-call | flops 13200000000 | tf_op jit(solution)/shard_map/pallas_call | solution.py:796
  551.8 45.7 %collective-permute-done.60 = bf16[4,4,128,128]{3,2,1,0:T(8,128)(2,1)S(1)} collective-permute-done((bf16[4,4,128,128]{3,2,1,0:T(8,128)(2,1)S(1)}, bf16[4,4,128,128]{3,2,1,0:T(8,128)(2,1)S(1)}, u32[]{:S(2)}, u32[]{:S(2)}) %collective-permute-start.60) | collective-permute-done | bytes 524320 | tf_op jit(solution)/shard_map/ppermute | solution.py:52
  600.3 14.8 %collective-permute-done.61 = bf16[4,4,128,128]{3,2,1,0:T(8,128)(2,1)S(1)} collective-permute-done((bf16[4,4,128,128]{3,2,1,0:T(8,128)(2,1)S(1)}, bf16[4,4,128,128]{3,2,1,0:T(8,128)(2,1)S(1)}, u32[]{:S(2)}, u32[]{:S(2)}) %collective-permute-start.61) | collective-permute-done | bytes 524320 | tf_op jit(solution)/shard_map/ppermute | solution.py:52
  630.2 36.4 %shard_map.212 = (bf16[4,272,1536]{2,1,0:T(8,128)(2,1)}, bf16[4,272,128]{2,1,0:T(8,128)(2,1)}, bf16[4,272,2048]{2,1,0:T(8,128)(2,1)}, f32[3,4,512]{2,1,0:T(4,128)}) custom-call(f32[3,4,512]{2,1,0:T(4,128)} %convert_bitcast_fusion.refs_15_.taps_ref, bf16[2048,1536]{1,0:T(8,128)(2,1)} %get-tuple-element.102.w_ref, bf16[2048,128]{1,0:T(8,128)(2,1)} %pad.10.refs_14_.beta_ref, ...), custom_call_target="tpu_custom_call" | custom-call | flops 48399998976 | tf_op jit(solution)/shard_map/pallas_call | solution.py:796
  711.7 12.4 %collective-permute-done.77 = bf16[128,2048]{1,0:T(8,128)(2,1)S(1)} collective-permute-done((bf16[128,2048]{1,0:T(8,128)(2,1)S(1)}, bf16[128,2048]{1,0:T(8,128)(2,1)S(1)}, u32[]{:S(2)}, u32[]{:S(2)}) %collective-permute-start.77) | collective-permute-done | bytes 524320 | tf_op jit(solution)/shard_map/ppermute | solution.py:30
  725.0 10.8 %collective-permute-done.75 = bf16[128,2048]{1,0:T(8,128)(2,1)S(1)} collective-permute-done((bf16[128,2048]{1,0:T(8,128)(2,1)S(1)}, bf16[128,2048]{1,0:T(8,128)(2,1)S(1)}, u32[]{:S(2)}, u32[]{:S(2)}) %collective-permute-start.75) | collective-permute-done | bytes 524320 | tf_op jit(solution)/shard_map/ppermute | solution.py:30
  748.1 26.3 %collective-permute-done.74 = bf16[256,1536]{1,0:T(8,128)(2,1)S(1)} collective-permute-done((bf16[256,1536]{1,0:T(8,128)(2,1)S(1)}, bf16[256,1536]{1,0:T(8,128)(2,1)S(1)}, u32[]{:S(2)}, u32[]{:S(2)}) %collective-permute-start.74) | collective-permute-done | bytes 786464 | tf_op jit(solution)/shard_map/ppermute | solution.py:57
  774.4 51.5 %collective-permute-done.73 = bf16[256,1536]{1,0:T(8,128)(2,1)S(1)} collective-permute-done((bf16[256,1536]{1,0:T(8,128)(2,1)S(1)}, bf16[256,1536]{1,0:T(8,128)(2,1)S(1)}, u32[]{:S(2)}, u32[]{:S(2)}) %collective-permute-start.73) | collective-permute-done | bytes 786464 | tf_op jit(solution)/shard_map/ppermute | solution.py:57
  854.9 17.4 %collective-permute-done.70 = bf16[256,2048]{1,0:T(8,128)(2,1)} collective-permute-done((bf16[256,2048]{1,0:T(8,128)(2,1)}, bf16[256,2048]{1,0:T(8,128)(2,1)}, u32[]{:S(2)}, u32[]{:S(2)}) %collective-permute-start.70) | collective-permute-done | bytes 1048608 | tf_op jit(solution)/shard_map/ppermute | solution.py:30
  880.9 11.8 %shard_map.214 = f32[2,256,11264]{2,1,0:T(8,128)} custom-call(s32[3]{0:T(128)} %pad_add_fusion.idx_ref.refs_0_, bf16[256,2816]{1,0:T(8,128)(2,1)} %copy-done.9, bf16[256,2816]{1,0:T(8,128)(2,1)} %collective-permute-done.85.refs_1_, bf16[256,2816]{1,0:T(8,128)(2,1)} %collective-permute-done.86.refs_2_, bf16[128,2816]{1,0:T(8,128)(2,1)} %collective-permute-done.87.refs_3_, ...), custom_call_target="tpu_custom_call" | custom-call | flops 55000000 | tf_op jit(solution)/shard_map/pallas_call | solution.py:760
  898.4 19.4 %collective-permute-done.103.refs_1_ = bf16[256,1536]{1,0:T(8,128)(2,1)} collective-permute-done((bf16[256,1536]{1,0:T(8,128)(2,1)}, bf16[256,1536]{1,0:T(8,128)(2,1)}, u32[]{:S(2)}, u32[]{:S(2)}) %collective-permute-start.103) | collective-permute-done | bytes 786464 | tf_op jit(solution)/shard_map/ppermute | solution.py:30
  957.5 9.9 %shard_map.216 = f32[1408,2048]{1,0:T(8,128)} custom-call(s32[3]{0:T(128)} %pad_add_fusion.idx_ref.refs_0_, bf16[1920,256]{1,0:T(8,128)(2,1)} %bitcast.213, bf16[1920,256]{1,0:T(8,128)(2,1)} %copy-done.7, bf16[1920,256]{1,0:T(8,128)(2,1)} %copy-done.8, bf16[1024,256]{1,0:T(8,128)(2,1)} %collective-permute-done.96.refs_3_, bf16[896,256]{1,0:T(8,128)(2,1)} %copy-done.19, ...), custom_call_target="tpu_custom_call" | custom-call | flops 55000000 | tf_op jit(solution)/shard_map/pallas_call | solution.py:760
  (540 shorter events, 374.6 us)
Async XLA Ops:
  7.2 174.1 %all-gather.6.cloned.1.call-start = ((), (), s32[]{:S(2)}) async-start(), calls=%async_computation.7 | async-start | bytes 4915200 | tf_op jit(solution)/shard_map/all_gather | solution.py:907
  20.6 93.3 %collective-permute-start.4 = (bf16[256,2048]{1,0:T(8,128)(2,1)}, bf16[256,2048]{1,0:T(8,128)(2,1)}, u32[]{:S(2)}, u32[]{:S(2)}) collective-permute-start(bf16[256,2048]{1,0:T(8,128)(2,1)} %bitcast.14.refs_6_.cot_ref), channel_id=1, source_target_pairs={{0,8},{4,12},{8,0},{12,4},{16,24},{20,28},{24,16},{28,20},{1,9},{5... | collective-permute-start | bytes 3145736 | tf_op jit(solution)/shard_map/ppermute | solution.py:30
  27.6 51.9 %collective-permute-start.11 = (bf16[256,1536]{1,0:T(8,128)(2,1)}, bf16[256,1536]{1,0:T(8,128)(2,1)S(1)}, u32[]{:S(2)}, u32[]{:S(2)}) collective-permute-start(bf16[256,1536]{1,0:T(8,128)(2,1)} %pad_maximum_fusion.14.refs_6_), channel_id=1, source_target_pairs={{0,2},{1,3},{2,0},{3,1},{4,6},{5,7},{6,4},{7,5},{8,10},{9,11},{10,... | collective-permute-start | bytes 2359304 | tf_op jit(solution)/shard_map/ppermute | solution.py:57
  28.0 53.1 %collective-permute-start.12 = (bf16[256,1536]{1,0:T(8,128)(2,1)}, bf16[256,1536]{1,0:T(8,128)(2,1)S(1)}, u32[]{:S(2)}, u32[]{:S(2)}) collective-permute-start(bf16[256,1536]{1,0:T(8,128)(2,1)} %pad_maximum_fusion.14.refs_6_), channel_id=1, source_target_pairs={{0,3},{1,0},{2,1},{3,2},{4,7},{5,4},{6,5},{7,6},{8,11},{9,8},{10,9... | collective-permute-start | bytes 2359304 | tf_op jit(solution)/shard_map/ppermute | solution.py:57
  33.6 80.8 %collective-permute-start.6 = (bf16[272,2048]{1,0:T(8,128)(2,1)}, bf16[272,2048]{1,0:T(8,128)(2,1)}, u32[]{:S(2)}, u32[]{:S(2)}) collective-permute-start(bf16[272,2048]{1,0:T(8,128)(2,1)} %shard_map.203.refs_1_), channel_id=1, source_target_pairs={{0,8},{4,12},{8,0},{12,4},{16,24},{20,28},{24,16},{28,20},{1,9},{5... | collective-permute-start | bytes 3342344 | tf_op jit(solution)/shard_map/ppermute | solution.py:30
  48.5 63.7 %collective-permute-start.7 = (bf16[272,2048]{1,0:T(8,128)(2,1)}, bf16[272,2048]{1,0:T(8,128)(2,1)}, u32[]{:S(2)}, u32[]{:S(2)}) collective-permute-start(bf16[272,2048]{1,0:T(8,128)(2,1)} %shard_map.203.refs_1_), channel_id=1, source_target_pairs={{0,16},{4,20},{8,24},{12,28},{16,0},{20,4},{24,8},{28,12},{1,17},{... | collective-permute-start | bytes 3342344 | tf_op jit(solution)/shard_map/ppermute | solution.py:30
  79.6 36.5 %collective-permute-start.5 = (bf16[256,2048]{1,0:T(8,128)(2,1)}, bf16[256,2048]{1,0:T(8,128)(2,1)}, u32[]{:S(2)}, u32[]{:S(2)}) collective-permute-start(bf16[256,2048]{1,0:T(8,128)(2,1)} %bitcast.14.refs_6_.cot_ref), channel_id=1, source_target_pairs={{0,16},{4,20},{8,24},{12,28},{16,0},{20,4},{24,8},{28,12},{1,17},{... | collective-permute-start | bytes 3145736 | tf_op jit(solution)/shard_map/ppermute | solution.py:30
  81.1 254.3 %all-gather.4.cloned.1.call-start = ((), (), s32[]{:S(2)}) async-start(), calls=%async_computation.3 | async-start | bytes 7208960 | tf_op jit(solution)/shard_map/all_gather | solution.py:945
  163.1 372.9 %reduce-scatter.4.cloned.1.call-start = ((), (), s32[]{:S(2)}) async-start(), calls=%async_computation.4 | async-start | bytes 3604480 | tf_op jit(solution)/shard_map/reduce_scatter | solution.py:1041
  165.6 36.7 %collective-permute-start.20 = (bf16[4,4,128,128]{3,2,1,0:T(8,128)(2,1)}, bf16[4,4,128,128]{3,2,1,0:T(8,128)(2,1)S(1)}, u32[]{:S(2)}, u32[]{:S(2)}) collective-permute-start(bf16[4,4,128,128]{3,2,1,0:T(8,128)(2,1)} %fusion.13), channel_id=1, source_target_pairs={{0,1},{1,2},{2,3},{4,5},{5,6},{6,7},{8,9},{9,10},{10,11},{12,13},{... | collective-permute-start | bytes 1572872 | tf_op jit(solution)/shard_map/ppermute | solution.py:52
  183.1 34.9 %collective-permute-start.26 = (bf16[2048,256]{1,0:T(8,128)(2,1)S(1)}, bf16[2048,256]{1,0:T(8,128)(2,1)}, u32[]{:S(2)}, u32[]{:S(2)}) collective-permute-start(bf16[2048,256]{1,0:T(8,128)(2,1)S(1)} %bitcast.224), channel_id=1, source_target_pairs={{0,16},{4,20},{8,24},{12,28},{16,0},{20,4},{24,8},{28,12},{1,17},{... | collective-permute-start | bytes 3145736 | tf_op jit(solution)/shard_map/ppermute | solution.py:30
  336.2 36.5 %collective-permute-start.44 = (bf16[1024,2816]{1,0:T(8,128)(2,1)}, bf16[1024,2816]{1,0:T(8,128)(2,1)}, u32[]{:S(2)}, u32[]{:S(2)}) collective-permute-start(bf16[1024,2816]{1,0:T(8,128)(2,1)} %all-gather.4.cloned.1.call-done.refs_11_), channel_id=1, source_target_pairs={{0,4},{4,0},{8,12},{12,8},{16,20},{20,16},{24,28},{28,24},{1,5},{5... | collective-permute-start | bytes 17301512 | tf_op jit(solution)/shard_map/ppermute | solution.py:30
  461.6 161.1 %reduce-scatter.6.cloned.1.call-start = ((), (), s32[]{:S(2)}) async-start(), calls=%async_computation.5 | async-start | bytes 3604480 | tf_op jit(solution)/shard_map/reduce_scatter | solution.py:1043
  501.7 350.6 %reduce-scatter.8.cloned.1.call-start = ((), (), s32[]{:S(2)}) async-start(), calls=%async_computation.6 | async-start | bytes 4915200 | tf_op jit(solution)/shard_map/reduce_scatter | solution.py:1088
  520.1 96.8 %collective-permute-start.63 = (bf16[3456,256]{1,0:T(8,128)(2,1)}, bf16[3456,256]{1,0:T(8,128)(2,1)}, u32[]{:S(2)}, u32[]{:S(2)}) collective-permute-start(bf16[3456,256]{1,0:T(8,128)(2,1)} %pad_maximum_fusion.1), channel_id=1, source_target_pairs={{0,8},{4,12},{8,0},{12,4},{16,24},{20,28},{24,16},{28,20},{1,9},{5... | collective-permute-start | bytes 5308424 | tf_op jit(solution)/shard_map/ppermute | solution.py:30
  522.7 94.1 %collective-permute-start.64 = (bf16[3456,256]{1,0:T(8,128)(2,1)}, bf16[3456,256]{1,0:T(8,128)(2,1)}, u32[]{:S(2)}, u32[]{:S(2)}) collective-permute-start(bf16[3456,256]{1,0:T(8,128)(2,1)} %pad_maximum_fusion.2), channel_id=1, source_target_pairs={{0,16},{4,20},{8,24},{12,28},{16,0},{20,4},{24,8},{28,12},{1,17},{... | collective-permute-start | bytes 5308424 | tf_op jit(solution)/shard_map/ppermute | solution.py:30
  524.7 92.2 %collective-permute-start.65 = (bf16[3456,256]{1,0:T(8,128)(2,1)}, bf16[3456,256]{1,0:T(8,128)(2,1)}, u32[]{:S(2)}, u32[]{:S(2)}) collective-permute-start(bf16[3456,256]{1,0:T(8,128)(2,1)} %pad_maximum_fusion.3), channel_id=1, source_target_pairs={{0,24},{4,28},{8,16},{12,20},{16,8},{20,12},{24,0},{28,4},{1,25},{... | collective-permute-start | bytes 5308424 | tf_op jit(solution)/shard_map/ppermute | solution.py:30
  550.1 47.4 %collective-permute-start.60 = (bf16[4,4,128,128]{3,2,1,0:T(8,128)(2,1)S(1)}, bf16[4,4,128,128]{3,2,1,0:T(8,128)(2,1)S(1)}, u32[]{:S(2)}, u32[]{:S(2)}) collective-permute-start(bf16[4,4,128,128]{3,2,1,0:T(8,128)(2,1)S(1)} %fusion.15), channel_id=1, source_target_pairs={{1,0},{2,1},{3,2},{5,4},{6,5},{7,6},{9,8},{10,9},{11,10},{13,12},{... | collective-permute-start | bytes 1572872 | tf_op jit(solution)/shard_map/ppermute | solution.py:52
  676.8 61.1 %collective-permute-start.85 = (bf16[256,2816]{1,0:T(8,128)(2,1)S(1)}, bf16[256,2816]{1,0:T(8,128)(2,1)}, u32[]{:S(2)}, u32[]{:S(2)}) collective-permute-start(bf16[256,2816]{1,0:T(8,128)(2,1)S(1)} %pad_maximum_fusion.5.refs_0_), channel_id=1, source_target_pairs={{0,8},{4,12},{8,0},{12,4},{16,24},{20,28},{24,16},{28,20},{1,9},{5... | collective-permute-start | bytes 4325384 | tf_op jit(solution)/shard_map/ppermute | solution.py:30
  679.6 59.7 %collective-permute-start.86 = (bf16[256,2816]{1,0:T(8,128)(2,1)S(1)}, bf16[256,2816]{1,0:T(8,128)(2,1)}, u32[]{:S(2)}, u32[]{:S(2)}) collective-permute-start(bf16[256,2816]{1,0:T(8,128)(2,1)S(1)} %pad_maximum_fusion.5.refs_0_), channel_id=1, source_target_pairs={{0,16},{4,20},{8,24},{12,28},{16,0},{20,4},{24,8},{28,12},{1,17},{... | collective-permute-start | bytes 4325384 | tf_op jit(solution)/shard_map/ppermute | solution.py:30
  706.1 33.6 %collective-permute-start.67 = (bf16[128,2048]{1,0:T(8,128)(2,1)S(1)}, bf16[128,2048]{1,0:T(8,128)(2,1)S(1)}, u32[]{:S(2)}, u32[]{:S(2)}) collective-permute-start(bf16[128,2048]{1,0:T(8,128)(2,1)S(1)} %get-tuple-element.167), channel_id=1, source_target_pairs={{0,16},{4,20},{8,24},{12,28},{16,0},{20,4},{24,8},{28,12},{1,17},{... | collective-permute-start | bytes 1572872 | tf_op jit(solution)/shard_map/ppermute | solution.py:30
  735.8 38.5 %collective-permute-start.74 = (bf16[256,1536]{1,0:T(8,128)(2,1)S(1)}, bf16[256,1536]{1,0:T(8,128)(2,1)S(1)}, u32[]{:S(2)}, u32[]{:S(2)}) collective-permute-start(bf16[256,1536]{1,0:T(8,128)(2,1)S(1)} %get-tuple-element.181), channel_id=1, source_target_pairs={{0,3},{1,0},{2,1},{3,2},{4,7},{5,4},{6,5},{7,6},{8,11},{9,8},{10,9... | collective-permute-start | bytes 2359304 | tf_op jit(solution)/shard_map/ppermute | solution.py:57
  738.0 87.9 %collective-permute-start.73 = (bf16[256,1536]{1,0:T(8,128)(2,1)S(1)}, bf16[256,1536]{1,0:T(8,128)(2,1)S(1)}, u32[]{:S(2)}, u32[]{:S(2)}) collective-permute-start(bf16[256,1536]{1,0:T(8,128)(2,1)S(1)} %get-tuple-element.182), channel_id=1, source_target_pairs={{0,2},{1,3},{2,0},{3,1},{4,6},{5,7},{6,4},{7,5},{8,10},{9,11},{10,... | collective-permute-start | bytes 2359304 | tf_op jit(solution)/shard_map/ppermute | solution.py:57
  739.3 88.1 %collective-permute-start.76 = (bf16[256,2048]{1,0:T(8,128)(2,1)S(1)}, bf16[256,2048]{1,0:T(8,128)(2,1)S(1)}, u32[]{:S(2)}, u32[]{:S(2)}) collective-permute-start(bf16[256,2048]{1,0:T(8,128)(2,1)S(1)} %pad_maximum_fusion.11), channel_id=1, source_target_pairs={{0,8},{4,12},{8,0},{12,4},{16,24},{20,28},{24,16},{28,20},{1,9},{5... | collective-permute-start | bytes 3145736 | tf_op jit(solution)/shard_map/ppermute | solution.py:30
  739.7 89.2 %collective-permute-start.78 = (bf16[256,2048]{1,0:T(8,128)(2,1)S(1)}, bf16[256,2048]{1,0:T(8,128)(2,1)S(1)}, u32[]{:S(2)}, u32[]{:S(2)}) collective-permute-start(bf16[256,2048]{1,0:T(8,128)(2,1)S(1)} %pad_maximum_fusion.12), channel_id=1, source_target_pairs={{0,16},{4,20},{8,24},{12,28},{16,0},{20,4},{24,8},{28,12},{1,17},{... | collective-permute-start | bytes 3145736 | tf_op jit(solution)/shard_map/ppermute | solution.py:30
  741.5 85.6 %collective-permute-start.72 = (bf16[256,1536]{1,0:T(8,128)(2,1)S(1)}, bf16[256,1536]{1,0:T(8,128)(2,1)S(1)}, u32[]{:S(2)}, u32[]{:S(2)}) collective-permute-start(bf16[256,1536]{1,0:T(8,128)(2,1)S(1)} %get-tuple-element.180), channel_id=1, source_target_pairs={{0,1},{1,2},{2,3},{3,0},{4,5},{5,6},{6,7},{7,4},{8,9},{9,10},{10,1... | collective-permute-start | bytes 2359304 | tf_op jit(solution)/shard_map/ppermute | solution.py:57
  774.4 75.5 %collective-permute-start.90 = (bf16[256,2816]{1,0:T(8,128)(2,1)}, bf16[256,2816]{1,0:T(8,128)(2,1)}, u32[]{:S(2)}, u32[]{:S(2)}) collective-permute-start(bf16[256,2816]{1,0:T(8,128)(2,1)} %collective-permute-done.85.refs_1_), channel_id=1, source_target_pairs={{0,4},{4,0},{8,12},{12,8},{16,20},{20,16},{24,28},{28,24},{1,5},{5... | collective-permute-start | bytes 4325384 | tf_op jit(solution)/shard_map/ppermute | solution.py:30
  848.4 45.3 %collective-permute-start.68 = (bf16[256,2048]{1,0:T(8,128)(2,1)}, bf16[256,2048]{1,0:T(8,128)(2,1)S(1)}, u32[]{:S(2)}, u32[]{:S(2)}) collective-permute-start(bf16[256,2048]{1,0:T(8,128)(2,1)} %pad_maximum_fusion.9), channel_id=1, source_target_pairs={{0,8},{4,12},{8,0},{12,4},{16,24},{20,28},{24,16},{28,20},{1,9},{5... | collective-permute-start | bytes 3145736 | tf_op jit(solution)/shard_map/ppermute | solution.py:30
  853.2 68.9 %collective-permute-start.94 = (bf16[1920,256]{1,0:T(8,128)(2,1)}, bf16[1920,256]{1,0:T(8,128)(2,1)S(1)}, u32[]{:S(2)}, u32[]{:S(2)}) collective-permute-start(bf16[1920,256]{1,0:T(8,128)(2,1)} %bitcast.210), channel_id=1, source_target_pairs={{0,8},{4,12},{8,0},{12,4},{16,24},{20,28},{24,16},{28,20},{1,9},{5... | collective-permute-start | bytes 2949128 | tf_op jit(solution)/shard_map/ppermute | solution.py:30
  854.4 67.7 %collective-permute-start.95 = (bf16[1920,256]{1,0:T(8,128)(2,1)}, bf16[1920,256]{1,0:T(8,128)(2,1)S(1)}, u32[]{:S(2)}, u32[]{:S(2)}) collective-permute-start(bf16[1920,256]{1,0:T(8,128)(2,1)} %bitcast.211), channel_id=1, source_target_pairs={{0,16},{4,20},{8,24},{12,28},{16,0},{20,4},{24,8},{28,12},{1,17},{... | collective-permute-start | bytes 2949128 | tf_op jit(solution)/shard_map/ppermute | solution.py:30
  872.3 45.5 %collective-permute-start.103 = (bf16[256,1536]{1,0:T(8,128)(2,1)}, bf16[256,1536]{1,0:T(8,128)(2,1)}, u32[]{:S(2)}, u32[]{:S(2)}) collective-permute-start(bf16[256,1536]{1,0:T(8,128)(2,1)} %fusion.12.refs_0_), channel_id=1, source_target_pairs={{0,8},{4,12},{8,0},{12,4},{16,24},{20,28},{24,16},{28,20},{1,9},{5... | collective-permute-start | bytes 2359304 | tf_op jit(solution)/shard_map/ppermute | solution.py:30
  880.3 37.5 %collective-permute-start.104 = (bf16[256,1536]{1,0:T(8,128)(2,1)}, bf16[256,1536]{1,0:T(8,128)(2,1)}, u32[]{:S(2)}, u32[]{:S(2)}) collective-permute-start(bf16[256,1536]{1,0:T(8,128)(2,1)} %fusion.12.refs_0_), channel_id=1, source_target_pairs={{0,16},{4,20},{8,24},{12,28},{16,0},{20,4},{24,8},{28,12},{1,17},{... | collective-permute-start | bytes 2359304 | tf_op jit(solution)/shard_map/ppermute | solution.py:30
  (167 other events, 2907.6 us)
Sparse Core Ops, SparseCore 0:
  81.3 89.3 all-gather.5
  172.8 134.3 all-gather.3
  461.7 74.2 reduce-scatter.3
  538.1 67.8 reduce-scatter.5
  682.2 92.8 reduce-scatter.7

commit v5 on v4

--- a/solution.py
+++ b/solution.py
@@ -770,7 +770,7 @@
 
 
 def cost(us):
-    return pl.CostEstimate(flops=int(us * 1.1e9), bytes_accessed=0, transcendentals=0)
+    return pl.CostEstimate(flops=int(us * 2.2e9), bytes_accessed=0, transcendentals=0)
 
 
 def block(shape, fixed=False):

time: 988 us -> 1010 us (1.022)
  waiting for transfers between devices: 450 us -> 497 us
  matrix products: 84.5 us -> 70.6 us
  starting transfers between devices: 129 us -> 116 us
    all_gather x1, waiting for transfers between devices: 0.02 us -> 34.8 us  [body(): both = lax.all_gather(after(piece, *qkv_late), 'group', axis=0)]
    ppermute x8, waiting for transfers between devices: 112 us -> 77.3 us  [z_shift(): lax.ppermute(x, 'group', [(i, i + by) for i in range(n) if 0 <= i + by < n])]
    ppermute x92, waiting for transfers between devices: 204 us -> 237 us  [swap(): return lax.ppermute(x, 'replica', [(i, i ^ bits) for i in range(n)])]
    reduce_scatter x1, waiting for transfers between devices: 8.4 us -> 23.9 us  [body(): lax.psum_scatter(gate_sums[0], 'group', scatter_dimension=0)]
    dot_general x12, matrix products: 77.7 us -> 63.9 us  [mm(): return lax.dot_general(a, b, (dims, ((), ())), preferred_element_type=F32)]
    ppermute x8, starting transfers between devices: 43.4 us -> 31.2 us  [z_shift(): lax.ppermute(x, 'group', [(i, i + by) for i in range(n) if 0 <= i + by < n])]
  transfers between devices with their start and end apart: 117 -> 117, of which waited for: 45 -> 43; matrix products, arithmetic and copies ran while one was open for 16% -> 13% of each run, Pallas kernels for 12% -> 11%
where the time goes in v5:
time: 1010 us; the launch traced here: 1000 us
  waiting for transfers between devices  497 us (49%)
  Pallas kernels  209 us (21%)
  starting transfers between devices  116 us (11%)
  matrix products  70.6 us (7%)
  local copies, waits for them, and re-layouts  63.9 us (6%)
  other arithmetic  27.3 us (3%)
  between operations  15.7 us (2%)
    ppermute x92, waiting for transfers between devices, swap(): return lax.ppermute(x, 'replica', [(i, i ^ bits) for i in range(n)])  237 us
    pallas_call x5, Pallas kernels, call(): pl.pallas_call(kernel, grid=(count,), in_specs=(lead if extra else []) +...  135 us
    ppermute x12, waiting for transfers between devices, z_turn(): return lax.ppermute(x, 'group', [(i, (i + by) % n) for i in range(n)])  124 us
    ppermute x8, waiting for transfers between devices, z_shift(): lax.ppermute(x, 'group', [(i, i + by) for i in range(n) if 0 <= i + by < n])  77.3 us
    ppermute x92, starting transfers between devices, swap(): return lax.ppermute(x, 'replica', [(i, i ^ bits) for i in range(n)])  70.7 us
    dot_general x12, matrix products, mm(): return lax.dot_general(a, b, (dims, ((), ())), preferred_element_type=F32)  63.9 us
    all_gather x1, waiting for transfers between devices, body(): both = lax.all_gather(after(piece, *qkv_late), 'group', axis=0)  34.8 us
    pallas_call x4, Pallas kernels, spread_part(): pl.pallas_call(kernel, grid=(height // q,), in_specs=[pl.BlockSpec(memory...  34.1 us
  transfers between devices with their start and end apart: 117, of which 43 were waited for; matrix products, arithmetic and copies ran while one was open for 13% of the time, Pallas kernels for 11%

profile of v5, /device:TPU:0, one launch (start us, length us, event | category | flops | bytes accessed | tf_op | source)
XLA Modules:
  0.0 1000.2 jit_solution(4426931930698122356)
XLA Ops:
  38.5 12.4 %collective-permute-done.18 = s32[1,256]{1,0:T(1,128)S(1)} collective-permute-done((s32[1,256]{1,0:T(1,128)S(1)}, s32[1,256]{1,0:T(1,128)S(1)}, u32[]{:S(2)}, u32[]{:S(2)}) %collective-permute-start.18) | collective-permute-done | bytes 1056 | tf_op jit(solution)/shard_map/ppermute | solution.py:30
  54.6 27.1 %collective-permute-done.11.refs_8_ = bf16[256,1536]{1,0:T(8,128)(2,1)} collective-permute-done((bf16[256,1536]{1,0:T(8,128)(2,1)S(1)}, bf16[256,1536]{1,0:T(8,128)(2,1)}, u32[]{:S(2)}, u32[]{:S(2)}) %collective-permute-start.11) | collective-permute-done | bytes 786464 | tf_op jit(solution)/shard_map/ppermute | solution.py:57
  88.5 12.8 %collective-permute-done.12.refs_9_ = bf16[256,1536]{1,0:T(8,128)(2,1)} collective-permute-done((bf16[256,1536]{1,0:T(8,128)(2,1)S(1)}, bf16[256,1536]{1,0:T(8,128)(2,1)}, u32[]{:S(2)}, u32[]{:S(2)}) %collective-permute-start.12) | collective-permute-done | bytes 786464 | tf_op jit(solution)/shard_map/ppermute | solution.py:57
  107.3 11.4 %collective-permute-done.8.refs_4_ = bf16[128,2048]{1,0:T(8,128)(2,1)} collective-permute-done((bf16[128,2048]{1,0:T(8,128)(2,1)S(1)}, bf16[128,2048]{1,0:T(8,128)(2,1)}, u32[]{:S(2)}, u32[]{:S(2)}) %collective-permute-start.8) | collective-permute-done | bytes 524320 | tf_op jit(solution)/shard_map/ppermute | solution.py:30
  118.6 32.4 %shard_map.204 = (bf16[4,256,512]{2,1,0:T(8,128)(2,1)}, bf16[4,256,512]{2,1,0:T(8,128)(2,1)}, bf16[4,256,512]{2,1,0:T(8,128)(2,1)}, bf16[4,4,256,256]{3,2,1,0:T(...) custom-call(s32[3]{0:T(128)} %pad_add_fusion.idx_ref.refs_0_, ...), custom_call_target="tpu_custom_call" | custom-call | flops 88000004096 | tf_op jit(solution)/shard_map/pallas_call | solution.py:796
  155.0 34.8 %all-gather.6.cloned.1.call-done = bf16[7680,256]{1,0:T(8,128)(2,1)} async-done(((bf16[1920,256]{1,0:T(8,128)(2,1)}), bf16[7680,256]{1,0:T(8,128)(2,1)}) %all-gather.6.cloned.1.call-update) | async-done | bytes 3932176 | tf_op jit(solution)/shard_map/all_gather | solution.py:907
  202.6 14.8 %collective-permute-done.25.refs_1_ = bf16[2048,256]{1,0:T(8,128)(2,1)} collective-permute-done((bf16[2048,256]{1,0:T(8,128)(2,1)S(1)}, bf16[2048,256]{1,0:T(8,128)(2,1)}, u32[]{:S(2)}, u32[]{:S(2)}) %collective-permute-start.25) | collective-permute-done | bytes 1048608 | tf_op jit(solution)/shard_map/ppermute | solution.py:30
  223.5 9.2 collective-permute-done.22.refs_14_
  232.7 17.2 %collective-permute-done.23.refs_15_ = bf16[1408,256]{1,0:T(8,128)(2,1)S(1)} collective-permute-done((bf16[1408,256]{1,0:T(8,128)(2,1)S(1)}, bf16[1408,256]{1,0:T(8,128)(2,1)S(1)}, u32[]{:S(2)}, u32[]{:S(2)}) %collective-permute-start.23) | collective-permute-done | bytes 720928 | tf_op jit(solution)/shard_map/ppermute | solution.py:30
  249.9 9.8 collective-permute-done.27.refs_3_
  259.7 16.8 %collective-permute-start.29 = (bf16[4,4,128,128]{3,2,1,0:T(8,128)(2,1)S(1)}, bf16[4,4,128,128]{3,2,1,0:T(8,128)(2,1)S(1)}, u32[]{:S(2)}, u32[]{:S(2)}) collective-permute-start(bf16[4,4,128,128]{3,2,1,0:T(8,128)(2,1)S(1)} %convolution_add_fusion.3), channel_id=1, source_target_pairs={{0,1},{1,2},{2,3},{4,5},{5,6},{6,7},{8,9},{9,10},{10,11},{12,13},{... | collective-permute-start | bytes 1572872 | tf_op jit(solution)/shard_map/ppermute | solution.py:52
  278.7 8.3 collective-permute-done.29.s_ref
  321.9 21.7 %collective-permute-done.38.refs_2_ = bf16[256,2048]{1,0:T(8,128)(2,1)S(1)} collective-permute-done((bf16[256,2048]{1,0:T(8,128)(2,1)}, bf16[256,2048]{1,0:T(8,128)(2,1)S(1)}, u32[]{:S(2)}, u32[]{:S(2)}) %collective-permute-start.38) | collective-permute-done | bytes 1048608 | tf_op jit(solution)/shard_map/ppermute | solution.py:30
  348.9 11.1 %collective-permute-done.42.refs_9_ = bf16[128,2048]{1,0:T(8,128)(2,1)S(1)} collective-permute-done((bf16[128,2048]{1,0:T(8,128)(2,1)S(1)}, bf16[128,2048]{1,0:T(8,128)(2,1)S(1)}, u32[]{:S(2)}, u32[]{:S(2)}) %collective-permute-start.42) | collective-permute-done | bytes 524320 | tf_op jit(solution)/shard_map/ppermute | solution.py:30
  370.4 9.6 collective-permute-done.40.refs_4_
  381.0 47.2 %shard_map.208 = (bf16[4,256,1408]{2,1,0:T(8,128)(2,1)}, bf16[4,256,2816]{2,1,0:T(8,128)(2,1)}, bf16[4,256,2048]{2,1,0:T(8,128)(2,1)}, bf16[4,256,1024]{2,1,0:T(...) custom-call(s32[3]{0:T(128)} %pad_add_fusion.idx_ref.refs_0_, ...), custom_call_target="tpu_custom_call" | custom-call | flops 99000000512 | tf_op jit(solution)/shard_map/pallas_call | solution.py:796
  461.0 13.7 %collective-permute-done.50.p1 = bf16[256,2048]{1,0:T(8,128)(2,1)S(1)} collective-permute-done((bf16[256,2048]{1,0:T(8,128)(2,1)S(1)}, bf16[256,2048]{1,0:T(8,128)(2,1)S(1)}, u32[]{:S(2)}, u32[]{:S(2)}) %collective-permute-start.50) | collective-permute-done | bytes 1048608 | tf_op jit(solution)/shard_map/ppermute | solution.py:30
  475.7 8.7 add_convert_fusion.2
  484.7 9.8 shard_map.209
  530.1 23.9 %reduce-scatter.4.cloned.1.call-done = bf16[1,256,1408]{2,1,0:T(8,128)(2,1)} async-done(((bf16[4,256,1408]{2,1,0:T(8,128)(2,1)}), bf16[1,256,1408]{2,1,0:T(8,128)(2,1)}) %reduce-scatter.4.cloned.1.call-update) | async-done | bytes 720912 | tf_op jit(solution)/shard_map/reduce_scatter | solution.py:1041
  554.1 12.5 %shard_map.210 = (bf16[4,256,512]{2,1,0:T(8,128)(2,1)}, f32[4,256,512]{2,1,0:T(8,128)}, bf16[4,256,512]{2,1,0:T(8,128)(2,1)}, f32[4,4,128,128]{3,2,1,0:T(8,128)}, f32[8,128]{1,0:T(8,128)}) custom-call(f32[1,128]{1,0:T(1,128)} %bitcast_convert_fusion.1.gain_ref, bf16[4,256,512]{2,1,0:T(8,128)(2,1)} %pad_maximum_fusion.8.dn_ref, ...), custom_call_target="tpu_custom_call" | custom-call | flops 26400000000 | tf_op jit(solution)/shard_map/pallas_call | solution.py:796
  569.6 37.7 %collective-permute-done.60 = bf16[4,4,128,128]{3,2,1,0:T(8,128)(2,1)S(1)} collective-permute-done((bf16[4,4,128,128]{3,2,1,0:T(8,128)(2,1)S(1)}, bf16[4,4,128,128]{3,2,1,0:T(8,128)(2,1)S(1)}, u32[]{:S(2)}, u32[]{:S(2)}) %collective-permute-start.60) | collective-permute-done | bytes 524320 | tf_op jit(solution)/shard_map/ppermute | solution.py:52
  610.1 22.8 %collective-permute-done.61 = bf16[4,4,128,128]{3,2,1,0:T(8,128)(2,1)S(1)} collective-permute-done((bf16[4,4,128,128]{3,2,1,0:T(8,128)(2,1)S(1)}, bf16[4,4,128,128]{3,2,1,0:T(8,128)(2,1)S(1)}, u32[]{:S(2)}, u32[]{:S(2)}) %collective-permute-start.61) | collective-permute-done | bytes 524320 | tf_op jit(solution)/shard_map/ppermute | solution.py:52
  649.5 36.4 %shard_map.212 = (bf16[4,272,1536]{2,1,0:T(8,128)(2,1)}, bf16[4,272,128]{2,1,0:T(8,128)(2,1)}, bf16[4,272,2048]{2,1,0:T(8,128)(2,1)}, f32[3,4,512]{2,1,0:T(4,128)}) custom-call(f32[3,4,512]{2,1,0:T(4,128)} %convert_bitcast_fusion.refs_15_.taps_ref, bf16[2048,1536]{1,0:T(8,128)(2,1)} %get-tuple-element.102.w_ref, bf16[2048,128]{1,0:T(8,128)(2,1)} %pad.10.refs_14_.beta_ref, ...), custom_call_target="tpu_custom_call" | custom-call | flops 96799997952 | tf_op jit(solution)/shard_map/pallas_call | solution.py:796
  729.9 12.2 %collective-permute-done.77 = bf16[128,2048]{1,0:T(8,128)(2,1)S(1)} collective-permute-done((bf16[128,2048]{1,0:T(8,128)(2,1)S(1)}, bf16[128,2048]{1,0:T(8,128)(2,1)S(1)}, u32[]{:S(2)}, u32[]{:S(2)}) %collective-permute-start.77) | collective-permute-done | bytes 524320 | tf_op jit(solution)/shard_map/ppermute | solution.py:30
  743.0 10.8 %collective-permute-done.75 = bf16[128,2048]{1,0:T(8,128)(2,1)S(1)} collective-permute-done((bf16[128,2048]{1,0:T(8,128)(2,1)S(1)}, bf16[128,2048]{1,0:T(8,128)(2,1)S(1)}, u32[]{:S(2)}, u32[]{:S(2)}) %collective-permute-start.75) | collective-permute-done | bytes 524320 | tf_op jit(solution)/shard_map/ppermute | solution.py:30
  764.5 26.7 %collective-permute-done.74 = bf16[256,1536]{1,0:T(8,128)(2,1)S(1)} collective-permute-done((bf16[256,1536]{1,0:T(8,128)(2,1)S(1)}, bf16[256,1536]{1,0:T(8,128)(2,1)S(1)}, u32[]{:S(2)}, u32[]{:S(2)}) %collective-permute-start.74) | collective-permute-done | bytes 786464 | tf_op jit(solution)/shard_map/ppermute | solution.py:57
  791.3 51.4 %collective-permute-done.73 = bf16[256,1536]{1,0:T(8,128)(2,1)S(1)} collective-permute-done((bf16[256,1536]{1,0:T(8,128)(2,1)S(1)}, bf16[256,1536]{1,0:T(8,128)(2,1)S(1)}, u32[]{:S(2)}, u32[]{:S(2)}) %collective-permute-start.73) | collective-permute-done | bytes 786464 | tf_op jit(solution)/shard_map/ppermute | solution.py:57
  871.7 17.3 %collective-permute-done.70 = bf16[256,2048]{1,0:T(8,128)(2,1)} collective-permute-done((bf16[256,2048]{1,0:T(8,128)(2,1)}, bf16[256,2048]{1,0:T(8,128)(2,1)}, u32[]{:S(2)}, u32[]{:S(2)}) %collective-permute-start.70) | collective-permute-done | bytes 1048608 | tf_op jit(solution)/shard_map/ppermute | solution.py:30
  897.6 11.8 %shard_map.214 = f32[2,256,11264]{2,1,0:T(8,128)} custom-call(s32[3]{0:T(128)} %pad_add_fusion.idx_ref.refs_0_, bf16[256,2816]{1,0:T(8,128)(2,1)} %copy-done.11, bf16[256,2816]{1,0:T(8,128)(2,1)} %collective-permute-done.85.refs_1_, bf16[256,2816]{1,0:T(8,128)(2,1)} %collective-permute-done.86.refs_2_, bf16[128,2816]{1,0:T(8,128)(2,1)} %collective-permute-done.87.refs_3_, ...), custom_call_target="tpu_custom_call" | custom-call | flops 110000000 | tf_op jit(solution)/shard_map/pallas_call | solution.py:760
  915.2 19.4 %collective-permute-done.103.refs_1_ = bf16[256,1536]{1,0:T(8,128)(2,1)} collective-permute-done((bf16[256,1536]{1,0:T(8,128)(2,1)}, bf16[256,1536]{1,0:T(8,128)(2,1)}, u32[]{:S(2)}, u32[]{:S(2)}) %collective-permute-start.103) | collective-permute-done | bytes 786464 | tf_op jit(solution)/shard_map/ppermute | solution.py:30
  974.3 9.9 shard_map.216
  (540 shorter events, 362.7 us)
Async XLA Ops:
  7.2 182.7 %all-gather.6.cloned.1.call-start = ((), (), s32[]{:S(2)}) async-start(), calls=%async_computation.7 | async-start | bytes 4915200 | tf_op jit(solution)/shard_map/all_gather | solution.py:907
  25.9 56.7 %collective-permute-start.7 = (bf16[272,2048]{1,0:T(8,128)(2,1)}, bf16[272,2048]{1,0:T(8,128)(2,1)}, u32[]{:S(2)}, u32[]{:S(2)}) collective-permute-start(bf16[272,2048]{1,0:T(8,128)(2,1)} %shard_map.203.refs_1_), channel_id=1, source_target_pairs={{0,16},{4,20},{8,24},{12,28},{16,0},{20,4},{24,8},{28,12},{1,17},{... | collective-permute-start | bytes 3342344 | tf_op jit(solution)/shard_map/ppermute | solution.py:30
  31.1 50.6 %collective-permute-start.11 = (bf16[256,1536]{1,0:T(8,128)(2,1)S(1)}, bf16[256,1536]{1,0:T(8,128)(2,1)}, u32[]{:S(2)}, u32[]{:S(2)}) collective-permute-start(bf16[256,1536]{1,0:T(8,128)(2,1)S(1)} %pad_maximum_fusion.14.refs_6_), channel_id=1, source_target_pairs={{0,2},{1,3},{2,0},{3,1},{4,6},{5,7},{6,4},{7,5},{8,10},{9,11},{10,... | collective-permute-start | bytes 2359304 | tf_op jit(solution)/shard_map/ppermute | solution.py:57
  50.9 50.9 %collective-permute-start.4 = (bf16[256,2048]{1,0:T(8,128)(2,1)}, bf16[256,2048]{1,0:T(8,128)(2,1)}, u32[]{:S(2)}, u32[]{:S(2)}) collective-permute-start(bf16[256,2048]{1,0:T(8,128)(2,1)} %bitcast.251), channel_id=1, source_target_pairs={{0,8},{4,12},{8,0},{12,4},{16,24},{20,28},{24,16},{28,20},{1,9},{5... | collective-permute-start | bytes 3145736 | tf_op jit(solution)/shard_map/ppermute | solution.py:30
  52.4 49.4 %collective-permute-start.6 = (bf16[272,2048]{1,0:T(8,128)(2,1)}, bf16[272,2048]{1,0:T(8,128)(2,1)}, u32[]{:S(2)}, u32[]{:S(2)}) collective-permute-start(bf16[272,2048]{1,0:T(8,128)(2,1)} %shard_map.203.refs_1_), channel_id=1, source_target_pairs={{0,8},{4,12},{8,0},{12,4},{16,24},{20,28},{24,16},{28,20},{1,9},{5... | collective-permute-start | bytes 3342344 | tf_op jit(solution)/shard_map/ppermute | solution.py:30
  53.0 51.5 %collective-permute-start.5 = (bf16[256,2048]{1,0:T(8,128)(2,1)}, bf16[256,2048]{1,0:T(8,128)(2,1)}, u32[]{:S(2)}, u32[]{:S(2)}) collective-permute-start(bf16[256,2048]{1,0:T(8,128)(2,1)} %bitcast.252), channel_id=1, source_target_pairs={{0,16},{4,20},{8,24},{12,28},{16,0},{20,4},{24,8},{28,12},{1,17},{... | collective-permute-start | bytes 3145736 | tf_op jit(solution)/shard_map/ppermute | solution.py:30
  107.2 236.9 %all-gather.4.cloned.1.call-start = ((), (), s32[]{:S(2)}) async-start(), calls=%async_computation.3 | async-start | bytes 7208960 | tf_op jit(solution)/shard_map/all_gather | solution.py:945
  151.1 403.0 %reduce-scatter.4.cloned.1.call-start = ((), (), s32[]{:S(2)}) async-start(), calls=%async_computation.4 | async-start | bytes 3604480 | tf_op jit(solution)/shard_map/reduce_scatter | solution.py:1041
  153.7 40.7 %collective-permute-start.20 = (bf16[4,4,128,128]{3,2,1,0:T(8,128)(2,1)}, bf16[4,4,128,128]{3,2,1,0:T(8,128)(2,1)S(1)}, u32[]{:S(2)}, u32[]{:S(2)}) collective-permute-start(bf16[4,4,128,128]{3,2,1,0:T(8,128)(2,1)} %fusion.13), channel_id=1, source_target_pairs={{0,1},{1,2},{2,3},{4,5},{5,6},{6,7},{8,9},{9,10},{10,11},{12,13},{... | collective-permute-start | bytes 1572872 | tf_op jit(solution)/shard_map/ppermute | solution.py:52
  202.3 47.7 %collective-permute-start.23 = (bf16[1408,256]{1,0:T(8,128)(2,1)S(1)}, bf16[1408,256]{1,0:T(8,128)(2,1)S(1)}, u32[]{:S(2)}, u32[]{:S(2)}) collective-permute-start(bf16[1408,256]{1,0:T(8,128)(2,1)S(1)} %get-tuple-element.188), channel_id=1, source_target_pairs={{0,16},{4,20},{8,24},{12,28},{16,0},{20,4},{24,8},{28,12},{1,17},{... | collective-permute-start | bytes 2162696 | tf_op jit(solution)/shard_map/ppermute | solution.py:30
  221.0 38.7 %collective-permute-start.27 = (bf16[1024,256]{1,0:T(8,128)(2,1)S(1)}, bf16[1024,256]{1,0:T(8,128)(2,1)S(1)}, u32[]{:S(2)}, u32[]{:S(2)}) collective-permute-start(bf16[1024,256]{1,0:T(8,128)(2,1)S(1)} %slice.373), channel_id=1, source_target_pairs={{0,16},{4,20},{8,24},{12,28},{16,0},{20,4},{24,8},{28,12},{1,17},{... | collective-permute-start | bytes 1572872 | tf_op jit(solution)/shard_map/ppermute | solution.py:30
  222.8 36.9 %collective-permute-start.28 = (bf16[1024,256]{1,0:T(8,128)(2,1)S(1)}, bf16[1024,256]{1,0:T(8,128)(2,1)S(1)}, u32[]{:S(2)}, u32[]{:S(2)}) collective-permute-start(bf16[1024,256]{1,0:T(8,128)(2,1)S(1)} %slice.374), channel_id=1, source_target_pairs={{0,8},{4,12},{8,0},{12,4},{16,24},{20,28},{24,16},{28,20},{1,9},{5... | collective-permute-start | bytes 1572872 | tf_op jit(solution)/shard_map/ppermute | solution.py:30
  344.5 36.4 %collective-permute-start.44 = (bf16[1024,2816]{1,0:T(8,128)(2,1)}, bf16[1024,2816]{1,0:T(8,128)(2,1)}, u32[]{:S(2)}, u32[]{:S(2)}) collective-permute-start(bf16[1024,2816]{1,0:T(8,128)(2,1)} %all-gather.4.cloned.1.call-done.refs_11_), channel_id=1, source_target_pairs={{0,4},{4,0},{8,12},{12,8},{16,20},{20,16},{24,28},{28,24},{1,5},{5... | collective-permute-start | bytes 17301512 | tf_op jit(solution)/shard_map/ppermute | solution.py:30
  484.4 156.2 %reduce-scatter.6.cloned.1.call-start = ((), (), s32[]{:S(2)}) async-start(), calls=%async_computation.5 | async-start | bytes 3604480 | tf_op jit(solution)/shard_map/reduce_scatter | solution.py:1043
  503.7 365.3 %reduce-scatter.8.cloned.1.call-start = ((), (), s32[]{:S(2)}) async-start(), calls=%async_computation.6 | async-start | bytes 4915200 | tf_op jit(solution)/shard_map/reduce_scatter | solution.py:1088
  522.6 112.2 %collective-permute-start.63 = (bf16[3456,256]{1,0:T(8,128)(2,1)}, bf16[3456,256]{1,0:T(8,128)(2,1)}, u32[]{:S(2)}, u32[]{:S(2)}) collective-permute-start(bf16[3456,256]{1,0:T(8,128)(2,1)} %pad_maximum_fusion.1), channel_id=1, source_target_pairs={{0,8},{4,12},{8,0},{12,4},{16,24},{20,28},{24,16},{28,20},{1,9},{5... | collective-permute-start | bytes 5308424 | tf_op jit(solution)/shard_map/ppermute | solution.py:30
  525.1 109.7 %collective-permute-start.64 = (bf16[3456,256]{1,0:T(8,128)(2,1)}, bf16[3456,256]{1,0:T(8,128)(2,1)}, u32[]{:S(2)}, u32[]{:S(2)}) collective-permute-start(bf16[3456,256]{1,0:T(8,128)(2,1)} %pad_maximum_fusion.2), channel_id=1, source_target_pairs={{0,16},{4,20},{8,24},{12,28},{16,0},{20,4},{24,8},{28,12},{1,17},{... | collective-permute-start | bytes 5308424 | tf_op jit(solution)/shard_map/ppermute | solution.py:30
  527.3 107.5 %collective-permute-start.65 = (bf16[3456,256]{1,0:T(8,128)(2,1)}, bf16[3456,256]{1,0:T(8,128)(2,1)}, u32[]{:S(2)}, u32[]{:S(2)}) collective-permute-start(bf16[3456,256]{1,0:T(8,128)(2,1)} %pad_maximum_fusion.3), channel_id=1, source_target_pairs={{0,24},{4,28},{8,16},{12,20},{16,8},{20,12},{24,0},{28,4},{1,25},{... | collective-permute-start | bytes 5308424 | tf_op jit(solution)/shard_map/ppermute | solution.py:30
  568.3 39.0 %collective-permute-start.60 = (bf16[4,4,128,128]{3,2,1,0:T(8,128)(2,1)S(1)}, bf16[4,4,128,128]{3,2,1,0:T(8,128)(2,1)S(1)}, u32[]{:S(2)}, u32[]{:S(2)}) collective-permute-start(bf16[4,4,128,128]{3,2,1,0:T(8,128)(2,1)S(1)} %fusion.15), channel_id=1, source_target_pairs={{1,0},{2,1},{3,2},{5,4},{6,5},{7,6},{9,8},{10,9},{11,10},{13,12},{... | collective-permute-start | bytes 1572872 | tf_op jit(solution)/shard_map/ppermute | solution.py:52
  696.2 58.0 %collective-permute-start.85 = (bf16[256,2816]{1,0:T(8,128)(2,1)S(1)}, bf16[256,2816]{1,0:T(8,128)(2,1)}, u32[]{:S(2)}, u32[]{:S(2)}) collective-permute-start(bf16[256,2816]{1,0:T(8,128)(2,1)S(1)} %pad_maximum_fusion.5.refs_0_), channel_id=1, source_target_pairs={{0,8},{4,12},{8,0},{12,4},{16,24},{20,28},{24,16},{28,20},{1,9},{5... | collective-permute-start | bytes 4325384 | tf_op jit(solution)/shard_map/ppermute | solution.py:30
  697.7 59.8 %collective-permute-start.86 = (bf16[256,2816]{1,0:T(8,128)(2,1)S(1)}, bf16[256,2816]{1,0:T(8,128)(2,1)}, u32[]{:S(2)}, u32[]{:S(2)}) collective-permute-start(bf16[256,2816]{1,0:T(8,128)(2,1)S(1)} %pad_maximum_fusion.5.refs_0_), channel_id=1, source_target_pairs={{0,16},{4,20},{8,24},{12,28},{16,0},{20,4},{24,8},{28,12},{1,17},{... | collective-permute-start | bytes 4325384 | tf_op jit(solution)/shard_map/ppermute | solution.py:30
  753.9 37.2 %collective-permute-start.74 = (bf16[256,1536]{1,0:T(8,128)(2,1)S(1)}, bf16[256,1536]{1,0:T(8,128)(2,1)S(1)}, u32[]{:S(2)}, u32[]{:S(2)}) collective-permute-start(bf16[256,1536]{1,0:T(8,128)(2,1)S(1)} %get-tuple-element.181), channel_id=1, source_target_pairs={{0,3},{1,0},{2,1},{3,2},{4,7},{5,4},{6,5},{7,6},{8,11},{9,8},{10,9... | collective-permute-start | bytes 2359304 | tf_op jit(solution)/shard_map/ppermute | solution.py:57
  754.2 88.5 %collective-permute-start.73 = (bf16[256,1536]{1,0:T(8,128)(2,1)S(1)}, bf16[256,1536]{1,0:T(8,128)(2,1)S(1)}, u32[]{:S(2)}, u32[]{:S(2)}) collective-permute-start(bf16[256,1536]{1,0:T(8,128)(2,1)S(1)} %get-tuple-element.182), channel_id=1, source_target_pairs={{0,2},{1,3},{2,0},{3,1},{4,6},{5,7},{6,4},{7,5},{8,10},{9,11},{10,... | collective-permute-start | bytes 2359304 | tf_op jit(solution)/shard_map/ppermute | solution.py:57
  757.4 86.8 %collective-permute-start.76 = (bf16[256,2048]{1,0:T(8,128)(2,1)S(1)}, bf16[256,2048]{1,0:T(8,128)(2,1)S(1)}, u32[]{:S(2)}, u32[]{:S(2)}) collective-permute-start(bf16[256,2048]{1,0:T(8,128)(2,1)S(1)} %pad_maximum_fusion.11), channel_id=1, source_target_pairs={{0,8},{4,12},{8,0},{12,4},{16,24},{20,28},{24,16},{28,20},{1,9},{5... | collective-permute-start | bytes 3145736 | tf_op jit(solution)/shard_map/ppermute | solution.py:30
  758.0 87.7 %collective-permute-start.78 = (bf16[256,2048]{1,0:T(8,128)(2,1)S(1)}, bf16[256,2048]{1,0:T(8,128)(2,1)S(1)}, u32[]{:S(2)}, u32[]{:S(2)}) collective-permute-start(bf16[256,2048]{1,0:T(8,128)(2,1)S(1)} %pad_maximum_fusion.12), channel_id=1, source_target_pairs={{0,16},{4,20},{8,24},{12,28},{16,0},{20,4},{24,8},{28,12},{1,17},{... | collective-permute-start | bytes 3145736 | tf_op jit(solution)/shard_map/ppermute | solution.py:30
  759.6 84.1 %collective-permute-start.72 = (bf16[256,1536]{1,0:T(8,128)(2,1)S(1)}, bf16[256,1536]{1,0:T(8,128)(2,1)S(1)}, u32[]{:S(2)}, u32[]{:S(2)}) collective-permute-start(bf16[256,1536]{1,0:T(8,128)(2,1)S(1)} %get-tuple-element.180), channel_id=1, source_target_pairs={{0,1},{1,2},{2,3},{3,0},{4,5},{5,6},{6,7},{7,4},{8,9},{9,10},{10,1... | collective-permute-start | bytes 2359304 | tf_op jit(solution)/shard_map/ppermute | solution.py:57
  791.1 75.6 %collective-permute-start.90 = (bf16[256,2816]{1,0:T(8,128)(2,1)}, bf16[256,2816]{1,0:T(8,128)(2,1)}, u32[]{:S(2)}, u32[]{:S(2)}) collective-permute-start(bf16[256,2816]{1,0:T(8,128)(2,1)} %collective-permute-done.85.refs_1_), channel_id=1, source_target_pairs={{0,4},{4,0},{8,12},{12,8},{16,20},{20,16},{24,28},{28,24},{1,5},{5... | collective-permute-start | bytes 4325384 | tf_op jit(solution)/shard_map/ppermute | solution.py:30
  865.2 45.3 %collective-permute-start.68 = (bf16[256,2048]{1,0:T(8,128)(2,1)}, bf16[256,2048]{1,0:T(8,128)(2,1)S(1)}, u32[]{:S(2)}, u32[]{:S(2)}) collective-permute-start(bf16[256,2048]{1,0:T(8,128)(2,1)} %pad_maximum_fusion.9), channel_id=1, source_target_pairs={{0,8},{4,12},{8,0},{12,4},{16,24},{20,28},{24,16},{28,20},{1,9},{5... | collective-permute-start | bytes 3145736 | tf_op jit(solution)/shard_map/ppermute | solution.py:30
  869.9 68.9 %collective-permute-start.94 = (bf16[1920,256]{1,0:T(8,128)(2,1)}, bf16[1920,256]{1,0:T(8,128)(2,1)S(1)}, u32[]{:S(2)}, u32[]{:S(2)}) collective-permute-start(bf16[1920,256]{1,0:T(8,128)(2,1)} %bitcast.210), channel_id=1, source_target_pairs={{0,8},{4,12},{8,0},{12,4},{16,24},{20,28},{24,16},{28,20},{1,9},{5... | collective-permute-start | bytes 2949128 | tf_op jit(solution)/shard_map/ppermute | solution.py:30
  871.2 67.7 %collective-permute-start.95 = (bf16[1920,256]{1,0:T(8,128)(2,1)}, bf16[1920,256]{1,0:T(8,128)(2,1)S(1)}, u32[]{:S(2)}, u32[]{:S(2)}) collective-permute-start(bf16[1920,256]{1,0:T(8,128)(2,1)} %bitcast.211), channel_id=1, source_target_pairs={{0,16},{4,20},{8,24},{12,28},{16,0},{20,4},{24,8},{28,12},{1,17},{... | collective-permute-start | bytes 2949128 | tf_op jit(solution)/shard_map/ppermute | solution.py:30
  889.1 45.5 %collective-permute-start.103 = (bf16[256,1536]{1,0:T(8,128)(2,1)}, bf16[256,1536]{1,0:T(8,128)(2,1)}, u32[]{:S(2)}, u32[]{:S(2)}) collective-permute-start(bf16[256,1536]{1,0:T(8,128)(2,1)} %fusion.12.refs_0_), channel_id=1, source_target_pairs={{0,8},{4,12},{8,0},{12,4},{16,24},{20,28},{24,16},{28,20},{1,9},{5... | collective-permute-start | bytes 2359304 | tf_op jit(solution)/shard_map/ppermute | solution.py:30
  897.1 37.5 %collective-permute-start.104 = (bf16[256,1536]{1,0:T(8,128)(2,1)}, bf16[256,1536]{1,0:T(8,128)(2,1)}, u32[]{:S(2)}, u32[]{:S(2)}) collective-permute-start(bf16[256,1536]{1,0:T(8,128)(2,1)} %fusion.12.refs_0_), channel_id=1, source_target_pairs={{0,16},{4,20},{8,24},{12,28},{16,0},{20,4},{24,8},{28,12},{1,17},{... | collective-permute-start | bytes 2359304 | tf_op jit(solution)/shard_map/ppermute | solution.py:30
  (167 other events, 2979.5 us)
Sparse Core Ops, SparseCore 0:
  107.3 82.5 all-gather.5
  192.0 122.2 all-gather.3
  484.6 69.4 reduce-scatter.3
  556.2 77.3 reduce-scatter.5
  700.0 92.6 reduce-scatter.7
